TPU v7x, 32 devices: a whole 2x2x4 slice. The times are simulated.
32 devices in a mesh: cells: 8 (over z, x), cols: 4 (over y, core).
Axes of the slice: x: 2, y: 2, z: 4, core: 2. Of those that a mesh axis runs over, the one named last changes fastest.
Arguments:
- current: float32 [64, 256, 256], P('cells', 'cols'), may hold values from -6 to 6
- voltage: float32 [64, 256, 256], P('cells', 'cols'), may hold values from -6 to 6
- resistance: float32 [64, 256], P('cells'), may hold values from 0.1 to 1
- elastance: float32 [64, 256], P('cells'), may hold values from 0.1 to 1
- port_gain: float32 [64, 256], P('cells'), may hold values from -6 to 6
- symbols: int32 [3, 32, 256], P(None, 'cells'), may hold values from 0 to 3
- neighbours: int32 [64, 16], P('cells'), may hold values from 0 to 63, as said below
- live_counts: int32 [64], P('cells'), may hold values from 1 to 16, as said below
- membership: int32 [64, 1], P('cells'), may hold values from 0 to 15
- inductance_near: bfloat16 [64, 16, 256, 256], P('cells', None, 'cols'), may hold values from -0.09375 to 0.09375
- source_basis: bfloat16 [64, 64, 256], P('cells'), may hold values from -0.1875 to 0.1875
- target_basis: bfloat16 [64, 64, 256], P('cells'), may hold values from -0.75 to 0.75
- translation: bfloat16 [1024, 1024], replicated, may hold values from -0.1875 to 0.1875
Outputs:
- final_current: float32 [64, 256, 256], P('cells', 'cols')
- final_voltage: float32 [64, 256, 256], P('cells', 'cols')
Inputs may be any that keep to these rules, and one draw needn't show every extreme that they name: `neighbours`: entry 0 of block row t is t itself; every entry names a block at most 8 blocks from t. Block row t uses the first live_counts[t] entries of its list. `membership`: every cluster has at least one block.
All inputs are finite; a program needn't handle non-finite values.
Results may differ from a plain program's by a relative error of at most 0.003.
Values may be sent and summed in bfloat16 or wider, within the bound.
No kernel may reach another device: no remote copies, remote signals or barrier semaphores. Data moves between devices by JAX's collectives and lax.ppermute only.
A program may use at most 64 MiB of HBM per device.

v0:
```python
import jax
import jax.numpy as jnp
from jax import lax
from jax.sharding import PartitionSpec as P

REACH = 8
CLUSTERS = 16
STEPS = 3


def padded(block, sides, width):
    for axis, dim in sides:
        count = lax.axis_size(axis)
        forward = [(i, i + 1) for i in range(count - 1)]
        backward = [(target, source) for source, target in forward]
        low = lax.ppermute(
            lax.slice_in_dim(block, block.shape[dim] - width, None, axis=dim), axis, forward
        )
        high = lax.ppermute(lax.slice_in_dim(block, 0, width, axis=dim), axis, backward)
        block = jnp.concatenate([low, block, high], axis=dim)
    return block


def near_field(excite_cols, neighbours, live_counts, inductance_near, anchor):
    block_count, list_length = neighbours.shape
    extended = padded(excite_cols, (("cells", 0),), REACH)
    local_index = neighbours - anchor
    live_mask = jnp.arange(list_length, dtype=jnp.int32)[None, :] < live_counts[:, None]
    gathered = extended[local_index]
    masked = jnp.where(live_mask[:, :, None, None], gathered, jnp.zeros((), jnp.bfloat16))
    return lax.dot_general(
        inductance_near,
        masked,
        (((1, 2), (1, 2)), ((0,), (0,))),
        preferred_element_type=jnp.float32,
    )


def cluster_terms(source_rows, excite_rows, onehot):
    coefficients = lax.dot_general(
        source_rows, excite_rows, (((2,), (1,)), ((0,), (0,))), preferred_element_type=jnp.float32
    )
    return jnp.einsum("gb,bks->gks", onehot, coefficients, precision=lax.Precision.HIGHEST)


def far_field(totals, translation_wide, onehot, target_rows):
    cluster_count, basis_rank, scenario_count = totals.shape
    translated = jnp.dot(
        translation_wide,
        totals.reshape(cluster_count * basis_rank, scenario_count),
        precision=lax.Precision.HIGHEST,
    )
    chosen = jnp.dot(
        onehot.T,
        translated.reshape(cluster_count, basis_rank * scenario_count),
        precision=lax.Precision.HIGHEST,
    )
    chosen = chosen.reshape(onehot.shape[1], basis_rank, scenario_count)
    return lax.dot_general(
        target_rows.astype(jnp.float32),
        chosen,
        (((1,), (1,)), ((0,), (0,))),
        precision=lax.Precision.HIGHEST,
    )


def per_device(
    current,
    voltage,
    resistance,
    elastance,
    port_gain,
    symbols,
    neighbours,
    live_counts,
    membership,
    inductance_near,
    source_basis,
    target_basis,
    translation,
):
    block_count = neighbours.shape[0]
    column_index = lax.axis_index("cols")
    cell_share = inductance_near.shape[2]
    anchor = lax.axis_index("cells") * block_count - REACH
    onehot = (membership[:, 0][None, :] == jnp.arange(CLUSTERS, dtype=jnp.int32)[:, None]).astype(
        jnp.float32
    )
    levels = jnp.repeat((2 * symbols - 3).astype(jnp.float32) / 3.0, 2, axis=1)
    translation_wide = translation.astype(jnp.float32)
    resist_rows = lax.dynamic_slice_in_dim(resistance, column_index * cell_share, cell_share, 1)
    elast_rows = lax.dynamic_slice_in_dim(elastance, column_index * cell_share, cell_share, 1)
    port_rows = lax.dynamic_slice_in_dim(port_gain, column_index * cell_share, cell_share, 1)
    source_rows = lax.dynamic_slice_in_dim(source_basis, column_index * cell_share, cell_share, 2)
    target_rows = lax.dynamic_slice_in_dim(target_basis, column_index * cell_share, cell_share, 2)
    for marching in range(STEPS):
        excite = (
            port_rows[:, :, None] * levels[marching][:, None, :]
            - resist_rows[:, :, None] * current
            - voltage
        ).astype(jnp.bfloat16)
        near_part = near_field(excite, neighbours, live_counts, inductance_near, anchor)
        near_rows = lax.psum_scatter(near_part, "cols", scatter_dimension=1, tiled=True)
        totals = lax.psum(cluster_terms(source_rows, excite, onehot), ("cells", "cols"))
        far_rows = far_field(totals, translation_wide, onehot, target_rows)
        current = current + near_rows + far_rows
        voltage = voltage + elast_rows[:, :, None] * current
    return (current, voltage)


def solution(mesh):
    placed = (
        P("cells", "cols", None),
        P("cells", "cols", None),
        P("cells", None),
        P("cells", None),
        P("cells", None),
        P(None, "cells", None),
        P("cells", None),
        P("cells"),
        P("cells", None),
        P("cells", None, "cols", None),
        P("cells", None, None),
        P("cells", None, None),
        P(),
    )
    return jax.shard_map(
        per_device,
        mesh=mesh,
        in_specs=placed,
        out_specs=(P("cells", "cols", None), P("cells", "cols", None)),
        check_vma=False,
    )
```

profile of v0, /device:TPU:0, one launch (start us, length us, event | category | flops | bytes accessed | tf_op | source)
XLA Modules:
  0.0 488.3 jit_solution(12022773174671665120)
XLA Ops:
  11.2 4.9 collective-permute-start
  22.0 5.2 %collective-permute-done = bf16[8,64,256]{2,1,0:T(8,128)(2,1)S(1)} collective-permute-done((bf16[8,64,256]{2,1,0:T(8,128)(2,1)S(1)}, bf16[8,64,256]{2,1,0:T(8,128)(2,1)S(1)}, u32[]{:S(2)}, u32[]{:S(2)}) %collective-permute-start) | collective-permute-done | bytes 262176 | tf_op jit(solution)/shard_map/ppermute | solution.py:16
  28.2 2.8 gather_fusion
  31.0 6.4 %fusion.12 = f32[8,256,256]{1,2,0:T(8,128)} fusion(bf16[8,16,64,256]{3,2,1,0:T(8,128)(2,1)} %param.22, bf16[8,16,64,256]{3,2,1,0:T(8,128)(2,1)} %bitcast.76, pred[8,16]{1,0:T(8,128)(4,1)S(1)} %iota_compare_fusion.1), kind=kOutput, calls=%fused_computation.15 | convolution fusion | flops 1075838976 | bytes 10485888 | tf_op jit(solution)/shard_map/dot_general | solution.py:31
  37.4 3.1 copy.47
  40.6 114.2 %all-reduce.4.cloned.1.call-done = f32[1024,256]{1,0:T(8,128)} async-done(((f32[1024,256]{1,0:T(8,128)}), f32[1024,256]{1,0:T(8,128)}) %all-reduce.4.cloned.1.call-update) | async-done | bytes 1048592 | tf_op jit(solution)/shard_map/psum | solution.py:104
  154.8 5.7 %convolution_bitcast_fusion.2 = f32[1024,256]{0,1:T(8,128)} fusion(f32[1024,256]{1,0:T(8,128)} %all-reduce.4.cloned.1.call-done, bf16[1024,1024]{1,0:T(8,128)(2,1)S(1)} %copy-done), kind=kOutput, calls=%fused_computation.20 | convolution fusion | flops 3221225472 | bytes 4194304 | tf_op jit(solution)/shard_map/dot_general | solution.py:48
  167.2 2.8 subtract_convert_fusion.1
  170.0 3.4 collective-permute-start.2
  178.7 5.0 %collective-permute-done.2 = bf16[8,64,256]{2,1,0:T(8,128)(2,1)S(1)} collective-permute-done((bf16[8,64,256]{2,1,0:T(8,128)(2,1)S(1)}, bf16[8,64,256]{2,1,0:T(8,128)(2,1)S(1)}, u32[]{:S(2)}, u32[]{:S(2)}) %collective-permute-start.2) | collective-permute-done | bytes 262176 | tf_op jit(solution)/shard_map/ppermute | solution.py:16
  185.6 2.8 gather_fusion.1
  188.4 6.5 %fusion.15 = f32[8,256,256]{1,2,0:T(8,128)} fusion(bf16[8,16,64,256]{3,2,1,0:T(8,128)(2,1)} %param.22, bf16[8,16,64,256]{3,2,1,0:T(8,128)(2,1)} %bitcast.77, pred[8,16]{1,0:T(8,128)(4,1)S(1)} %iota_compare_fusion.1), kind=kOutput, calls=%fused_computation.16 | convolution fusion | flops 1075838976 | bytes 10485888 | tf_op jit(solution)/shard_map/dot_general | solution.py:31
  194.8 3.0 copy.55
  198.0 111.3 %all-reduce.6.cloned.1.call-done = f32[1024,256]{1,0:T(8,128)} async-done(((f32[1024,256]{1,0:T(8,128)}), f32[1024,256]{1,0:T(8,128)}) %all-reduce.6.cloned.1.call-update) | async-done | bytes 1048592 | tf_op jit(solution)/shard_map/psum | solution.py:104
  309.3 5.7 %convolution_bitcast_fusion.1 = f32[1024,256]{0,1:T(8,128)} fusion(f32[1024,256]{1,0:T(8,128)} %all-reduce.6.cloned.1.call-done, bf16[1024,1024]{1,0:T(8,128)(2,1)S(1)} %copy-done), kind=kOutput, calls=%fused_computation.19 | convolution fusion | flops 3221225472 | bytes 4194304 | tf_op jit(solution)/shard_map/dot_general | solution.py:48
  322.5 2.9 subtract_convert_fusion
  325.4 3.4 collective-permute-start.4
  334.0 5.0 %collective-permute-done.4 = bf16[8,64,256]{2,1,0:T(8,128)(2,1)S(1)} collective-permute-done((bf16[8,64,256]{2,1,0:T(8,128)(2,1)S(1)}, bf16[8,64,256]{2,1,0:T(8,128)(2,1)S(1)}, u32[]{:S(2)}, u32[]{:S(2)}) %collective-permute-start.4) | collective-permute-done | bytes 262176 | tf_op jit(solution)/shard_map/ppermute | solution.py:16
  341.0 2.8 gather_fusion.2
  343.7 6.5 %fusion.18 = f32[8,256,256]{1,2,0:T(8,128)} fusion(bf16[8,16,64,256]{3,2,1,0:T(8,128)(2,1)} %param.22, bf16[8,16,64,256]{3,2,1,0:T(8,128)(2,1)} %bitcast.75, pred[8,16]{1,0:T(8,128)(4,1)S(1)} %iota_compare_fusion.1), kind=kOutput, calls=%fused_computation.17 | convolution fusion | flops 1075838976 | bytes 10485888 | tf_op jit(solution)/shard_map/dot_general | solution.py:31
  350.2 3.0 copy.62
  353.3 111.4 %all-reduce.8.cloned.1.call-done = f32[1024,256]{1,0:T(8,128)} async-done(((f32[1024,256]{1,0:T(8,128)}), f32[1024,256]{1,0:T(8,128)}) %all-reduce.8.cloned.1.call-update) | async-done | bytes 1048592 | tf_op jit(solution)/shard_map/psum | solution.py:104
  464.7 5.7 %convolution_bitcast_fusion = f32[1024,256]{0,1:T(8,128)} fusion(f32[1024,256]{1,0:T(8,128)} %all-reduce.8.cloned.1.call-done, bf16[1024,1024]{1,0:T(8,128)(2,1)S(1)} %copy-done), kind=kOutput, calls=%fused_computation.18 | convolution fusion | flops 3221225472 | bytes 4194304 | tf_op jit(solution)/shard_map/dot_general | solution.py:48
  477.8 3.1 multiply_add_fusion
  (83 shorter events, 46.3 us)
Async XLA Ops:
  8.0 146.8 %copy-start = (bf16[1024,1024]{1,0:T(8,128)(2,1)S(1)}, bf16[1024,1024]{1,0:T(8,128)(2,1)}, u32[]{:S(2)}) copy-start(bf16[1024,1024]{1,0:T(8,128)(2,1)} %param.25) | copy-start | bytes 6291460
  8.0 13.8 %copy-start.10 = (s32[8,16]{1,0:T(8,128)S(1)}, s32[8,16]{1,0:T(8,128)}, u32[]{:S(2)}) copy-start(s32[8,16]{1,0:T(8,128)} %param.19) | copy-start | bytes 1540
  8.0 13.9 %copy-start.12 = (s32[8]{0:T(128)S(1)}, s32[8]{0:T(128)}, u32[]{:S(2)}) copy-start(s32[8]{0:T(128)} %param.20) | copy-start | bytes 100
  8.0 146.8 %all-reduce.4.cloned.1.call-start = ((), (), s32[]{:S(2)}) async-start(), calls=%async_computation.4 | async-start | bytes 2097152 | tf_op jit(solution)/shard_map/psum | solution.py:104
  11.2 16.0 %collective-permute-start = (bf16[8,64,256]{2,1,0:T(8,128)(2,1)S(1)}, bf16[8,64,256]{2,1,0:T(8,128)(2,1)S(1)}, u32[]{:S(2)}, u32[]{:S(2)}) collective-permute-start(bf16[8,64,256]{2,1,0:T(8,128)(2,1)S(1)} %subtract_convert_fusion.2), channel_id=1, source_target_pairs={{0,4},{4,8},{8,12},{12,16},{16,20},{20,24},{24,28},{1,5},{5,9},{9,... | collective-permute-start | bytes 786440 | tf_op jit(solution)/shard_map/ppermute | solution.py:16
  16.0 11.2 %collective-permute-start.1 = (bf16[8,64,256]{2,1,0:T(8,128)(2,1)S(1)}, bf16[8,64,256]{2,1,0:T(8,128)(2,1)}, u32[]{:S(2)}, u32[]{:S(2)}) collective-permute-start(bf16[8,64,256]{2,1,0:T(8,128)(2,1)S(1)} %subtract_convert_fusion.2), channel_id=1, source_target_pairs={{4,0},{8,4},{12,8},{16,12},{20,16},{24,20},{28,24},{5,1},{9,5},{13... | collective-permute-start | bytes 786440 | tf_op jit(solution)/shard_map/ppermute | solution.py:19
  21.7 145.5 %reduce-scatter.4.cloned.1.call-start = ((), (), s32[]{:S(2)}) async-start(), calls=%async_computation.3 | async-start | bytes 2621440 | tf_op jit(solution)/shard_map/reduce_scatter | solution.py:103
  37.4 3.2 copy-start.11
  40.5 268.9 %all-reduce.6.cloned.1.call-start = ((), (), s32[]{:S(2)}) async-start(), calls=%async_computation.6 | async-start | bytes 2097152 | tf_op jit(solution)/shard_map/psum | solution.py:104
  40.6 124.8 %copy-start.9 = (s32[8,1]{0,1:T(1,128)S(1)}, s32[8,1]{0,1:T(1,128)}, u32[]{:S(2)}) copy-start(s32[8,1]{0,1:T(1,128)} %param.21) | copy-start | bytes 100
  40.6 126.6 %copy-start.1 = (f32[8,64,256]{2,1,0:T(8,128)S(1)}, f32[8,64,256]{2,1,0:T(8,128)}, u32[]{:S(2)}) copy-start(f32[8,64,256]{2,1,0:T(8,128)} %param.14) | copy-start | bytes 1572868
  170.0 13.7 %copy-start.5 = (bf16[8,64,256]{2,1,0:T(8,128)(2,1)}, bf16[8,64,256]{2,1,0:T(8,128)(2,1)S(1)}, u32[]{:S(2)}) copy-start(bf16[8,64,256]{2,1,0:T(8,128)(2,1)S(1)} %get-tuple-element.9) | copy-start | bytes 786436
  170.0 13.7 %collective-permute-start.2 = (bf16[8,64,256]{2,1,0:T(8,128)(2,1)S(1)}, bf16[8,64,256]{2,1,0:T(8,128)(2,1)S(1)}, u32[]{:S(2)}, u32[]{:S(2)}) collective-permute-start(bf16[8,64,256]{2,1,0:T(8,128)(2,1)S(1)} %get-tuple-element.9), channel_id=1, source_target_pairs={{0,4},{4,8},{8,12},{12,16},{16,20},{20,24},{24,28},{1,5},{5,9},{9,... | collective-permute-start | bytes 786440 | tf_op jit(solution)/shard_map/ppermute | solution.py:16
  173.4 11.0 %collective-permute-start.3 = (bf16[8,64,256]{2,1,0:T(8,128)(2,1)S(1)}, bf16[8,64,256]{2,1,0:T(8,128)(2,1)}, u32[]{:S(2)}, u32[]{:S(2)}) collective-permute-start(bf16[8,64,256]{2,1,0:T(8,128)(2,1)S(1)} %get-tuple-element.9), channel_id=1, source_target_pairs={{4,0},{8,4},{12,8},{16,12},{20,16},{24,20},{28,24},{5,1},{9,5},{13... | collective-permute-start | bytes 786440 | tf_op jit(solution)/shard_map/ppermute | solution.py:19
  178.4 144.0 %reduce-scatter.6.cloned.1.call-start = ((), (), s32[]{:S(2)}) async-start(), calls=%async_computation.5 | async-start | bytes 2621440 | tf_op jit(solution)/shard_map/reduce_scatter | solution.py:103
  183.7 0.7 copy-start.7
  197.9 266.8 %all-reduce.8.cloned.1.call-start = ((), (), s32[]{:S(2)}) async-start(), calls=%async_computation.8 | async-start | bytes 2097152 | tf_op jit(solution)/shard_map/psum | solution.py:104
  198.0 124.5 %copy-start.2 = (f32[8,64,256]{2,1,0:T(8,128)S(1)}, f32[8,64,256]{2,1,0:T(8,128)}, u32[]{:S(2)}) copy-start(f32[8,64,256]{2,1,0:T(8,128)} %get-tuple-element.10) | copy-start | bytes 1572868
  325.4 13.7 %copy-start.4 = (bf16[8,64,256]{2,1,0:T(8,128)(2,1)}, bf16[8,64,256]{2,1,0:T(8,128)(2,1)S(1)}, u32[]{:S(2)}) copy-start(bf16[8,64,256]{2,1,0:T(8,128)(2,1)S(1)} %get-tuple-element.11) | copy-start | bytes 786436
  325.4 13.7 %collective-permute-start.4 = (bf16[8,64,256]{2,1,0:T(8,128)(2,1)S(1)}, bf16[8,64,256]{2,1,0:T(8,128)(2,1)S(1)}, u32[]{:S(2)}, u32[]{:S(2)}) collective-permute-start(bf16[8,64,256]{2,1,0:T(8,128)(2,1)S(1)} %get-tuple-element.11), channel_id=1, source_target_pairs={{0,4},{4,8},{8,12},{12,16},{16,20},{20,24},{24,28},{1,5},{5,9},{9,... | collective-permute-start | bytes 786440 | tf_op jit(solution)/shard_map/ppermute | solution.py:16
  328.7 11.0 %collective-permute-start.5 = (bf16[8,64,256]{2,1,0:T(8,128)(2,1)S(1)}, bf16[8,64,256]{2,1,0:T(8,128)(2,1)}, u32[]{:S(2)}, u32[]{:S(2)}) collective-permute-start(bf16[8,64,256]{2,1,0:T(8,128)(2,1)S(1)} %get-tuple-element.11), channel_id=1, source_target_pairs={{4,0},{8,4},{12,8},{16,12},{20,16},{24,20},{28,24},{5,1},{9,5},{13... | collective-permute-start | bytes 786440 | tf_op jit(solution)/shard_map/ppermute | solution.py:19
  333.8 144.0 %reduce-scatter.8.cloned.1.call-start = ((), (), s32[]{:S(2)}) async-start(), calls=%async_computation.7 | async-start | bytes 2621440 | tf_op jit(solution)/shard_map/reduce_scatter | solution.py:103
  353.2 124.6 %copy-start.3 = (f32[8,64,256]{2,1,0:T(8,128)S(1)}, f32[8,64,256]{2,1,0:T(8,128)}, u32[]{:S(2)}) copy-start(f32[8,64,256]{2,1,0:T(8,128)} %get-tuple-element.10) | copy-start | bytes 1572868
  353.3 124.6 %copy-start.6 = (bf16[8,64,256]{2,1,0:T(8,128)(2,1)S(1)}, bf16[8,64,256]{2,1,0:T(8,128)(2,1)}, u32[]{:S(2)}) copy-start(bf16[8,64,256]{2,1,0:T(8,128)(2,1)} %param.24) | copy-start | bytes 786436
  (1 other events, 0.7 us)
Sparse Core Ops, SparseCore 0:
  21.8 132.9 all-reduce.3
  178.6 130.7 all-reduce.5
  333.9 130.7 all-reduce.7
Sparse Core Ops, SparseCore 1:
  40.5 33.8 reduce-scatter.3
  198.0 30.7 reduce-scatter.5
  353.3 30.7 reduce-scatter.7
where the time goes:
time: 489 us; the launch traced here: 488 us
  waiting for transfers between devices  352 us (72%)
  matrix products  58.6 us (12%)
  local copies, waits for them, and re-layouts  39.7 us (8%)
  starting transfers between devices  16.1 us (3%)
  between operations  15.7 us (3%)
  other arithmetic  5.81 us (1%)
    psum x3, waiting for transfers between devices, per_device(): lax.psum(cluster_terms(source_rows, excite, onehot), ('cells', 'cols'))  337 us
    dot_general x3, matrix products, near_field(): lax.dot_general(inductance_near, masked, (((1, 2), (1, 2)), ((0,), (0,)))...  19.3 us
    dot_general x3, matrix products, far_field(): jnp.dot(translation_wide, totals.reshape(cluster_count * basis_rank, scen...  17.1 us
    ppermute x3, waiting for transfers between devices, padded(): lax.ppermute(lax.slice_in_dim(block, block.shape[dim] - width, None, axis...  15.2 us
    ppermute x3, starting transfers between devices, padded(): lax.ppermute(lax.slice_in_dim(block, block.shape[dim] - width, None, axis...  11.6 us
  transfers between devices with their start and end apart: 12, of which 6 were waited for; matrix products, arithmetic and copies ran while one was open for 19% of the time, Pallas kernels for 0%

commit v1 on v0

v1 whole, which is shorter than its diff:
```python
import functools

import jax
import jax.numpy as jnp
from jax import lax
from jax.experimental import pallas as pl
from jax.experimental.pallas import tpu as pltpu
from jax.sharding import PartitionSpec as P

CLUSTERS = 16
STEPS = 3
BF = jnp.bfloat16
F32 = jnp.float32
I16 = jnp.int16
TILE = 16
SMEM = pl.BlockSpec(memory_space=pltpu.SMEM)
VMEM = pl.BlockSpec(memory_space=pltpu.VMEM)
HBM = pl.BlockSpec(memory_space=pltpu.HBM)
ANY = pl.BlockSpec(memory_space=pl.ANY)


def local_call(body, ins, outs, scratch=(), scalars=0, after=(), where=VMEM, flops=0):
    specs = [SMEM] * scalars + [where] * (len(ins) - scalars) + [ANY] * len(after)
    moved = sum(a.size * a.dtype.itemsize for a in ins) + sum(o.size * o.dtype.itemsize for o in outs)

    def run(*refs):
        body(*refs[: len(ins)], *refs[len(ins) + len(after) :])

    return pl.pallas_call(
        run,
        out_shape=tuple(outs),
        in_specs=specs,
        out_specs=tuple(VMEM for _ in outs),
        scratch_shapes=list(scratch),
        compiler_params=pltpu.CompilerParams(vmem_limit_bytes=16 << 20),
        cost_estimate=pl.CostEstimate(flops=flops, bytes_accessed=moved, transcendentals=0),
    )(*ins, *after)


def shaped(shape, dtype):
    return jax.ShapeDtypeStruct(shape, dtype)


def pick(flag, one, zero):
    return jnp.where(flag == 1, one, zero)


def top(x):
    return jnp.max(jnp.abs(x).reshape(x.shape[0] // 8, 8, x.shape[1]), axis=0)


def exponent(bound):
    return jnp.ceil(jnp.log2(jnp.maximum(bound, 1e-30)))


def scaled(x, factor):
    return (x.reshape(x.shape[0] // 8, 8, x.shape[1]) * factor[None]).reshape(x.shape)


def encode(x, power):
    return jnp.round(scaled(x, jnp.exp2(14.0 - power))).astype(jnp.int32).astype(I16)


def decode(x, power):
    return scaled(x.astype(jnp.int32).astype(F32), jnp.exp2(power - 14.0))


def put_powers(ref, first, second):
    ref[...] = jnp.concatenate([first, second], axis=0).astype(jnp.int32).astype(I16)


def get_powers(ref):
    both = ref[...].astype(jnp.int32).astype(F32)
    return both[:8], both[8:]


def split(x):
    high = x.astype(BF)
    return high, (x - high.astype(F32)).astype(BF)


def drive(step, b, blocks, symbols_ref, cells_ref):
    lane = b * symbols_ref.shape[1] // blocks
    level = (2 * symbols_ref[step, lane : lane + 1, :] - 3).astype(F32) / 3.0
    return cells_ref[0, :, b : b + 1] * level


def send_totals(wide_ref, message):
    clusters, ranks, _ = wide_ref.shape
    power = exponent(functools.reduce(jnp.maximum, [top(wide_ref[g]) for g in range(clusters)]))
    for g in range(clusters):
        message[g * ranks : (g + 1) * ranks, :] = encode(wide_ref[g], power)
    put_powers(message.at[clusters * ranks :, :], power, power)


def first_kernel(
    blocks, meta, current, voltage, port, resist, elast, symbols,
    excite_ref, other_ref, cells_ref, damp_ref, cur, vol, flat, syms, turned, sems,
):
    share = current.shape[1]
    core, col = meta[0], meta[2]
    copies = [
        pltpu.make_async_copy(source, target, sems.at[k])
        for k, (source, target) in enumerate(
            [
                (port, flat.at[0]),
                (resist, flat.at[1]),
                (elast, flat.at[2]),
                (symbols, syms),
                (current, cur),
                (voltage, vol),
            ]
        )
    ]
    for copy in copies:
        copy.start()
    for k in range(3):
        copies[k].wait()
        turned[k] = flat[k].T
        cells_ref[k] = turned[k, pl.ds(pl.multiple_of(col * share, share), share), :]
    damp_ref[...] = turned[1] + turned[2]
    for copy in copies[3:]:
        copy.wait()
    half = cur.shape[2] // 2
    for b in range(blocks):
        excite = (
            drive(0, b, blocks, syms, cells_ref) - cells_ref[1, :, b : b + 1] * cur[b] - vol[b]
        ).astype(BF)
        excite_ref[b] = excite
        other_ref[b] = pick(core, excite[:, :half], excite[:, half:])


def source_kernel(meta, excite, other, basis, message, keep_ref, ready):
    blocks, share, scen = excite.shape
    rank, half = basis.shape[1] // 2, scen // 2
    core, row = meta[0], meta[1]
    bound = jnp.zeros((8, half), F32)
    for b in range(blocks):
        own = pick(core, excite[b, :, half:], excite[b, :, :half])
        got = other[b]
        chip = jnp.concatenate([pick(core, got, own), pick(core, own, got)], axis=0)
        side = basis[b, :, pl.ds(pl.multiple_of(row * 2 * share, 2 * share), 2 * share)]
        part = jnp.dot(side, chip, preferred_element_type=F32)
        keep_ref[b] = pick(row, part[rank:], part[:rank])
        sent = pick(row, part[:rank], part[rank:])
        ready[b] = sent
        bound = jnp.maximum(bound, top(sent))
    power = exponent(bound)
    for b in range(blocks):
        message[b * rank : (b + 1) * rank, :] = encode(ready[b], power)
    put_powers(message.at[blocks * rank :, :], power, power)


def cluster_kernel(member, kept, got, wide_ref, message):
    blocks, ranks, _ = kept.shape
    power, _ = get_powers(got.at[blocks * ranks :, :])
    wide_ref[...] = jnp.zeros(wide_ref.shape, F32)
    for b in range(blocks):
        wide_ref[member[b]] += kept[b] + decode(got[b * ranks : (b + 1) * ranks, :], power)
    send_totals(wide_ref, message)


def add_kernel(wide, got, wide_ref, message):
    clusters, ranks, _ = wide.shape
    power, _ = get_powers(got.at[clusters * ranks :, :])
    for g in range(clusters):
        wide_ref[g] = wide[g] + decode(got[g * ranks : (g + 1) * ranks, :], power)
    send_totals(wide_ref, message)


def translate_kernel(meta, member, wide, got, translation, chosen_ref, totals, rows):
    clusters, ranks, scen = wide.shape
    row = meta[1]
    power, _ = get_powers(got.at[clusters * ranks :, :])
    for g in range(clusters):
        high, low = split(wide[g] + decode(got[g * ranks : (g + 1) * ranks, :], power))
        both = jnp.concatenate([high, low], axis=1)
        none = jnp.zeros(both.shape, BF)
        totals[2 * g * ranks : (2 * g + 1) * ranks, :] = pick(row, none, both)
        totals[(2 * g + 1) * ranks : (2 * g + 2) * ranks, :] = pick(row, both, none)
    blocks, rank = chosen_ref.shape[:2]
    for b in range(blocks):
        rows[b * rank : (b + 1) * rank, :] = translation[
            pl.ds(pl.multiple_of(member[b] * rank, rank), rank), :
        ]
    both = jnp.dot(rows[...], totals[...], preferred_element_type=F32)
    for b in range(blocks):
        block = both[b * rank : (b + 1) * rank]
        chosen_ref[b] = block[:, :scen] + block[:, scen:]


def near_kernel(places, induct, own, pair, past, part_ref, around, stacked):
    blocks, share = own.shape[:2]
    entries = places.shape[1]
    for k, source in enumerate((own, pair, past)):
        around[k * blocks : (k + 1) * blocks] = source[...]
    around[3 * blocks] = jnp.zeros(around.shape[1:], BF)
    for t in range(blocks):
        for j in range(entries):
            stacked[t % 2, j * share : (j + 1) * share, :] = around[places[t, j]]
        part_ref[t] = lax.dot_general(
            induct[t], stacked[t % 2], (((0,), (0,)), ((), ())), preferred_element_type=F32
        )


def finish_kernel(step, last, meta, part, chosen, target, *refs):
    blocks, cells, scen = part.shape
    half = scen // 2
    core, col = meta[0], meta[2]
    if last:
        message, keep_ref = refs
    else:
        current, voltage, cells_ref, damp, symbols, basis, message, keep_ref, coef_ref, change = refs
    share = keep_ref.shape[1] // 2
    for b in range(blocks):
        high, low = split(chosen[b])
        far = lax.dot_general(
            jnp.concatenate([target[b], target[b]], axis=0),
            jnp.concatenate([high, low], axis=0),
            (((0,), (0,)), ((), ())),
            preferred_element_type=F32,
        )
        none = jnp.zeros_like(far)
        total = part[b] + jnp.concatenate([pick(core, none, far), pick(core, far, none)], axis=1)
        quarters = [total[k * share : (k + 1) * share] for k in range(4)]
        keep_ref[b, :share, :] = pick(core, quarters[1], quarters[0])
        keep_ref[b, share:, :] = pick(core, quarters[3], quarters[2])
        sent = [pick(core, quarters[0], quarters[1]), pick(core, quarters[2], quarters[3])]
        power = exponent(jnp.maximum(top(sent[0]), top(sent[1])))
        for k in range(2):
            message[b, k * share : (k + 1) * share, :] = encode(sent[k], power)
        second = power
        if not last:
            change[...] = -damp[:, b : b + 1] * total
            rows = pl.ds(pl.multiple_of(col * share, share), share)
            change[rows, :] += (
                drive(step + 1, b, blocks, symbols, cells_ref)
                - voltage[b]
                - (cells_ref[1, :, b : b + 1] + cells_ref[2, :, b : b + 1]) * current[b]
            )
            high, low = split(change[...])
            coefs = jnp.dot(
                jnp.concatenate([basis[b], basis[b]], axis=1),
                jnp.concatenate([high, low], axis=0),
                preferred_element_type=F32,
            )
            own = pick(core, coefs[:, half:], coefs[:, :half])
            their = pick(core, coefs[:, :half], coefs[:, half:])
            rank = coefs.shape[0] // 2
            coef_ref[b] = jnp.concatenate([own[:rank], own[rank:]], axis=1)
            their = jnp.concatenate([their[:rank], their[rank:]], axis=1)
            second = exponent(top(their))
            message[b, 2 * share : 2 * share + rank, :] = encode(their, second)
        put_powers(message.at[b, message.shape[1] - TILE :, :], power, second)


def halve_kernel(last, meta, kept, got, *refs):
    blocks = kept.shape[0]
    row = meta[1]
    if last:
        message, keep_ref, ready = refs
    else:
        coefs, message, keep_ref, coef_ref, ready, ready_coefs = refs
    share = keep_ref.shape[1]
    scen = kept.shape[2]
    half = scen // 2
    bound = jnp.zeros((8, scen), F32)
    second = jnp.zeros((8, scen), F32)
    for b in range(blocks):
        power, power_coefs = get_powers(got.at[b, got.shape[1] - TILE :, :])
        low = kept[b, :share] + decode(got[b, :share], power)
        high = kept[b, share:] + decode(got[b, share : 2 * share], power)
        keep_ref[b] = pick(row, high, low)
        sent = pick(row, low, high)
        ready[b] = sent
        bound = jnp.maximum(bound, top(sent))
        if not last:
            rank = coefs.shape[1]
            both = coefs[b] + decode(got[b, 2 * share : 2 * share + rank], power_coefs)
            coef_ref[b] = pick(row, both[:, half:], both[:, :half])
            sent = pick(row, both[:, :half], both[:, half:])
            sent = jnp.concatenate([sent[: rank // 2], sent[rank // 2 :]], axis=1)
            ready_coefs[b] = sent
            second = jnp.maximum(second, top(sent))
    power = exponent(bound)
    for b in range(blocks):
        message[b * share : (b + 1) * share, :] = encode(ready[b], power)
    if not last:
        second = exponent(second)
        start, rows = blocks * share, ready_coefs.shape[1]
        for b in range(blocks):
            message[start + b * rows : start + (b + 1) * rows, :] = encode(ready_coefs[b], second)
    put_powers(message.at[message.shape[0] - TILE :, :], power, second if not last else power)


def update_kernel(step, last, *refs):
    if last:
        current, voltage, kept, got, cells, current_ref, voltage_ref = refs
    else:
        member, current, voltage, kept, got, cells, coefs, symbols = refs[:8]
        current_ref, voltage_ref, excite_ref, wide_ref, message = refs[8:]
    blocks, share, scen = current.shape
    power, second = get_powers(got.at[got.shape[0] - TILE :, :])
    for b in range(blocks):
        cur = current[b] + (kept[b] + decode(got[b * share : (b + 1) * share, :], power))
        vol = voltage[b] + cells[2, :, b : b + 1] * cur
        current_ref[b] = cur
        voltage_ref[b] = vol
        if not last:
            excite = drive(step + 1, b, blocks, symbols, cells) - cells[1, :, b : b + 1] * cur - vol
            excite_ref[b] = excite.astype(BF)
    if not last:
        wide_ref[...] = jnp.zeros(wide_ref.shape, F32)
        start, rows, half = blocks * share, coefs.shape[1] // 2, scen // 2
        for b in range(blocks):
            sent = decode(got[start + b * rows : start + (b + 1) * rows, :], second)
            sent = jnp.concatenate([sent[:, :half], sent[:, half:]], axis=0)
            wide_ref[member[b]] += coefs[b] + sent
        send_totals(wide_ref, message)


def swap(array, axis, distance):
    count = lax.axis_size(axis)
    return lax.ppermute(array, axis, [(i, i ^ distance) for i in range(count)])


def pass_on(array, axis):
    count = lax.axis_size(axis)
    up = [(i, i + 2) for i in range(0, count - 2, 2)]
    down = [(i, i - 2) for i in range(3, count, 2)]
    return lax.ppermute(array, axis, up + down)


def per_device(
    current,
    voltage,
    resistance,
    elastance,
    port_gain,
    symbols,
    neighbours,
    live_counts,
    membership,
    inductance_near,
    source_basis,
    target_basis,
    translation,
):
    blocks, entries = neighbours.shape
    share, cells = inductance_near.shape[2:]
    scen = current.shape[2]
    rank = source_basis.shape[1]
    groups = lax.axis_size("cells")
    half, hrank = scen // 2, rank // 2
    group, col = lax.axis_index("cells"), lax.axis_index("cols")
    meta = jnp.stack([col % 2, col // 2, col]).astype(jnp.int32)
    member = membership[:, 0]
    owner = neighbours // blocks
    slot = jnp.where(owner == group, 0, jnp.where(owner == (group ^ 1), 1, 2))
    live = jnp.arange(entries, dtype=jnp.int32)[None, :] < live_counts[:, None]
    places = jnp.where(live, slot * blocks + neighbours % blocks, 3 * blocks).astype(jnp.int32)
    induct = inductance_near.reshape(blocks, entries * share, cells)

    rows_f32 = shaped((blocks, share, scen), F32)
    rows_bf = shaped((blocks, share, scen), BF)
    wide_f32 = shaped((CLUSTERS, hrank, half), F32)
    wide_msg = shaped((CLUSTERS * hrank + TILE, half), I16)
    coef_f32 = shaped((blocks, hrank, half), F32)

    excite, other, columns, damp = local_call(
        functools.partial(first_kernel, blocks),
        (meta, current, voltage, port_gain, resistance, elastance, symbols),
        (
            rows_bf,
            shaped((blocks, share, half), BF),
            shaped((3, share, blocks), F32),
            shaped((cells, blocks), F32),
        ),
        scratch=(
            pltpu.VMEM(current.shape, F32),
            pltpu.VMEM(voltage.shape, F32),
            pltpu.VMEM((3,) + port_gain.shape, F32),
            pltpu.VMEM(symbols.shape, jnp.int32),
            pltpu.VMEM((3, cells, blocks), F32),
            pltpu.SemaphoreType.DMA((6,)),
        ),
        scalars=1,
        where=HBM,
    )
    for step in range(STEPS):
        last = step == STEPS - 1
        pair = swap(excite, "cells", 1)
        if step == 0:
            other = swap(other, "cols", 1)
            send, kept = local_call(
                source_kernel,
                (meta, excite, other, source_basis),
                (shaped((blocks * hrank + TILE, half), I16), coef_f32),
                scratch=(pltpu.VMEM((blocks, hrank, half), F32),),
                scalars=1,
            )
            got = swap(send, "cols", 2)
            wide, send = local_call(cluster_kernel, (member, kept, got), (wide_f32, wide_msg), scalars=1)
        distance = groups // 2
        while distance > 1:
            got = swap(send, "cells", groups // distance)
            wide, send = local_call(add_kernel, (wide, got), (wide_f32, wide_msg))
            distance //= 2
        got = swap(send, "cells", 1)
        (chosen,) = local_call(
            translate_kernel,
            (meta, member, wide, got, translation),
            (shaped((blocks, rank, half), F32),),
            scratch=(
                pltpu.VMEM((CLUSTERS * rank, scen), BF),
                pltpu.VMEM((blocks * rank, CLUSTERS * rank), BF),
            ),
            scalars=2,
        )
        past = pass_on(pair, "cells")
        (part,) = local_call(
            near_kernel,
            (places, induct, excite, pair, past),
            (shaped((blocks, cells, scen), F32),),
            scratch=(
                pltpu.VMEM((3 * blocks + 1, share, scen), BF),
                pltpu.VMEM((2, entries * share, scen), BF),
            ),
            scalars=1,
        )
        both_f32 = shaped((blocks, 2 * share, scen), F32)
        if last:
            send, kept = local_call(
                functools.partial(finish_kernel, step, last),
                (meta, part, chosen, target_basis),
                (shaped((blocks, 2 * share + TILE, scen), I16), both_f32),
                scalars=1,
            )
            got = swap(send, "cols", 1)
            send, kept = local_call(
                functools.partial(halve_kernel, last),
                (meta, kept, got),
                (shaped((blocks * share + TILE, scen), I16), rows_f32),
                scratch=(pltpu.VMEM((blocks, share, scen), F32),),
                scalars=1,
            )
            got = swap(send, "cols", 2)
            current, voltage = local_call(
                functools.partial(update_kernel, step, last),
                (current, voltage, kept, got, columns),
                (rows_f32, rows_f32),
            )
        else:
            send, kept, coefs = local_call(
                functools.partial(finish_kernel, step, last),
                (meta, part, chosen, target_basis, current, voltage, columns, damp, symbols, source_basis),
                (
                    shaped((blocks, 2 * share + hrank + TILE, scen), I16),
                    both_f32,
                    shaped((blocks, hrank, scen), F32),
                ),
                scratch=(pltpu.VMEM((cells, scen), F32),),
                scalars=1,
            )
            got = swap(send, "cols", 1)
            send, kept, coefs = local_call(
                functools.partial(halve_kernel, last),
                (meta, kept, got, coefs),
                (shaped((blocks * (share + hrank // 2) + TILE, scen), I16), rows_f32, coef_f32),
                scratch=(
                    pltpu.VMEM((blocks, share, scen), F32),
                    pltpu.VMEM((blocks, hrank // 2, scen), F32),
                ),
                scalars=1,
            )
            got = swap(send, "cols", 2)
            current, voltage, excite, wide, send = local_call(
                functools.partial(update_kernel, step, last),
                (member, current, voltage, kept, got, columns, coefs, symbols),
                (rows_f32, rows_f32, rows_bf, wide_f32, wide_msg),
                scalars=1,
            )
    return (current, voltage)


def solution(mesh):
    placed = (
        P("cells", "cols", None),
        P("cells", "cols", None),
        P("cells", None),
        P("cells", None),
        P("cells", None),
        P(None, "cells", None),
        P("cells", None),
        P("cells"),
        P("cells", None),
        P("cells", None, "cols", None),
        P("cells", None, None),
        P("cells", None, None),
        P(),
    )
    return jax.shard_map(
        per_device,
        mesh=mesh,
        in_specs=placed,
        out_specs=(P("cells", "cols", None), P("cells", "cols", None)),
        check_vma=False,
    )
```

time: 489 us -> 133 us (0.27)
  waiting for transfers between devices: 352 us -> 60.8 us
  matrix products: 58.6 us -> 0 us
  local copies, waits for them, and re-layouts: 39.7 us -> 8.96 us
  Pallas kernels: 0 us -> 23.4 us
  starting transfers between devices: 16.1 us -> 37.8 us
  between operations: 15.7 us -> 1.01 us
  other arithmetic: 5.81 us -> 0.15 us
    psum x3 -> x0, waiting for transfers between devices: 337 us -> none  [per_device(): lax.psum(cluster_terms(source_rows, excite, onehot), ('cells', 'cols'))]
    dot_general x18 -> x0, matrix products: 58.6 us -> none  [the longest x3 19.3 us: near_field(): lax.dot_general(inductance_near, masked, (((1, 2), (1, 2)), ((0,), (0,)))...]
    ppermute x6 -> x23, waiting for transfers between devices: 15.2 us -> 60.8 us  [the longest x20 58.8 us: swap(): return lax.ppermute(array, axis, [(i, i ^ distance) for i in range(count)])]
    pallas_call x0 -> x24, Pallas kernels: none -> 23.4 us  [local_call(): pl.pallas_call(run, out_shape=tuple(outs), in_specs=specs, out_specs=tupl...]
    ppermute x6 -> x23, starting transfers between devices: 15.5 us -> 37.8 us  [the longest x20 28.8 us: swap(): return lax.ppermute(array, axis, [(i, i ^ distance) for i in range(count)])]
    dot_general x9 -> x0, local copies, waits for them, and re-layouts: 21.7 us -> none  [the longest x3 9.14 us: near_field(): lax.dot_general(inductance_near, masked, (((1, 2), (1, 2)), ((0,), (0,)))...]
    gather x3 -> x0, local copies, waits for them, and re-layouts: 8.29 us -> none  [near_field(): gathered = extended[local_index]]
    unnamed x26 -> x38, local copies, waits for them, and re-layouts: 1.47 us -> 8.96 us
  transfers between devices with their start and end apart: 12 -> 23, of which waited for: 6 -> 18; matrix products, arithmetic and copies ran while one was open for 19% -> 0% of each run, Pallas kernels for 0% -> 4%
where the time goes in v1:
time: 133 us; the launch traced here: 132 us
  waiting for transfers between devices  60.8 us (46%)
  starting transfers between devices  37.8 us (28%)
  Pallas kernels  23.4 us (18%)
  local copies, waits for them, and re-layouts  8.96 us (7%)
    ppermute x20, waiting for transfers between devices, swap(): return lax.ppermute(array, axis, [(i, i ^ distance) for i in range(count)])  58.8 us
    ppermute x20, starting transfers between devices, swap(): return lax.ppermute(array, axis, [(i, i ^ distance) for i in range(count)])  28.8 us
    pallas_call x24, Pallas kernels, local_call(): pl.pallas_call(run, out_shape=tuple(outs), in_specs=specs, out_specs=tupl...  23.4 us
    unnamed x38, local copies, waits for them, and re-layouts  8.96 us
    ppermute x3, starting transfers between devices, pass_on(): return lax.ppermute(array, axis, up + down)  8.96 us
  transfers between devices with their start and end apart: 23, of which 18 were waited for; matrix products, arithmetic and copies ran while one was open for 0% of the time, Pallas kernels for 4%

profile of v1, /device:TPU:0, one launch (start us, length us, event | category | flops | bytes accessed | tf_op | source)
XLA Modules:
  0.0 132.1 jit_solution(12074775889587798368)
XLA Ops:
  10.3 2.9 %collective-permute-start.3 = (s16[272,128]{1,0:T(8,128)(2,1)S(1)}, s16[272,128]{1,0:T(8,128)(2,1)S(1)}, u32[]{:S(2)}, u32[]{:S(2)}) collective-permute-start(s16[272,128]{1,0:T(8,128)(2,1)S(1)} %get-tuple-element.51), channel_id=1, source_target_pairs={{0,2},{1,3},{2,0},{3,1},{4,6},{5,7},{6,4},{7,5},{8,10},{9,11},{10,... | collective-permute-start | bytes 208904 | tf_op jit(solution)/shard_map/ppermute | solution.py:324
  18.9 3.3 %collective-permute-done.4.refs_1_ = s16[528,128]{1,0:T(8,128)(2,1)S(1)} collective-permute-done((s16[528,128]{1,0:T(8,128)(2,1)S(1)}, s16[528,128]{1,0:T(8,128)(2,1)S(1)}, u32[]{:S(2)}, u32[]{:S(2)}) %collective-permute-start.4) | collective-permute-done | bytes 135200 | tf_op jit(solution)/shard_map/ppermute | solution.py:324
  22.3 2.8 %collective-permute-start.5 = (s16[528,128]{1,0:T(8,128)(2,1)S(1)}, s16[528,128]{1,0:T(8,128)(2,1)S(1)}, u32[]{:S(2)}, u32[]{:S(2)}) collective-permute-start(s16[528,128]{1,0:T(8,128)(2,1)S(1)} %get-tuple-element.55), channel_id=1, source_target_pairs={{0,16},{4,20},{8,24},{12,28},{16,0},{20,4},{24,8},{28,12},{1,17},{... | collective-permute-start | bytes 405512 | tf_op jit(solution)/shard_map/ppermute | solution.py:324
  25.1 3.5 %collective-permute-start.1 = (bf16[8,64,256]{2,1,0:T(8,128)(2,1)S(1)}, bf16[8,64,256]{2,1,0:T(8,128)(2,1)S(1)}, u32[]{:S(2)}, u32[]{:S(2)}) collective-permute-start(bf16[8,64,256]{2,1,0:T(8,128)(2,1)S(1)} %collective-permute-done.refs_3_), channel_id=1, source_target_pairs={{0,8},{8,16},{16,24},{12,4},{20,12},{28,20},{1,9},{9,17},{17,25},{... | collective-permute-start | bytes 786440 | tf_op jit(solution)/shard_map/ppermute | solution.py:331
  33.3 2.2 %copy-done = bf16[8,16,64,256]{3,2,1,0:T(8,128)(2,1)S(1)} copy-done((bf16[8,16,64,256]{3,2,1,0:T(8,128)(2,1)S(1)}, bf16[8,16,64,256]{3,2,1,0:T(8,128)(2,1)}, u32[]{:S(2)}) %copy-start) | copy-done | bytes 4194328
  38.8 2.3 %shard_map.147 = (s16[8,176,256]{2,1,0:T(8,128)(2,1)S(1)}, f32[8,128,256]{2,1,0:T(8,128)S(1)}, f32[8,32,256]{2,1,0:T(8,128)S(1)}) custom-call(s32[3]{0:T(128)S(1)} %pad_add_fusion.refs_0_, f32[8,256,256]{2,1,0:T(8,128)S(1)} %shard_map.141.refs_1_, f32[8,64,128]{2,1,0:T(8,128)S(1)} %shard_map.146.refs_2_, bf16[8,64,256]{2,1,0:T(8,128)(2,1)S(1)} %copy-done.9, ...), custom_call_target="tpu_custom_call" | custom-call | bytes 5990412 | tf_op jit(solution)/shard_map/pallas_call | solution.py:29
  41.2 2.2 %collective-permute-done.7.refs_2_ = s16[8,176,256]{2,1,0:T(8,128)(2,1)S(1)} collective-permute-done((s16[8,176,256]{2,1,0:T(8,128)(2,1)S(1)}, s16[8,176,256]{2,1,0:T(8,128)(2,1)S(1)}, u32[]{:S(2)}, u32[]{:S(2)}) %collective-permute-start.7) | collective-permute-done | bytes 720928 | tf_op jit(solution)/shard_map/ppermute | solution.py:324
  45.8 8.4 %collective-permute-done.8.refs_4_ = s16[656,256]{1,0:T(8,128)(2,1)S(1)} collective-permute-done((s16[656,256]{1,0:T(8,128)(2,1)S(1)}, s16[656,256]{1,0:T(8,128)(2,1)S(1)}, u32[]{:S(2)}, u32[]{:S(2)}) %collective-permute-start.8) | collective-permute-done | bytes 335904 | tf_op jit(solution)/shard_map/ppermute | solution.py:324
  55.1 2.4 %collective-permute-start.9 = (bf16[8,64,256]{2,1,0:T(8,128)(2,1)S(1)}, bf16[8,64,256]{2,1,0:T(8,128)(2,1)S(1)}, u32[]{:S(2)}, u32[]{:S(2)}) collective-permute-start(bf16[8,64,256]{2,1,0:T(8,128)(2,1)S(1)} %get-tuple-element.68.refs_2_), channel_id=1, source_target_pairs={{0,4},{4,0},{8,12},{12,8},{16,20},{20,16},{24,28},{28,24},{1,5},{5... | collective-permute-start | bytes 786440 | tf_op jit(solution)/shard_map/ppermute | solution.py:324
  59.6 3.0 %collective-permute-done.11.refs_1_ = s16[528,128]{1,0:T(8,128)(2,1)S(1)} collective-permute-done((s16[528,128]{1,0:T(8,128)(2,1)S(1)}, s16[528,128]{1,0:T(8,128)(2,1)S(1)}, u32[]{:S(2)}, u32[]{:S(2)}) %collective-permute-start.11) | collective-permute-done | bytes 135200 | tf_op jit(solution)/shard_map/ppermute | solution.py:324
  62.7 2.7 %collective-permute-start.12 = (s16[528,128]{1,0:T(8,128)(2,1)S(1)}, s16[528,128]{1,0:T(8,128)(2,1)S(1)}, u32[]{:S(2)}, u32[]{:S(2)}) collective-permute-start(s16[528,128]{1,0:T(8,128)(2,1)S(1)} %get-tuple-element.72), channel_id=1, source_target_pairs={{0,16},{4,20},{8,24},{12,28},{16,0},{20,4},{24,8},{28,12},{1,17},{... | collective-permute-start | bytes 405512 | tf_op jit(solution)/shard_map/ppermute | solution.py:324
  65.4 2.3 %collective-permute-start.10 = (bf16[8,64,256]{2,1,0:T(8,128)(2,1)S(1)}, bf16[8,64,256]{2,1,0:T(8,128)(2,1)S(1)}, u32[]{:S(2)}, u32[]{:S(2)}) collective-permute-start(bf16[8,64,256]{2,1,0:T(8,128)(2,1)S(1)} %collective-permute-done.9.refs_3_), channel_id=1, source_target_pairs={{0,8},{8,16},{16,24},{12,4},{20,12},{28,20},{1,9},{9,17},{17,25},{... | collective-permute-start | bytes 786440 | tf_op jit(solution)/shard_map/ppermute | solution.py:331
  67.7 2.8 %collective-permute-done.12.refs_1_ = s16[528,128]{1,0:T(8,128)(2,1)S(1)} collective-permute-done((s16[528,128]{1,0:T(8,128)(2,1)S(1)}, s16[528,128]{1,0:T(8,128)(2,1)S(1)}, u32[]{:S(2)}, u32[]{:S(2)}) %collective-permute-start.12) | collective-permute-done | bytes 135200 | tf_op jit(solution)/shard_map/ppermute | solution.py:324
  70.5 2.9 %collective-permute-start.13 = (s16[528,128]{1,0:T(8,128)(2,1)S(1)}, s16[528,128]{1,0:T(8,128)(2,1)S(1)}, u32[]{:S(2)}, u32[]{:S(2)}) collective-permute-start(s16[528,128]{1,0:T(8,128)(2,1)S(1)} %get-tuple-element.74), channel_id=1, source_target_pairs={{0,4},{4,0},{8,12},{12,8},{16,20},{20,16},{24,28},{28,24},{1,5},{5... | collective-permute-start | bytes 405512 | tf_op jit(solution)/shard_map/ppermute | solution.py:324
  73.5 3.0 %collective-permute-done.13.refs_3_ = s16[528,128]{1,0:T(8,128)(2,1)S(1)} collective-permute-done((s16[528,128]{1,0:T(8,128)(2,1)S(1)}, s16[528,128]{1,0:T(8,128)(2,1)S(1)}, u32[]{:S(2)}, u32[]{:S(2)}) %collective-permute-start.13) | collective-permute-done | bytes 135200 | tf_op jit(solution)/shard_map/ppermute | solution.py:324
  79.5 2.3 %shard_map.154 = (s16[8,176,256]{2,1,0:T(8,128)(2,1)S(1)}, f32[8,128,256]{2,1,0:T(8,128)S(1)}, f32[8,32,256]{2,1,0:T(8,128)S(1)}) custom-call(s32[3]{0:T(128)S(1)} %pad_add_fusion.refs_0_, f32[8,256,256]{2,1,0:T(8,128)S(1)} %shard_map.150.refs_1_, f32[8,64,128]{2,1,0:T(8,128)S(1)} %shard_map.153.refs_2_, bf16[8,64,256]{2,1,0:T(8,128)(2,1)S(1)} %copy-done.9, ...), custom_call_target="tpu_custom_call" | custom-call | bytes 5990412 | tf_op jit(solution)/shard_map/pallas_call | solution.py:29
  81.8 2.2 %collective-permute-done.14.refs_2_ = s16[8,176,256]{2,1,0:T(8,128)(2,1)S(1)} collective-permute-done((s16[8,176,256]{2,1,0:T(8,128)(2,1)S(1)}, s16[8,176,256]{2,1,0:T(8,128)(2,1)S(1)}, u32[]{:S(2)}, u32[]{:S(2)}) %collective-permute-start.14) | collective-permute-done | bytes 720928 | tf_op jit(solution)/shard_map/ppermute | solution.py:324
  86.3 8.5 %collective-permute-done.15.refs_4_ = s16[656,256]{1,0:T(8,128)(2,1)S(1)} collective-permute-done((s16[656,256]{1,0:T(8,128)(2,1)S(1)}, s16[656,256]{1,0:T(8,128)(2,1)S(1)}, u32[]{:S(2)}, u32[]{:S(2)}) %collective-permute-start.15) | collective-permute-done | bytes 335904 | tf_op jit(solution)/shard_map/ppermute | solution.py:324
  95.8 2.1 %collective-permute-start.16 = (bf16[8,64,256]{2,1,0:T(8,128)(2,1)S(1)}, bf16[8,64,256]{2,1,0:T(8,128)(2,1)S(1)}, u32[]{:S(2)}, u32[]{:S(2)}) collective-permute-start(bf16[8,64,256]{2,1,0:T(8,128)(2,1)S(1)} %get-tuple-element.83.refs_2_), channel_id=1, source_target_pairs={{0,4},{4,0},{8,12},{12,8},{16,20},{20,16},{24,28},{28,24},{1,5},{5... | collective-permute-start | bytes 786440 | tf_op jit(solution)/shard_map/ppermute | solution.py:324
  97.9 5.0 %collective-permute-done.18.refs_1_ = s16[528,128]{1,0:T(8,128)(2,1)S(1)} collective-permute-done((s16[528,128]{1,0:T(8,128)(2,1)S(1)}, s16[528,128]{1,0:T(8,128)(2,1)S(1)}, u32[]{:S(2)}, u32[]{:S(2)}) %collective-permute-start.18) | collective-permute-done | bytes 135200 | tf_op jit(solution)/shard_map/ppermute | solution.py:324
  103.7 3.2 %collective-permute-start.17 = (bf16[8,64,256]{2,1,0:T(8,128)(2,1)S(1)}, bf16[8,64,256]{2,1,0:T(8,128)(2,1)S(1)}, u32[]{:S(2)}, u32[]{:S(2)}) collective-permute-start(bf16[8,64,256]{2,1,0:T(8,128)(2,1)S(1)} %collective-permute-done.16.refs_3_), channel_id=1, source_target_pairs={{0,8},{8,16},{16,24},{12,4},{20,12},{28,20},{1,9},{9,17},{17,25},{... | collective-permute-start | bytes 786440 | tf_op jit(solution)/shard_map/ppermute | solution.py:331
  106.9 3.3 %collective-permute-done.19.refs_1_ = s16[528,128]{1,0:T(8,128)(2,1)S(1)} collective-permute-done((s16[528,128]{1,0:T(8,128)(2,1)S(1)}, s16[528,128]{1,0:T(8,128)(2,1)S(1)}, u32[]{:S(2)}, u32[]{:S(2)}) %collective-permute-start.19) | collective-permute-done | bytes 135200 | tf_op jit(solution)/shard_map/ppermute | solution.py:324
  111.8 3.6 %collective-permute-done.20.refs_3_ = s16[528,128]{1,0:T(8,128)(2,1)S(1)} collective-permute-done((s16[528,128]{1,0:T(8,128)(2,1)S(1)}, s16[528,128]{1,0:T(8,128)(2,1)S(1)}, u32[]{:S(2)}, u32[]{:S(2)}) %collective-permute-start.20) | collective-permute-done | bytes 135200 | tf_op jit(solution)/shard_map/ppermute | solution.py:324
  123.9 7.1 %collective-permute-done.22.refs_3_ = s16[528,256]{1,0:T(8,128)(2,1)S(1)} collective-permute-done((s16[528,256]{1,0:T(8,128)(2,1)S(1)}, s16[528,256]{1,0:T(8,128)(2,1)S(1)}, u32[]{:S(2)}, u32[]{:S(2)}) %collective-permute-start.22) | collective-permute-done | bytes 270368 | tf_op jit(solution)/shard_map/ppermute | solution.py:324
  (86 shorter events, 47.0 us)
Async XLA Ops:
  0.6 30.5 %copy-start.18 = (s32[8]{0:T(128)S(1)}, s32[8]{0:T(128)}, u32[]{:S(2)}) copy-start(s32[8]{0:T(128)} %param.20) | copy-start | bytes 100
  7.0 1.5 %collective-permute-start.2 = (bf16[8,64,128]{2,1,0:T(8,128)(2,1)S(1)}, bf16[8,64,128]{2,1,0:T(8,128)(2,1)S(1)}, u32[]{:S(2)}, u32[]{:S(2)}) collective-permute-start(bf16[8,64,128]{2,1,0:T(8,128)(2,1)S(1)} %get-tuple-element.49), channel_id=1, source_target_pairs={{0,1},{1,0},{2,3},{3,2},{4,5},{5,4},{6,7},{7,6},{8,9},{9,8},{10,11... | collective-permute-start | bytes 393224 | tf_op jit(solution)/shard_map/ppermute | solution.py:324
  10.3 5.4 %collective-permute-start.3 = (s16[272,128]{1,0:T(8,128)(2,1)S(1)}, s16[272,128]{1,0:T(8,128)(2,1)S(1)}, u32[]{:S(2)}, u32[]{:S(2)}) collective-permute-start(s16[272,128]{1,0:T(8,128)(2,1)S(1)} %get-tuple-element.51), channel_id=1, source_target_pairs={{0,2},{1,3},{2,0},{3,1},{4,6},{5,7},{6,4},{7,5},{8,10},{9,11},{10,... | collective-permute-start | bytes 208904 | tf_op jit(solution)/shard_map/ppermute | solution.py:324
  13.2 11.9 %collective-permute-start = (bf16[8,64,256]{2,1,0:T(8,128)(2,1)S(1)}, bf16[8,64,256]{2,1,0:T(8,128)(2,1)S(1)}, u32[]{:S(2)}, u32[]{:S(2)}) collective-permute-start(bf16[8,64,256]{2,1,0:T(8,128)(2,1)S(1)} %get-tuple-element.48.refs_2_.refs_1_), channel_id=1, source_target_pairs={{0,4},{4,0},{8,12},{12,8},{16,20},{20,16},{24,28},{28,24},{1,5},{5... | collective-permute-start | bytes 786440 | tf_op jit(solution)/shard_map/ppermute | solution.py:324
  17.0 5.2 %collective-permute-start.4 = (s16[528,128]{1,0:T(8,128)(2,1)S(1)}, s16[528,128]{1,0:T(8,128)(2,1)S(1)}, u32[]{:S(2)}, u32[]{:S(2)}) collective-permute-start(s16[528,128]{1,0:T(8,128)(2,1)S(1)} %get-tuple-element.53), channel_id=1, source_target_pairs={{0,8},{4,12},{8,0},{12,4},{16,24},{20,28},{24,16},{28,20},{1,9},{5... | collective-permute-start | bytes 405512 | tf_op jit(solution)/shard_map/ppermute | solution.py:324
  22.3 8.1 %collective-permute-start.5 = (s16[528,128]{1,0:T(8,128)(2,1)S(1)}, s16[528,128]{1,0:T(8,128)(2,1)S(1)}, u32[]{:S(2)}, u32[]{:S(2)}) collective-permute-start(s16[528,128]{1,0:T(8,128)(2,1)S(1)} %get-tuple-element.55), channel_id=1, source_target_pairs={{0,16},{4,20},{8,24},{12,28},{16,0},{20,4},{24,8},{28,12},{1,17},{... | collective-permute-start | bytes 405512 | tf_op jit(solution)/shard_map/ppermute | solution.py:324
  25.1 8.1 %collective-permute-start.1 = (bf16[8,64,256]{2,1,0:T(8,128)(2,1)S(1)}, bf16[8,64,256]{2,1,0:T(8,128)(2,1)S(1)}, u32[]{:S(2)}, u32[]{:S(2)}) collective-permute-start(bf16[8,64,256]{2,1,0:T(8,128)(2,1)S(1)} %collective-permute-done.refs_3_), channel_id=1, source_target_pairs={{0,8},{8,16},{16,24},{12,4},{20,12},{28,20},{1,9},{9,17},{17,25},{... | collective-permute-start | bytes 786440 | tf_op jit(solution)/shard_map/ppermute | solution.py:331
  30.5 7.0 %collective-permute-start.6 = (s16[528,128]{1,0:T(8,128)(2,1)S(1)}, s16[528,128]{1,0:T(8,128)(2,1)S(1)}, u32[]{:S(2)}, u32[]{:S(2)}) collective-permute-start(s16[528,128]{1,0:T(8,128)(2,1)S(1)} %get-tuple-element.57), channel_id=1, source_target_pairs={{0,4},{4,0},{8,12},{12,8},{16,20},{20,16},{24,28},{28,24},{1,5},{5... | collective-permute-start | bytes 405512 | tf_op jit(solution)/shard_map/ppermute | solution.py:324
  41.1 2.3 %collective-permute-start.7 = (s16[8,176,256]{2,1,0:T(8,128)(2,1)S(1)}, s16[8,176,256]{2,1,0:T(8,128)(2,1)S(1)}, u32[]{:S(2)}, u32[]{:S(2)}) collective-permute-start(s16[8,176,256]{2,1,0:T(8,128)(2,1)S(1)} %get-tuple-element.61), channel_id=1, source_target_pairs={{0,1},{1,0},{2,3},{3,2},{4,5},{5,4},{6,7},{7,6},{8,9},{9,8},{10,11... | collective-permute-start | bytes 2162696 | tf_op jit(solution)/shard_map/ppermute | solution.py:324
  44.2 10.0 %collective-permute-start.8 = (s16[656,256]{1,0:T(8,128)(2,1)S(1)}, s16[656,256]{1,0:T(8,128)(2,1)S(1)}, u32[]{:S(2)}, u32[]{:S(2)}) collective-permute-start(s16[656,256]{1,0:T(8,128)(2,1)S(1)} %get-tuple-element.64), channel_id=1, source_target_pairs={{0,2},{1,3},{2,0},{3,1},{4,6},{5,7},{6,4},{7,5},{8,10},{9,11},{10,... | collective-permute-start | bytes 1007624 | tf_op jit(solution)/shard_map/ppermute | solution.py:324
  55.1 10.3 %collective-permute-start.9 = (bf16[8,64,256]{2,1,0:T(8,128)(2,1)S(1)}, bf16[8,64,256]{2,1,0:T(8,128)(2,1)S(1)}, u32[]{:S(2)}, u32[]{:S(2)}) collective-permute-start(bf16[8,64,256]{2,1,0:T(8,128)(2,1)S(1)} %get-tuple-element.68.refs_2_), channel_id=1, source_target_pairs={{0,4},{4,0},{8,12},{12,8},{16,20},{20,16},{24,28},{28,24},{1,5},{5... | collective-permute-start | bytes 786440 | tf_op jit(solution)/shard_map/ppermute | solution.py:324
  57.6 5.0 %collective-permute-start.11 = (s16[528,128]{1,0:T(8,128)(2,1)S(1)}, s16[528,128]{1,0:T(8,128)(2,1)S(1)}, u32[]{:S(2)}, u32[]{:S(2)}) collective-permute-start(s16[528,128]{1,0:T(8,128)(2,1)S(1)} %get-tuple-element.70), channel_id=1, source_target_pairs={{0,8},{4,12},{8,0},{12,4},{16,24},{20,28},{24,16},{28,20},{1,9},{5... | collective-permute-start | bytes 405512 | tf_op jit(solution)/shard_map/ppermute | solution.py:324
  62.7 7.8 %collective-permute-start.12 = (s16[528,128]{1,0:T(8,128)(2,1)S(1)}, s16[528,128]{1,0:T(8,128)(2,1)S(1)}, u32[]{:S(2)}, u32[]{:S(2)}) collective-permute-start(s16[528,128]{1,0:T(8,128)(2,1)S(1)} %get-tuple-element.72), channel_id=1, source_target_pairs={{0,16},{4,20},{8,24},{12,28},{16,0},{20,4},{24,8},{28,12},{1,17},{... | collective-permute-start | bytes 405512 | tf_op jit(solution)/shard_map/ppermute | solution.py:324
  65.4 12.1 %collective-permute-start.10 = (bf16[8,64,256]{2,1,0:T(8,128)(2,1)S(1)}, bf16[8,64,256]{2,1,0:T(8,128)(2,1)S(1)}, u32[]{:S(2)}, u32[]{:S(2)}) collective-permute-start(bf16[8,64,256]{2,1,0:T(8,128)(2,1)S(1)} %collective-permute-done.9.refs_3_), channel_id=1, source_target_pairs={{0,8},{8,16},{16,24},{12,4},{20,12},{28,20},{1,9},{9,17},{17,25},{... | collective-permute-start | bytes 786440 | tf_op jit(solution)/shard_map/ppermute | solution.py:331
  70.5 5.9 %collective-permute-start.13 = (s16[528,128]{1,0:T(8,128)(2,1)S(1)}, s16[528,128]{1,0:T(8,128)(2,1)S(1)}, u32[]{:S(2)}, u32[]{:S(2)}) collective-permute-start(s16[528,128]{1,0:T(8,128)(2,1)S(1)} %get-tuple-element.74), channel_id=1, source_target_pairs={{0,4},{4,0},{8,12},{12,8},{16,20},{20,16},{24,28},{28,24},{1,5},{5... | collective-permute-start | bytes 405512 | tf_op jit(solution)/shard_map/ppermute | solution.py:324
  81.8 2.3 %collective-permute-start.14 = (s16[8,176,256]{2,1,0:T(8,128)(2,1)S(1)}, s16[8,176,256]{2,1,0:T(8,128)(2,1)S(1)}, u32[]{:S(2)}, u32[]{:S(2)}) collective-permute-start(s16[8,176,256]{2,1,0:T(8,128)(2,1)S(1)} %get-tuple-element.76), channel_id=1, source_target_pairs={{0,1},{1,0},{2,3},{3,2},{4,5},{5,4},{6,7},{7,6},{8,9},{9,8},{10,11... | collective-permute-start | bytes 2162696 | tf_op jit(solution)/shard_map/ppermute | solution.py:324
  84.9 10.0 %collective-permute-start.15 = (s16[656,256]{1,0:T(8,128)(2,1)S(1)}, s16[656,256]{1,0:T(8,128)(2,1)S(1)}, u32[]{:S(2)}, u32[]{:S(2)}) collective-permute-start(s16[656,256]{1,0:T(8,128)(2,1)S(1)} %get-tuple-element.79), channel_id=1, source_target_pairs={{0,2},{1,3},{2,0},{3,1},{4,6},{5,7},{6,4},{7,5},{8,10},{9,11},{10,... | collective-permute-start | bytes 1007624 | tf_op jit(solution)/shard_map/ppermute | solution.py:324
  95.8 7.9 %collective-permute-start.16 = (bf16[8,64,256]{2,1,0:T(8,128)(2,1)S(1)}, bf16[8,64,256]{2,1,0:T(8,128)(2,1)S(1)}, u32[]{:S(2)}, u32[]{:S(2)}) collective-permute-start(bf16[8,64,256]{2,1,0:T(8,128)(2,1)S(1)} %get-tuple-element.83.refs_2_), channel_id=1, source_target_pairs={{0,4},{4,0},{8,12},{12,8},{16,20},{20,16},{24,28},{28,24},{1,5},{5... | collective-permute-start | bytes 786440 | tf_op jit(solution)/shard_map/ppermute | solution.py:324
  97.9 5.0 %collective-permute-start.18 = (s16[528,128]{1,0:T(8,128)(2,1)S(1)}, s16[528,128]{1,0:T(8,128)(2,1)S(1)}, u32[]{:S(2)}, u32[]{:S(2)}) collective-permute-start(s16[528,128]{1,0:T(8,128)(2,1)S(1)} %get-tuple-element.85), channel_id=1, source_target_pairs={{0,8},{4,12},{8,0},{12,4},{16,24},{20,28},{24,16},{28,20},{1,9},{5... | collective-permute-start | bytes 405512 | tf_op jit(solution)/shard_map/ppermute | solution.py:324
  103.0 7.2 %collective-permute-start.19 = (s16[528,128]{1,0:T(8,128)(2,1)S(1)}, s16[528,128]{1,0:T(8,128)(2,1)S(1)}, u32[]{:S(2)}, u32[]{:S(2)}) collective-permute-start(s16[528,128]{1,0:T(8,128)(2,1)S(1)} %get-tuple-element.87), channel_id=1, source_target_pairs={{0,16},{4,20},{8,24},{12,28},{16,0},{20,4},{24,8},{28,12},{1,17},{... | collective-permute-start | bytes 405512 | tf_op jit(solution)/shard_map/ppermute | solution.py:324
  103.7 12.7 %collective-permute-start.17 = (bf16[8,64,256]{2,1,0:T(8,128)(2,1)S(1)}, bf16[8,64,256]{2,1,0:T(8,128)(2,1)S(1)}, u32[]{:S(2)}, u32[]{:S(2)}) collective-permute-start(bf16[8,64,256]{2,1,0:T(8,128)(2,1)S(1)} %collective-permute-done.16.refs_3_), channel_id=1, source_target_pairs={{0,8},{8,16},{16,24},{12,4},{20,12},{28,20},{1,9},{9,17},{17,25},{... | collective-permute-start | bytes 786440 | tf_op jit(solution)/shard_map/ppermute | solution.py:331
  110.3 5.1 %collective-permute-start.20 = (s16[528,128]{1,0:T(8,128)(2,1)S(1)}, s16[528,128]{1,0:T(8,128)(2,1)S(1)}, u32[]{:S(2)}, u32[]{:S(2)}) collective-permute-start(s16[528,128]{1,0:T(8,128)(2,1)S(1)} %get-tuple-element.89), channel_id=1, source_target_pairs={{0,4},{4,0},{8,12},{12,8},{16,20},{20,16},{24,28},{28,24},{1,5},{5... | collective-permute-start | bytes 405512 | tf_op jit(solution)/shard_map/ppermute | solution.py:324
  119.6 2.1 %collective-permute-start.21 = (s16[8,144,256]{2,1,0:T(8,128)(2,1)S(1)}, s16[8,144,256]{2,1,0:T(8,128)(2,1)S(1)}, u32[]{:S(2)}, u32[]{:S(2)}) collective-permute-start(s16[8,144,256]{2,1,0:T(8,128)(2,1)S(1)} %get-tuple-element.91), channel_id=1, source_target_pairs={{0,1},{1,0},{2,3},{3,2},{4,5},{5,4},{6,7},{7,6},{8,9},{9,8},{10,11... | collective-permute-start | bytes 1769480 | tf_op jit(solution)/shard_map/ppermute | solution.py:324
  122.5 8.6 %collective-permute-start.22 = (s16[528,256]{1,0:T(8,128)(2,1)S(1)}, s16[528,256]{1,0:T(8,128)(2,1)S(1)}, u32[]{:S(2)}, u32[]{:S(2)}) collective-permute-start(s16[528,256]{1,0:T(8,128)(2,1)S(1)} %get-tuple-element.93), channel_id=1, source_target_pairs={{0,2},{1,3},{2,0},{3,1},{4,6},{5,7},{6,4},{7,5},{8,10},{9,11},{10,... | collective-permute-start | bytes 811016 | tf_op jit(solution)/shard_map/ppermute | solution.py:324
  (18 other events, 72.8 us)

commit v2 on v1

v2 whole, which is shorter than its diff:
```python
import functools

import jax
import jax.numpy as jnp
from jax import lax
from jax.experimental import pallas as pl
from jax.experimental.pallas import tpu as pltpu
from jax.sharding import PartitionSpec as P

CLUSTERS = 16
STEPS = 3
BF = jnp.bfloat16
F32 = jnp.float32
I16 = jnp.int16
TILE = 16
SMEM = pl.BlockSpec(memory_space=pltpu.SMEM)
VMEM = pl.BlockSpec(memory_space=pltpu.VMEM)
HBM = pl.BlockSpec(memory_space=pltpu.HBM)
ANY = pl.BlockSpec(memory_space=pl.ANY)


def local_call(body, ins, outs, scratch=(), scalars=0, after=(), left=()):
    moved = sum(a.size * a.dtype.itemsize for a in ins) + sum(o.size * o.dtype.itemsize for o in outs)
    specs = [SMEM] * scalars + [VMEM] * (len(ins) - scalars) + [ANY] * len(after)
    ins = list(ins)
    for k in left:
        specs[k] = HBM
        ins[k] = pltpu.with_memory_space_constraint(ins[k], pltpu.HBM)

    def run(*refs):
        body(*refs[: len(ins)], *refs[len(ins) + len(after) :])

    return pl.pallas_call(
        run,
        out_shape=tuple(outs),
        in_specs=specs,
        out_specs=tuple(VMEM for _ in outs),
        scratch_shapes=list(scratch),
        compiler_params=pltpu.CompilerParams(vmem_limit_bytes=16 << 20),
        cost_estimate=pl.CostEstimate(flops=0, bytes_accessed=moved, transcendentals=0),
        name=getattr(body, "func", body).__name__,
    )(*ins, *after)


def shaped(shape, dtype):
    return jax.ShapeDtypeStruct(shape, dtype)


def pick(flag, one, zero):
    return jnp.where(flag == 1, one, zero)


def top(x):
    return jnp.max(jnp.abs(x).reshape(x.shape[0] // 8, 8, x.shape[1]), axis=0)


def exponent(bound):
    return jnp.ceil(jnp.log2(jnp.maximum(bound, 1e-30)))


def scaled(x, factor):
    return (x.reshape(x.shape[0] // 8, 8, x.shape[1]) * factor[None]).reshape(x.shape)


def encode(x, power):
    return jnp.round(scaled(x, jnp.exp2(14.0 - power))).astype(jnp.int32).astype(I16)


def decode(x, power):
    return scaled(x.astype(jnp.int32).astype(F32), jnp.exp2(power - 14.0))


def put_powers(ref, first, second):
    ref[...] = jnp.concatenate([first, second], axis=0).astype(jnp.int32).astype(I16)


def get_powers(ref):
    both = ref[...].astype(jnp.int32).astype(F32)
    return both[:8], both[8:]


def split(x):
    high = x.astype(BF)
    return high, (x - high.astype(F32)).astype(BF)


def drive(step, b, blocks, symbols_ref, cells_ref):
    lane = b * symbols_ref.shape[1] // blocks
    level = (2 * symbols_ref[step, lane : lane + 1, :] - 3).astype(F32) / 3.0
    return cells_ref[0, :, b : b + 1] * level


def core_half(core, x):
    half = x.shape[-1] // 2
    return pick(core, x[..., half:], x[..., :half])


def chip_rows(core, own, other):
    own, other = core_half(core, own), core_half(core, other)
    return jnp.concatenate([pick(core, other, own), pick(core, own, other)], axis=0)


def send_totals(wide_ref, message):
    clusters, ranks, _ = wide_ref.shape
    power = exponent(functools.reduce(jnp.maximum, [top(wide_ref[g]) for g in range(clusters)]))
    for g in range(clusters):
        message[g * ranks : (g + 1) * ranks, :] = encode(wide_ref[g], power)
    put_powers(message.at[clusters * ranks :, :], power, power)


def first_kernel(
    meta, current, voltage, port, resist, elast, symbols, source, target,
    excite_ref, cells_ref, damp_ref, source_ref, target_ref, cur, vol, flat, syms, turned, sems,
):
    blocks, share, _ = current.shape
    col = meta[2]
    pairs = [(port, flat.at[0]), (resist, flat.at[1]), (elast, flat.at[2]), (symbols, syms)]
    pairs += [(current, cur), (voltage, vol), (source, source_ref), (target, target_ref)]
    copies = [pltpu.make_async_copy(*pair, sems.at[k]) for k, pair in enumerate(pairs)]
    for copy in copies:
        copy.start()
    for k in range(3):
        copies[k].wait()
        turned[k] = flat[k].T
        cells_ref[k] = turned[k, pl.ds(pl.multiple_of(meta[1] * 2 * share, 2 * share), 2 * share), :]
    damp_ref[...] = turned[1] + turned[2]
    for copy in copies[3:6]:
        copy.wait()
    here = pl.ds(pl.multiple_of(col * share, share), share)
    port_own, resist_own = turned[0, here, :], turned[1, here, :]
    for b in range(blocks):
        lane = b * symbols.shape[1] // blocks
        level = (2 * syms[0, lane : lane + 1, :] - 3).astype(F32) / 3.0
        excite = port_own[:, b : b + 1] * level - resist_own[:, b : b + 1] * cur[b] - vol[b]
        excite_ref[b] = excite.astype(BF)
    for copy in copies[6:]:
        copy.wait()


def source_kernel(meta, own, other, basis, excite_ref, message, keep_ref, ready):
    blocks, share = own.shape[:2]
    half, rank = excite_ref.shape[2], basis.shape[1] // 2
    core, row = meta[0], meta[1]
    bound = jnp.zeros((8, half), F32)
    for b in range(blocks):
        excite = chip_rows(core, own[b], other[b])
        excite_ref[b] = excite
        side = basis[b, :, pl.ds(pl.multiple_of(row * 2 * share, 2 * share), 2 * share)]
        part = jnp.dot(side, excite, preferred_element_type=F32)
        keep_ref[b] = pick(row, part[rank:], part[:rank])
        sent = pick(row, part[:rank], part[rank:])
        ready[b] = sent
        bound = jnp.maximum(bound, top(sent))
    power = exponent(bound)
    for b in range(blocks):
        message[b * rank : (b + 1) * rank, :] = encode(ready[b], power)
    put_powers(message.at[blocks * rank :, :], power, power)


def layout_kernel(meta, current, current_other, voltage, voltage_other, current_ref, voltage_ref, held, sems):
    sources = (current, current_other, voltage, voltage_other)
    copies = [pltpu.make_async_copy(source, held.at[k], sems.at[k]) for k, source in enumerate(sources)]
    for copy in copies:
        copy.start()
    for copy in copies:
        copy.wait()
    for b in range(current.shape[0]):
        current_ref[b] = chip_rows(meta[0], held[0, b], held[1, b])
        voltage_ref[b] = chip_rows(meta[0], held[2, b], held[3, b])


def stage_kernel(first, second, first_ref, second_ref, sems):
    copies = [
        pltpu.make_async_copy(first, first_ref, sems.at[0]),
        pltpu.make_async_copy(second, second_ref, sems.at[1]),
    ]
    for copy in copies:
        copy.start()
    for copy in copies:
        copy.wait()


def cluster_kernel(member, kept, got, wide_ref, message):
    blocks, ranks, _ = kept.shape
    power, _ = get_powers(got.at[blocks * ranks :, :])
    wide_ref[...] = jnp.zeros(wide_ref.shape, F32)
    for b in range(blocks):
        wide_ref[member[b]] += kept[b] + decode(got[b * ranks : (b + 1) * ranks, :], power)
    send_totals(wide_ref, message)


def add_kernel(wide, got, wide_ref, message):
    clusters, ranks, _ = wide.shape
    power, _ = get_powers(got.at[clusters * ranks :, :])
    for g in range(clusters):
        wide_ref[g] = wide[g] + decode(got[g * ranks : (g + 1) * ranks, :], power)
    send_totals(wide_ref, message)


def translate_kernel(meta, member, wide, got, translation, chosen_ref, totals, rows):
    clusters, ranks, scen = wide.shape
    row = meta[1]
    power, _ = get_powers(got.at[clusters * ranks :, :])
    for g in range(clusters):
        high, low = split(wide[g] + decode(got[g * ranks : (g + 1) * ranks, :], power))
        both = jnp.concatenate([high, low], axis=1)
        none = jnp.zeros(both.shape, BF)
        totals[2 * g * ranks : (2 * g + 1) * ranks, :] = pick(row, none, both)
        totals[(2 * g + 1) * ranks : (2 * g + 2) * ranks, :] = pick(row, both, none)
    blocks, rank = chosen_ref.shape[:2]
    for b in range(blocks):
        rows[b * rank : (b + 1) * rank, :] = translation[
            pl.ds(pl.multiple_of(member[b] * rank, rank), rank), :
        ]
    both = jnp.dot(rows[...], totals[...], preferred_element_type=F32)
    for b in range(blocks):
        block = both[b * rank : (b + 1) * rank]
        chosen_ref[b] = block[:, :scen] + block[:, scen:]


def near_kernel(meta, places, induct, induct_other, own, pair, past, part_ref, around, stacked):
    blocks, rows = own.shape[:2]
    entries, share = places.shape[1], rows // 2
    for k, side in enumerate((meta[0], 1 - meta[0])):
        here = pl.ds(pl.multiple_of(side * share, share), share)
        for n, source in enumerate((own, pair, past)):
            for b in range(blocks):
                around[k, n * blocks + b] = source[b, here, :]
        around[k, 3 * blocks] = jnp.zeros(around.shape[2:], BF)
    for t in range(blocks):
        parts = []
        for k, matrix in enumerate((induct, induct_other)):
            for j in range(entries):
                stacked[t % 2, k, j * share : (j + 1) * share, :] = around[k, places[t, j]]
            parts.append(
                lax.dot_general(
                    stacked[t % 2, k], matrix[t], (((0,), (0,)), ((), ())), preferred_element_type=F32
                )
            )
        part_ref[t] = (parts[0] + parts[1]).T


def finish_kernel(step, last, meta, part, chosen, target, *refs):
    blocks, cells, scen = part.shape
    row = meta[1]
    if last:
        message, keep_ref, ready = refs
    else:
        current, voltage, cells_ref, damp, symbols, basis = refs[:6]
        message, keep_ref, coef_ref, ready, ready_coefs, change = refs[6:]
    rows = cells // 2
    bound = jnp.zeros((8, scen), F32)
    second = jnp.zeros((8, scen), F32)
    for b in range(blocks):
        high, low = split(chosen[b])
        total = part[b] + lax.dot_general(
            jnp.concatenate([target[b], target[b]], axis=0),
            jnp.concatenate([high, low], axis=0),
            (((0,), (0,)), ((), ())),
            preferred_element_type=F32,
        )
        keep_ref[b] = pick(row, total[rows:], total[:rows])
        sent = pick(row, total[:rows], total[rows:])
        ready[b] = sent
        bound = jnp.maximum(bound, top(sent))
        if not last:
            change[b] = -damp[:, b : b + 1] * total
            here = pl.ds(pl.multiple_of(row * rows, rows), rows)
            change[b, here, :] += (
                drive(step + 1, b, blocks, symbols, cells_ref)
                - voltage[b]
                - (cells_ref[1, :, b : b + 1] + cells_ref[2, :, b : b + 1]) * current[b]
            )
    if not last:
        for b in range(blocks):
            high, low = split(change[b])
            coefs = jnp.dot(
                jnp.concatenate([basis[b], basis[b]], axis=1),
                jnp.concatenate([high, low], axis=0),
                preferred_element_type=F32,
            )
            rank = coefs.shape[0] // 2
            coef_ref[b] = pick(row, coefs[rank:], coefs[:rank])
            sent = pick(row, coefs[:rank], coefs[rank:])
            ready_coefs[b] = sent
            second = jnp.maximum(second, top(sent))
    power, second = exponent(bound), exponent(second)
    for b in range(blocks):
        message[b * rows : (b + 1) * rows, :] = encode(ready[b], power)
    if not last:
        start, rank = blocks * rows, ready_coefs.shape[1]
        for b in range(blocks):
            message[start + b * rank : start + (b + 1) * rank, :] = encode(ready_coefs[b], second)
    put_powers(message.at[message.shape[0] - TILE :, :], power, second)


def update_kernel(step, last, *refs):
    if last:
        meta, current, voltage, kept, got, cells, mine_ref, sent_ref = refs
    else:
        member, current, voltage, kept, got, cells, coefs, symbols = refs[:8]
        current_ref, voltage_ref, excite_ref, wide_ref, message = refs[8:]
    blocks, rows, _ = current.shape
    power, second = get_powers(got.at[got.shape[0] - TILE :, :])
    for b in range(blocks):
        cur = current[b] + (kept[b] + decode(got[b * rows : (b + 1) * rows, :], power))
        vol = voltage[b] + cells[2, :, b : b + 1] * cur
        if last:
            for k, value in enumerate((cur, vol)):
                low, high = value[: rows // 2], value[rows // 2 :]
                mine_ref[k, b] = pick(meta[0], high, low)
                sent_ref[k, b] = pick(meta[0], low, high)
        else:
            current_ref[b] = cur
            voltage_ref[b] = vol
            excite = drive(step + 1, b, blocks, symbols, cells) - cells[1, :, b : b + 1] * cur - vol
            excite_ref[b] = excite.astype(BF)
    if not last:
        wide_ref[...] = jnp.zeros(wide_ref.shape, F32)
        start, ranks = blocks * rows, coefs.shape[1]
        for b in range(blocks):
            wide_ref[member[b]] += coefs[b] + decode(got[start + b * ranks : start + (b + 1) * ranks, :], second)
        send_totals(wide_ref, message)


def final_kernel(meta, mine, got, current_ref, voltage_ref):
    for k, result in enumerate((current_ref, voltage_ref)):
        for b in range(mine.shape[1]):
            own, other = mine[k, b], got[k, b]
            result[b] = jnp.concatenate([pick(meta[0], other, own), pick(meta[0], own, other)], axis=1)


def swap(array, axis, distance):
    count = lax.axis_size(axis)
    return lax.ppermute(array, axis, [(i, i ^ distance) for i in range(count)])


def pass_on(array, axis):
    count = lax.axis_size(axis)
    up = [(i, i + 2) for i in range(0, count - 2, 2)]
    down = [(i, i - 2) for i in range(3, count, 2)]
    return lax.ppermute(array, axis, up + down)


def per_device(
    current,
    voltage,
    resistance,
    elastance,
    port_gain,
    symbols,
    neighbours,
    live_counts,
    membership,
    inductance_near,
    source_basis,
    target_basis,
    translation,
):
    blocks, entries = neighbours.shape
    share, cells = inductance_near.shape[2:]
    scen = current.shape[2]
    rank = source_basis.shape[1]
    groups = lax.axis_size("cells")
    rows, half, hrank = 2 * share, scen // 2, rank // 2
    group, col = lax.axis_index("cells"), lax.axis_index("cols")
    core = col & 1
    meta = jnp.stack([core, col >> 1, col]).astype(jnp.int32)
    member = membership[:, 0]
    owner = neighbours // blocks
    slot = jnp.where(owner == group, 0, jnp.where(owner == (group ^ 1), 1, 2))
    live = jnp.arange(entries, dtype=jnp.int32)[None, :] < live_counts[:, None]
    places = jnp.where(live, slot * blocks + neighbours % blocks, 3 * blocks).astype(jnp.int32)
    induct = inductance_near.reshape(blocks, entries * share, cells)
    symbols_half = lax.dynamic_slice_in_dim(symbols, core * half, half, 2)

    state_f32 = shaped((blocks, rows, half), F32)
    state_bf = shaped((blocks, rows, half), BF)
    wide_f32 = shaped((CLUSTERS, hrank, half), F32)
    wide_msg = shaped((CLUSTERS * hrank + TILE, half), I16)
    coef_f32 = shaped((blocks, hrank, half), F32)

    first, columns, damp, source_basis, target_basis = local_call(
        first_kernel,
        (
            meta,
            current,
            voltage,
            port_gain,
            resistance,
            elastance,
            symbols,
            source_basis,
            target_basis,
        ),
        (
            shaped((blocks, share, scen), BF),
            shaped((3, rows, blocks), F32),
            shaped((cells, blocks), F32),
            shaped(source_basis.shape, BF),
            shaped(target_basis.shape, BF),
        ),
        scratch=(
            pltpu.VMEM(current.shape, F32),
            pltpu.VMEM(voltage.shape, F32),
            pltpu.VMEM((3,) + port_gain.shape, F32),
            pltpu.VMEM(symbols.shape, jnp.int32),
            pltpu.VMEM((3, cells, blocks), F32),
            pltpu.SemaphoreType.DMA((8,)),
        ),
        scalars=1,
        left=tuple(range(1, 9)),
    )
    first_other = swap(first, "cols", 1)
    excite, send, kept = local_call(
        source_kernel,
        (meta, first, first_other, source_basis),
        (state_bf, shaped((blocks * hrank + TILE, half), I16), coef_f32),
        scratch=(pltpu.VMEM((blocks, hrank, half), F32),),
        scalars=1,
    )
    for step in range(STEPS):
        last = step == STEPS - 1
        pair = swap(excite, "cells", 1)
        if step == 0:
            got = swap(send, "cols", 2)
            later, _ = lax.optimization_barrier(((current, voltage, induct), send))
            current_other, voltage_other, induct_other = (swap(a, "cols", 1) for a in later)
            wide, send = local_call(cluster_kernel, (member, kept, got), (wide_f32, wide_msg), scalars=1)
        distance = 2
        while distance < groups:
            got = swap(send, "cells", distance)
            if step == 0 and distance == 2:
                got, pair = lax.optimization_barrier((got, pair))
            wide, send = local_call(
                add_kernel,
                (wide, got),
                (wide_f32, wide_msg),
                after=(current,) if step == 0 and distance == 4 else (),
            )
            if distance == 2:
                pair, _ = lax.optimization_barrier((pair, send))
            distance *= 2
            if step > 0 or distance != 4:
                continue
            current, voltage = local_call(
                layout_kernel,
                (meta, current, current_other, voltage, voltage_other),
                (state_f32, state_f32),
                scratch=(pltpu.VMEM((4,) + current.shape, F32), pltpu.SemaphoreType.DMA((4,))),
                scalars=1,
                left=(1, 2, 3, 4),
                after=(send,),
            )
        got = swap(send, "cells", 1)
        if step == 0:
            induct_other, translation = local_call(
                stage_kernel,
                (induct_other, translation),
                (shaped(induct.shape, BF), shaped(translation.shape, BF)),
                scratch=(pltpu.SemaphoreType.DMA((2,)),),
                left=(0, 1),
                after=(send,),
            )
        (chosen,) = local_call(
            translate_kernel,
            (meta, member, wide, got, translation),
            (shaped((blocks, rank, half), F32),),
            scratch=(
                pltpu.VMEM((CLUSTERS * rank, scen), BF),
                pltpu.VMEM((blocks * rank, CLUSTERS * rank), BF),
            ),
            scalars=2,
        )
        past = pass_on(pair, "cells")
        (part,) = local_call(
            near_kernel,
            (meta, places, induct, induct_other, excite, pair, past),
            (shaped((blocks, cells, half), F32),),
            scratch=(
                pltpu.VMEM((2, 3 * blocks + 1, share, half), BF),
                pltpu.VMEM((2, 2, entries * share, half), BF),
            ),
            scalars=2,
        )
        if last:
            send, kept = local_call(
                functools.partial(finish_kernel, step, last),
                (meta, part, chosen, target_basis),
                (shaped((blocks * rows + TILE, half), I16), state_f32),
                scratch=(pltpu.VMEM((blocks, rows, half), F32),),
                scalars=1,
            )
            got = swap(send, "cols", 2)
            mine, send = local_call(
                functools.partial(update_kernel, step, last),
                (meta, current, voltage, kept, got, columns),
                (shaped((2, blocks, share, half), F32),) * 2,
                scalars=1,
            )
        else:
            send, kept, coefs = local_call(
                functools.partial(finish_kernel, step, last),
                (meta, part, chosen, target_basis, current, voltage, columns, damp, symbols_half, source_basis),
                (shaped((blocks * (rows + hrank) + TILE, half), I16), state_f32, coef_f32),
                scratch=(
                    pltpu.VMEM((blocks, rows, half), F32),
                    pltpu.VMEM((blocks, hrank, half), F32),
                    pltpu.VMEM((blocks, cells, half), F32),
                ),
                scalars=1,
            )
            got = swap(send, "cols", 2)
            current, voltage, excite, wide, send = local_call(
                functools.partial(update_kernel, step, last),
                (member, current, voltage, kept, got, columns, coefs, symbols_half),
                (state_f32, state_f32, state_bf, wide_f32, wide_msg),
                scalars=1,
            )
    got = swap(send, "cols", 1)
    return local_call(
        final_kernel, (meta, mine, got), (shaped((blocks, share, scen), F32),) * 2, scalars=1
    )


def solution(mesh):
    placed = (
        P("cells", "cols", None),
        P("cells", "cols", None),
        P("cells", None),
        P("cells", None),
        P("cells", None),
        P(None, "cells", None),
        P("cells", None),
        P("cells"),
        P("cells", None),
        P("cells", None, "cols", None),
        P("cells", None, None),
        P("cells", None, None),
        P(),
    )
    return jax.shard_map(
        per_device,
        mesh=mesh,
        in_specs=placed,
        out_specs=(P("cells", "cols", None), P("cells", "cols", None)),
        check_vma=False,
    )
```

time: 133 us -> 116 us (0.87)
  waiting for transfers between devices: 60.8 us -> 50.7 us
  local copies, waits for them, and re-layouts: 8.96 us -> 1.47 us
  Pallas kernels: 23.4 us -> 29.9 us
  starting transfers between devices: 37.8 us -> 32.2 us
    ppermute x20 -> x21, waiting for transfers between devices: 58.8 us -> 50.7 us  [swap(): return lax.ppermute(array, axis, [(i, i ^ distance) for i in range(count)])]
    ppermute x20 -> x21, starting transfers between devices: 28.8 us -> 21.2 us  [swap(): return lax.ppermute(array, axis, [(i, i ^ distance) for i in range(count)])]
    unnamed x38 -> x14, local copies, waits for them, and re-layouts: 8.96 us -> 1.47 us
    pallas_call x24, Pallas kernels: 23.4 us -> 29.9 us  [local_call(): pl.pallas_call(run, out_shape=tuple(outs), in_specs=specs, out_specs=tupl...]
    ppermute x3, starting transfers between devices: 8.96 us -> 11.1 us  [pass_on(): return lax.ppermute(array, axis, up + down)]
    ppermute x3, waiting for transfers between devices: 2.05 us -> 0.01 us  [pass_on(): return lax.ppermute(array, axis, up + down)]
  transfers between devices with their start and end apart: 23 -> 24, of which waited for: 18 -> 15; matrix products, arithmetic and copies ran while one was open for 0% -> 0% of each run, Pallas kernels for 4% -> 8%
where the time goes in v2:
time: 116 us; the launch traced here: 115 us
  waiting for transfers between devices  50.7 us (44%)
  starting transfers between devices  32.2 us (28%)
  Pallas kernels  29.9 us (26%)
  local copies, waits for them, and re-layouts  1.47 us (1%)
    ppermute x21, waiting for transfers between devices, swap(): return lax.ppermute(array, axis, [(i, i ^ distance) for i in range(count)])  50.7 us
    pallas_call x24, Pallas kernels, local_call(): pl.pallas_call(run, out_shape=tuple(outs), in_specs=specs, out_specs=tupl...  29.9 us
    ppermute x21, starting transfers between devices, swap(): return lax.ppermute(array, axis, [(i, i ^ distance) for i in range(count)])  21.2 us
    ppermute x3, starting transfers between devices, pass_on(): return lax.ppermute(array, axis, up + down)  11.1 us
  transfers between devices with their start and end apart: 24, of which 15 were waited for; matrix products, arithmetic and copies ran while one was open for 0% of the time, Pallas kernels for 8%

profile of v2, /device:TPU:0, one launch (start us, length us, event | category | flops | bytes accessed | tf_op | source)
XLA Modules:
  0.0 115.4 jit_solution(388885393225151823)
XLA Ops:
  0.7 2.1 %first_kernel.1 = (bf16[8,64,256]{2,1,0:T(8,128)(2,1)S(1)}, f32[3,128,8]{2,1,0:T(8,128)S(1)}, f32[256,8]{1,0:T(8,128)S(1)}, bf16[8,64,256]{2,1,0:T(8,128)(2,1)S(1)}, bf16[8,64,256]{2,1,0:T(8,128)(2,1)S(1)}) custom-call(s32[3]{0:T(128)S(1)} %pad_add_fusion.refs_0_, f32[8,64,256]{2,1,0:T(8,128)} %refs_1_.4, f32[8,64,256]{2,1,0:T(8,128)} %refs_3_.3, ...), custom_call_target="tpu_custom_call" | custom-call | bytes 2416652 | tf_op jit(solution)/shard_map/first_kernel/pallas_call | solution.py:33
  6.3 2.6 %collective-permute-start.5 = (bf16[8,128,128]{2,1,0:T(8,128)(2,1)S(1)}, bf16[8,128,128]{2,1,0:T(8,128)(2,1)S(1)}, u32[]{:S(2)}, u32[]{:S(2)}) collective-permute-start(bf16[8,128,128]{2,1,0:T(8,128)(2,1)S(1)} %get-tuple-element.64.refs_4_), channel_id=1, source_target_pairs={{0,4},{4,0},{8,12},{12,8},{16,20},{20,16},{24,28},{28,24},{1,5},{5... | collective-permute-start | bytes 786440 | tf_op jit(solution)/shard_map/ppermute | solution.py:335
  10.4 2.8 %collective-permute-done.3.refs_2_ = s16[272,128]{1,0:T(8,128)(2,1)S(1)} collective-permute-done((s16[272,128]{1,0:T(8,128)(2,1)S(1)}, s16[272,128]{1,0:T(8,128)(2,1)S(1)}, u32[]{:S(2)}, u32[]{:S(2)}) %collective-permute-start.3) | collective-permute-done | bytes 69664 | tf_op jit(solution)/shard_map/ppermute | solution.py:335
  16.2 3.4 %collective-permute-done.4.refs_1_ = s16[528,128]{1,0:T(8,128)(2,1)S(1)} collective-permute-done((s16[528,128]{1,0:T(8,128)(2,1)S(1)}, s16[528,128]{1,0:T(8,128)(2,1)S(1)}, u32[]{:S(2)}, u32[]{:S(2)}) %collective-permute-start.4) | collective-permute-done | bytes 135200 | tf_op jit(solution)/shard_map/ppermute | solution.py:335
  19.7 2.7 %collective-permute-start.7 = (s16[528,128]{1,0:T(8,128)(2,1)S(1)}, s16[528,128]{1,0:T(8,128)(2,1)S(1)}, u32[]{:S(2)}, u32[]{:S(2)}) collective-permute-start(s16[528,128]{1,0:T(8,128)(2,1)S(1)} %get-tuple-element.66.refs_5_), channel_id=1, source_target_pairs={{0,16},{4,20},{8,24},{12,28},{16,0},{20,4},{24,8},{28,12},{1,17},{... | collective-permute-start | bytes 405512 | tf_op jit(solution)/shard_map/ppermute | solution.py:335
  22.4 3.5 %collective-permute-start.8 = (bf16[8,128,128]{2,1,0:T(8,128)(2,1)S(1)}, bf16[8,128,128]{2,1,0:T(8,128)(2,1)S(1)}, u32[]{:S(2)}, u32[]{:S(2)}) collective-permute-start(bf16[8,128,128]{2,1,0:T(8,128)(2,1)S(1)} %collective-permute-done.5.refs_5_), channel_id=1, source_target_pairs={{0,8},{8,16},{16,24},{12,4},{20,12},{28,20},{1,9},{9,17},{17,25},{... | collective-permute-start | bytes 786440 | tf_op jit(solution)/shard_map/ppermute | solution.py:342
  26.7 2.2 %layout_kernel.1 = (f32[8,128,128]{2,1,0:T(8,128)S(1)}, f32[8,128,128]{2,1,0:T(8,128)S(1)}) custom-call(s32[3]{0:T(128)S(1)} %pad_add_fusion.refs_0_, f32[8,64,256]{2,1,0:T(8,128)} %refs_1_.4, f32[8,64,256]{2,1,0:T(8,128)} %copy-done.3, f32[8,64,256]{2,1,0:T(8,128)} %refs_3_.3, f32[8,64,256]{2,1,0:T(8,128)} %collective-permute-done.2.refs_4_, ...), custom_call_target="tpu_custom_call" | custom-call | bytes 3145740 | tf_op jit(solution)/shard_map/layout_kernel/pallas_call | solution.py:33
  29.2 3.0 %stage_kernel.1 = (bf16[8,1024,256]{2,1,0:T(8,128)(2,1)S(1)}, bf16[1024,1024]{1,0:T(8,128)(2,1)S(1)}) custom-call(bf16[8,1024,256]{2,1,0:T(8,128)(2,1)} %collective-permute-done.6.refs_0_, bf16[1024,1024]{1,0:T(8,128)(2,1)} %refs_1_.5, s16[528,128]{1,0:T(8,128)(2,1)S(1)} %get-tuple-element.71.refs_2_), custom_call_target="tpu_custom_call" | custom-call | bytes 12582912 | tf_op jit(solution)/shard_map/stage_kernel/pallas_call | solution.py:33
  32.2 1.9 %collective-permute-done.9.refs_3_ = s16[528,128]{1,0:T(8,128)(2,1)S(1)} collective-permute-done((s16[528,128]{1,0:T(8,128)(2,1)S(1)}, s16[528,128]{1,0:T(8,128)(2,1)S(1)}, u32[]{:S(2)}, u32[]{:S(2)}) %collective-permute-start.9) | collective-permute-done | bytes 135200 | tf_op jit(solution)/shard_map/ppermute | solution.py:335
  35.1 2.9 %near_kernel.3.refs_1_ = f32[8,256,128]{2,1,0:T(8,128)S(1)} custom-call(s32[3]{0:T(128)S(1)} %pad_add_fusion.refs_0_, s32[8,16]{1,0:T(8,128)S(1)} %fusion.1.refs_1_, bf16[8,1024,256]{2,1,0:T(8,128)(2,1)S(1)} %bitcast.6, bf16[8,1024,256]{2,1,0:T(8,128)(2,1)S(1)} %get-tuple-element.72.refs_3_, bf16[8,128,128]{2,1,0:T(8,128)(2,1)S(1)} %get-tuple-element.64.refs_4_, ...), custom_call_target="tpu_custom_call" | custom-call | bytes 10224140 | tf_op jit(solution)/shard_map/near_kernel/pallas_call | solution.py:33
  41.3 5.6 %collective-permute-done.10.refs_4_ = s16[1296,128]{1,0:T(8,128)(2,1)S(1)} collective-permute-done((s16[1296,128]{1,0:T(8,128)(2,1)S(1)}, s16[1296,128]{1,0:T(8,128)(2,1)S(1)}, u32[]{:S(2)}, u32[]{:S(2)}) %collective-permute-start.10) | collective-permute-done | bytes 331808 | tf_op jit(solution)/shard_map/ppermute | solution.py:335
  49.0 5.6 %collective-permute-done.12.refs_1_ = s16[528,128]{1,0:T(8,128)(2,1)S(1)} collective-permute-done((s16[528,128]{1,0:T(8,128)(2,1)S(1)}, s16[528,128]{1,0:T(8,128)(2,1)S(1)}, u32[]{:S(2)}, u32[]{:S(2)}) %collective-permute-start.12) | collective-permute-done | bytes 135200 | tf_op jit(solution)/shard_map/ppermute | solution.py:335
  56.1 4.4 %collective-permute-start.13 = (bf16[8,128,128]{2,1,0:T(8,128)(2,1)S(1)}, bf16[8,128,128]{2,1,0:T(8,128)(2,1)S(1)}, u32[]{:S(2)}, u32[]{:S(2)}) collective-permute-start(bf16[8,128,128]{2,1,0:T(8,128)(2,1)S(1)} %collective-permute-done.11.refs_5_), channel_id=1, source_target_pairs={{0,8},{8,16},{16,24},{12,4},{20,12},{28,20},{1,9},{9,17},{17,25},{... | collective-permute-start | bytes 786440 | tf_op jit(solution)/shard_map/ppermute | solution.py:342
  63.5 3.8 %collective-permute-done.15.refs_3_ = s16[528,128]{1,0:T(8,128)(2,1)S(1)} collective-permute-done((s16[528,128]{1,0:T(8,128)(2,1)S(1)}, s16[528,128]{1,0:T(8,128)(2,1)S(1)}, u32[]{:S(2)}, u32[]{:S(2)}) %collective-permute-start.15) | collective-permute-done | bytes 135200 | tf_op jit(solution)/shard_map/ppermute | solution.py:335
  68.4 2.9 %near_kernel.4.refs_1_ = f32[8,256,128]{2,1,0:T(8,128)S(1)} custom-call(s32[3]{0:T(128)S(1)} %pad_add_fusion.refs_0_, s32[8,16]{1,0:T(8,128)S(1)} %fusion.1.refs_1_, bf16[8,1024,256]{2,1,0:T(8,128)(2,1)S(1)} %bitcast.7, bf16[8,1024,256]{2,1,0:T(8,128)(2,1)S(1)} %get-tuple-element.72.refs_3_, bf16[8,128,128]{2,1,0:T(8,128)(2,1)S(1)} %get-tuple-element.85.refs_4_, ...), custom_call_target="tpu_custom_call" | custom-call | bytes 10224140 | tf_op jit(solution)/shard_map/near_kernel/pallas_call | solution.py:33
  71.3 1.7 %finish_kernel.4 = (s16[1296,128]{1,0:T(8,128)(2,1)S(1)}, f32[8,128,128]{2,1,0:T(8,128)S(1)}, f32[8,32,128]{2,1,0:T(8,128)S(1)}) custom-call(s32[3]{0:T(128)S(1)} %pad_add_fusion.refs_0_, f32[8,256,128]{2,1,0:T(8,128)S(1)} %near_kernel.4.refs_1_, f32[8,64,128]{2,1,0:T(8,128)S(1)} %translate_kernel.4.refs_2_, ...), custom_call_target="tpu_custom_call" | custom-call | bytes 3897356 | tf_op jit(solution)/shard_map/finish_kernel/pallas_call | solution.py:33
  74.6 5.6 %collective-permute-done.16.refs_4_ = s16[1296,128]{1,0:T(8,128)(2,1)S(1)} collective-permute-done((s16[1296,128]{1,0:T(8,128)(2,1)S(1)}, s16[1296,128]{1,0:T(8,128)(2,1)S(1)}, u32[]{:S(2)}, u32[]{:S(2)}) %collective-permute-start.16) | collective-permute-done | bytes 331808 | tf_op jit(solution)/shard_map/ppermute | solution.py:335
  82.5 5.0 %collective-permute-done.18.refs_1_ = s16[528,128]{1,0:T(8,128)(2,1)S(1)} collective-permute-done((s16[528,128]{1,0:T(8,128)(2,1)S(1)}, s16[528,128]{1,0:T(8,128)(2,1)S(1)}, u32[]{:S(2)}, u32[]{:S(2)}) %collective-permute-start.18) | collective-permute-done | bytes 135200 | tf_op jit(solution)/shard_map/ppermute | solution.py:335
  89.1 3.2 %collective-permute-start.19 = (bf16[8,128,128]{2,1,0:T(8,128)(2,1)S(1)}, bf16[8,128,128]{2,1,0:T(8,128)(2,1)S(1)}, u32[]{:S(2)}, u32[]{:S(2)}) collective-permute-start(bf16[8,128,128]{2,1,0:T(8,128)(2,1)S(1)} %collective-permute-done.17.refs_5_), channel_id=1, source_target_pairs={{0,8},{8,16},{16,24},{12,4},{20,12},{28,20},{1,9},{9,17},{17,25},{... | collective-permute-start | bytes 786440 | tf_op jit(solution)/shard_map/ppermute | solution.py:342
  92.3 2.1 %collective-permute-done.20.refs_1_ = s16[528,128]{1,0:T(8,128)(2,1)S(1)} collective-permute-done((s16[528,128]{1,0:T(8,128)(2,1)S(1)}, s16[528,128]{1,0:T(8,128)(2,1)S(1)}, u32[]{:S(2)}, u32[]{:S(2)}) %collective-permute-start.20) | collective-permute-done | bytes 135200 | tf_op jit(solution)/shard_map/ppermute | solution.py:335
  95.5 4.2 %collective-permute-done.21.refs_3_ = s16[528,128]{1,0:T(8,128)(2,1)S(1)} collective-permute-done((s16[528,128]{1,0:T(8,128)(2,1)S(1)}, s16[528,128]{1,0:T(8,128)(2,1)S(1)}, u32[]{:S(2)}, u32[]{:S(2)}) %collective-permute-start.21) | collective-permute-done | bytes 135200 | tf_op jit(solution)/shard_map/ppermute | solution.py:335
  100.7 2.9 %near_kernel.5.refs_1_ = f32[8,256,128]{2,1,0:T(8,128)S(1)} custom-call(s32[3]{0:T(128)S(1)} %pad_add_fusion.refs_0_, s32[8,16]{1,0:T(8,128)S(1)} %fusion.1.refs_1_, bf16[8,1024,256]{2,1,0:T(8,128)(2,1)S(1)} %bitcast.8, bf16[8,1024,256]{2,1,0:T(8,128)(2,1)S(1)} %get-tuple-element.72.refs_3_, bf16[8,128,128]{2,1,0:T(8,128)(2,1)S(1)} %get-tuple-element.98.refs_4_, ...), custom_call_target="tpu_custom_call" | custom-call | bytes 10224140 | tf_op jit(solution)/shard_map/near_kernel/pallas_call | solution.py:33
  106.1 4.9 %collective-permute-done.22.refs_4_ = s16[1040,128]{1,0:T(8,128)(2,1)S(1)} collective-permute-done((s16[1040,128]{1,0:T(8,128)(2,1)S(1)}, s16[1040,128]{1,0:T(8,128)(2,1)S(1)}, u32[]{:S(2)}, u32[]{:S(2)}) %collective-permute-start.22) | collective-permute-done | bytes 266272 | tf_op jit(solution)/shard_map/ppermute | solution.py:335
  111.9 1.9 %collective-permute-done.23.refs_2_ = f32[2,8,64,128]{3,2,1,0:T(8,128)S(1)} collective-permute-done((f32[2,8,64,128]{3,2,1,0:T(8,128)S(1)}, f32[2,8,64,128]{3,2,1,0:T(8,128)S(1)}, u32[]{:S(2)}, u32[]{:S(2)}) %collective-permute-start.23) | collective-permute-done | bytes 524320 | tf_op jit(solution)/shard_map/ppermute | solution.py:335
  (65 shorter events, 33.4 us)
Async XLA Ops:
  2.9 1.7 %collective-permute-start = (bf16[8,64,256]{2,1,0:T(8,128)(2,1)S(1)}, bf16[8,64,256]{2,1,0:T(8,128)(2,1)S(1)}, u32[]{:S(2)}, u32[]{:S(2)}) collective-permute-start(bf16[8,64,256]{2,1,0:T(8,128)(2,1)S(1)} %get-tuple-element.56.refs_1_), channel_id=1, source_target_pairs={{0,1},{1,0},{2,3},{3,2},{4,5},{5,4},{6,7},{7,6},{8,9},{9,8},{10,11... | collective-permute-start | bytes 786440 | tf_op jit(solution)/shard_map/ppermute | solution.py:335
  5.3 23.8 %collective-permute-start.6 = (bf16[8,1024,256]{2,1,0:T(8,128)(2,1)}, bf16[8,1024,256]{2,1,0:T(8,128)(2,1)}, u32[]{:S(2)}, u32[]{:S(2)}) collective-permute-start(bf16[8,1024,256]{2,1,0:T(8,128)(2,1)} %bitcast.5), channel_id=1, source_target_pairs={{0,1},{1,0},{2,3},{3,2},{4,5},{5,4},{6,7},{7,6},{8,9},{9,8},{10,11... | collective-permute-start | bytes 12582920 | tf_op jit(solution)/shard_map/ppermute | solution.py:335
  5.8 20.1 %collective-permute-start.1 = (f32[8,64,256]{2,1,0:T(8,128)}, f32[8,64,256]{2,1,0:T(8,128)S(1)}, u32[]{:S(2)}, u32[]{:S(2)}) collective-permute-start(f32[8,64,256]{2,1,0:T(8,128)} %refs_1_.4), channel_id=1, source_target_pairs={{0,1},{1,0},{2,3},{3,2},{4,5},{5,4},{6,7},{7,6},{8,9},{9,8},{10,11... | collective-permute-start | bytes 1572872 | tf_op jit(solution)/shard_map/ppermute | solution.py:335
  5.9 20.8 %collective-permute-start.2 = (f32[8,64,256]{2,1,0:T(8,128)}, f32[8,64,256]{2,1,0:T(8,128)}, u32[]{:S(2)}, u32[]{:S(2)}) collective-permute-start(f32[8,64,256]{2,1,0:T(8,128)} %refs_3_.3), channel_id=1, source_target_pairs={{0,1},{1,0},{2,3},{3,2},{4,5},{5,4},{6,7},{7,6},{8,9},{9,8},{10,11... | collective-permute-start | bytes 1572872 | tf_op jit(solution)/shard_map/ppermute | solution.py:335
  6.3 13.3 %collective-permute-start.5 = (bf16[8,128,128]{2,1,0:T(8,128)(2,1)S(1)}, bf16[8,128,128]{2,1,0:T(8,128)(2,1)S(1)}, u32[]{:S(2)}, u32[]{:S(2)}) collective-permute-start(bf16[8,128,128]{2,1,0:T(8,128)(2,1)S(1)} %get-tuple-element.64.refs_4_), channel_id=1, source_target_pairs={{0,4},{4,0},{8,12},{12,8},{16,20},{20,16},{24,28},{28,24},{1,5},{5... | collective-permute-start | bytes 786440 | tf_op jit(solution)/shard_map/ppermute | solution.py:335
  8.9 4.3 %collective-permute-start.3 = (s16[272,128]{1,0:T(8,128)(2,1)S(1)}, s16[272,128]{1,0:T(8,128)(2,1)S(1)}, u32[]{:S(2)}, u32[]{:S(2)}) collective-permute-start(s16[272,128]{1,0:T(8,128)(2,1)S(1)} %get-tuple-element.58), channel_id=1, source_target_pairs={{0,2},{1,3},{2,0},{3,1},{4,6},{5,7},{6,4},{7,5},{8,10},{9,11},{10,... | collective-permute-start | bytes 208904 | tf_op jit(solution)/shard_map/ppermute | solution.py:335
  14.5 5.1 %collective-permute-start.4 = (s16[528,128]{1,0:T(8,128)(2,1)S(1)}, s16[528,128]{1,0:T(8,128)(2,1)S(1)}, u32[]{:S(2)}, u32[]{:S(2)}) collective-permute-start(s16[528,128]{1,0:T(8,128)(2,1)S(1)} %get-tuple-element.63), channel_id=1, source_target_pairs={{0,8},{4,12},{8,0},{12,4},{16,24},{20,28},{24,16},{28,20},{1,9},{5... | collective-permute-start | bytes 405512 | tf_op jit(solution)/shard_map/ppermute | solution.py:335
  19.7 9.2 %collective-permute-start.7 = (s16[528,128]{1,0:T(8,128)(2,1)S(1)}, s16[528,128]{1,0:T(8,128)(2,1)S(1)}, u32[]{:S(2)}, u32[]{:S(2)}) collective-permute-start(s16[528,128]{1,0:T(8,128)(2,1)S(1)} %get-tuple-element.66.refs_5_), channel_id=1, source_target_pairs={{0,16},{4,20},{8,24},{12,28},{16,0},{20,4},{24,8},{28,12},{1,17},{... | collective-permute-start | bytes 405512 | tf_op jit(solution)/shard_map/ppermute | solution.py:335
  22.4 12.7 %collective-permute-start.8 = (bf16[8,128,128]{2,1,0:T(8,128)(2,1)S(1)}, bf16[8,128,128]{2,1,0:T(8,128)(2,1)S(1)}, u32[]{:S(2)}, u32[]{:S(2)}) collective-permute-start(bf16[8,128,128]{2,1,0:T(8,128)(2,1)S(1)} %collective-permute-done.5.refs_5_), channel_id=1, source_target_pairs={{0,8},{8,16},{16,24},{12,4},{20,12},{28,20},{1,9},{9,17},{17,25},{... | collective-permute-start | bytes 786440 | tf_op jit(solution)/shard_map/ppermute | solution.py:342
  29.0 5.1 %collective-permute-start.9 = (s16[528,128]{1,0:T(8,128)(2,1)S(1)}, s16[528,128]{1,0:T(8,128)(2,1)S(1)}, u32[]{:S(2)}, u32[]{:S(2)}) collective-permute-start(s16[528,128]{1,0:T(8,128)(2,1)S(1)} %get-tuple-element.71.refs_2_), channel_id=1, source_target_pairs={{0,4},{4,0},{8,12},{12,8},{16,20},{20,16},{24,28},{28,24},{1,5},{5... | collective-permute-start | bytes 405512 | tf_op jit(solution)/shard_map/ppermute | solution.py:335
  39.8 7.2 %collective-permute-start.10 = (s16[1296,128]{1,0:T(8,128)(2,1)S(1)}, s16[1296,128]{1,0:T(8,128)(2,1)S(1)}, u32[]{:S(2)}, u32[]{:S(2)}) collective-permute-start(s16[1296,128]{1,0:T(8,128)(2,1)S(1)} %get-tuple-element.81), channel_id=1, source_target_pairs={{0,2},{1,3},{2,0},{3,1},{4,6},{5,7},{6,4},{7,5},{8,10},{9,11},{10,... | collective-permute-start | bytes 995336 | tf_op jit(solution)/shard_map/ppermute | solution.py:335
  48.0 8.1 %collective-permute-start.11 = (bf16[8,128,128]{2,1,0:T(8,128)(2,1)S(1)}, bf16[8,128,128]{2,1,0:T(8,128)(2,1)S(1)}, u32[]{:S(2)}, u32[]{:S(2)}) collective-permute-start(bf16[8,128,128]{2,1,0:T(8,128)(2,1)S(1)} %get-tuple-element.85.refs_4_), channel_id=1, source_target_pairs={{0,4},{4,0},{8,12},{12,8},{16,20},{20,16},{24,28},{28,24},{1,5},{5... | collective-permute-start | bytes 786440 | tf_op jit(solution)/shard_map/ppermute | solution.py:335
  48.2 6.5 %collective-permute-start.12 = (s16[528,128]{1,0:T(8,128)(2,1)S(1)}, s16[528,128]{1,0:T(8,128)(2,1)S(1)}, u32[]{:S(2)}, u32[]{:S(2)}) collective-permute-start(s16[528,128]{1,0:T(8,128)(2,1)S(1)} %get-tuple-element.87), channel_id=1, source_target_pairs={{0,8},{4,12},{8,0},{12,4},{16,24},{20,28},{24,16},{28,20},{1,9},{5... | collective-permute-start | bytes 405512 | tf_op jit(solution)/shard_map/ppermute | solution.py:335
  54.7 7.4 %collective-permute-start.14 = (s16[528,128]{1,0:T(8,128)(2,1)S(1)}, s16[528,128]{1,0:T(8,128)(2,1)S(1)}, u32[]{:S(2)}, u32[]{:S(2)}) collective-permute-start(s16[528,128]{1,0:T(8,128)(2,1)S(1)} %get-tuple-element.88), channel_id=1, source_target_pairs={{0,16},{4,20},{8,24},{12,28},{16,0},{20,4},{24,8},{28,12},{1,17},{... | collective-permute-start | bytes 405512 | tf_op jit(solution)/shard_map/ppermute | solution.py:335
  56.1 12.3 %collective-permute-start.13 = (bf16[8,128,128]{2,1,0:T(8,128)(2,1)S(1)}, bf16[8,128,128]{2,1,0:T(8,128)(2,1)S(1)}, u32[]{:S(2)}, u32[]{:S(2)}) collective-permute-start(bf16[8,128,128]{2,1,0:T(8,128)(2,1)S(1)} %collective-permute-done.11.refs_5_), channel_id=1, source_target_pairs={{0,8},{8,16},{16,24},{12,4},{20,12},{28,20},{1,9},{9,17},{17,25},{... | collective-permute-start | bytes 786440 | tf_op jit(solution)/shard_map/ppermute | solution.py:342
  62.3 5.1 %collective-permute-start.15 = (s16[528,128]{1,0:T(8,128)(2,1)S(1)}, s16[528,128]{1,0:T(8,128)(2,1)S(1)}, u32[]{:S(2)}, u32[]{:S(2)}) collective-permute-start(s16[528,128]{1,0:T(8,128)(2,1)S(1)} %get-tuple-element.92), channel_id=1, source_target_pairs={{0,4},{4,0},{8,12},{12,8},{16,20},{20,16},{24,28},{28,24},{1,5},{5... | collective-permute-start | bytes 405512 | tf_op jit(solution)/shard_map/ppermute | solution.py:335
  73.0 7.2 %collective-permute-start.16 = (s16[1296,128]{1,0:T(8,128)(2,1)S(1)}, s16[1296,128]{1,0:T(8,128)(2,1)S(1)}, u32[]{:S(2)}, u32[]{:S(2)}) collective-permute-start(s16[1296,128]{1,0:T(8,128)(2,1)S(1)} %get-tuple-element.94), channel_id=1, source_target_pairs={{0,2},{1,3},{2,0},{3,1},{4,6},{5,7},{6,4},{7,5},{8,10},{9,11},{10,... | collective-permute-start | bytes 995336 | tf_op jit(solution)/shard_map/ppermute | solution.py:335
  81.2 7.9 %collective-permute-start.17 = (bf16[8,128,128]{2,1,0:T(8,128)(2,1)S(1)}, bf16[8,128,128]{2,1,0:T(8,128)(2,1)S(1)}, u32[]{:S(2)}, u32[]{:S(2)}) collective-permute-start(bf16[8,128,128]{2,1,0:T(8,128)(2,1)S(1)} %get-tuple-element.98.refs_4_), channel_id=1, source_target_pairs={{0,4},{4,0},{8,12},{12,8},{16,20},{20,16},{24,28},{28,24},{1,5},{5... | collective-permute-start | bytes 786440 | tf_op jit(solution)/shard_map/ppermute | solution.py:335
  82.5 5.0 %collective-permute-start.18 = (s16[528,128]{1,0:T(8,128)(2,1)S(1)}, s16[528,128]{1,0:T(8,128)(2,1)S(1)}, u32[]{:S(2)}, u32[]{:S(2)}) collective-permute-start(s16[528,128]{1,0:T(8,128)(2,1)S(1)} %get-tuple-element.100), channel_id=1, source_target_pairs={{0,8},{4,12},{8,0},{12,4},{16,24},{20,28},{24,16},{28,20},{1,9},{5... | collective-permute-start | bytes 405512 | tf_op jit(solution)/shard_map/ppermute | solution.py:335
  87.6 6.9 %collective-permute-start.20 = (s16[528,128]{1,0:T(8,128)(2,1)S(1)}, s16[528,128]{1,0:T(8,128)(2,1)S(1)}, u32[]{:S(2)}, u32[]{:S(2)}) collective-permute-start(s16[528,128]{1,0:T(8,128)(2,1)S(1)} %get-tuple-element.101), channel_id=1, source_target_pairs={{0,16},{4,20},{8,24},{12,28},{16,0},{20,4},{24,8},{28,12},{1,17},{... | collective-permute-start | bytes 405512 | tf_op jit(solution)/shard_map/ppermute | solution.py:335
  89.1 11.5 %collective-permute-start.19 = (bf16[8,128,128]{2,1,0:T(8,128)(2,1)S(1)}, bf16[8,128,128]{2,1,0:T(8,128)(2,1)S(1)}, u32[]{:S(2)}, u32[]{:S(2)}) collective-permute-start(bf16[8,128,128]{2,1,0:T(8,128)(2,1)S(1)} %collective-permute-done.17.refs_5_), channel_id=1, source_target_pairs={{0,8},{8,16},{16,24},{12,4},{20,12},{28,20},{1,9},{9,17},{17,25},{... | collective-permute-start | bytes 786440 | tf_op jit(solution)/shard_map/ppermute | solution.py:342
  94.6 5.1 %collective-permute-start.21 = (s16[528,128]{1,0:T(8,128)(2,1)S(1)}, s16[528,128]{1,0:T(8,128)(2,1)S(1)}, u32[]{:S(2)}, u32[]{:S(2)}) collective-permute-start(s16[528,128]{1,0:T(8,128)(2,1)S(1)} %get-tuple-element.105), channel_id=1, source_target_pairs={{0,4},{4,0},{8,12},{12,8},{16,20},{20,16},{24,28},{28,24},{1,5},{5... | collective-permute-start | bytes 405512 | tf_op jit(solution)/shard_map/ppermute | solution.py:335
  104.6 6.5 %collective-permute-start.22 = (s16[1040,128]{1,0:T(8,128)(2,1)S(1)}, s16[1040,128]{1,0:T(8,128)(2,1)S(1)}, u32[]{:S(2)}, u32[]{:S(2)}) collective-permute-start(s16[1040,128]{1,0:T(8,128)(2,1)S(1)} %get-tuple-element.107), channel_id=1, source_target_pairs={{0,2},{1,3},{2,0},{3,1},{4,6},{5,7},{6,4},{7,5},{8,10},{9,11},{10,... | collective-permute-start | bytes 798728 | tf_op jit(solution)/shard_map/ppermute | solution.py:335
  111.8 2.0 %collective-permute-start.23 = (f32[2,8,64,128]{3,2,1,0:T(8,128)S(1)}, f32[2,8,64,128]{3,2,1,0:T(8,128)S(1)}, u32[]{:S(2)}, u32[]{:S(2)}) collective-permute-start(f32[2,8,64,128]{3,2,1,0:T(8,128)S(1)} %get-tuple-element.109), channel_id=1, source_target_pairs={{0,1},{1,0},{2,3},{3,2},{4,5},{5,4},{6,7},{7,6},{8,9},{9,8},{10,11... | collective-permute-start | bytes 1572872 | tf_op jit(solution)/shard_map/ppermute | solution.py:335
  (7 other events, 98.0 us)

commit v3 on v2

--- a/solution.py
+++ b/solution.py
@@ -169,11 +169,17 @@
         voltage_ref[b] = chip_rows(meta[0], held[2, b], held[3, b])
 
 
-def stage_kernel(first, second, first_ref, second_ref, sems):
-    copies = [
-        pltpu.make_async_copy(first, first_ref, sems.at[0]),
-        pltpu.make_async_copy(second, second_ref, sems.at[1]),
-    ]
+def stage_kernel(member, induct, translation, induct_ref, rows_ref, sems):
+    blocks = member.shape[0]
+    rank = rows_ref.shape[0] // blocks
+    copies = [pltpu.make_async_copy(induct, induct_ref, sems.at[blocks])]
+    for b in range(blocks):
+        rows = pl.ds(pl.multiple_of(member[b] * rank, rank), rank)
+        copies.append(
+            pltpu.make_async_copy(
+                translation.at[rows, :], rows_ref.at[b * rank : (b + 1) * rank, :], sems.at[b]
+            )
+        )
     for copy in copies:
         copy.start()
     for copy in copies:
@@ -195,27 +201,6 @@
     for g in range(clusters):
         wide_ref[g] = wide[g] + decode(got[g * ranks : (g + 1) * ranks, :], power)
     send_totals(wide_ref, message)
-
-
-def translate_kernel(meta, member, wide, got, translation, chosen_ref, totals, rows):
-    clusters, ranks, scen = wide.shape
-    row = meta[1]
-    power, _ = get_powers(got.at[clusters * ranks :, :])
-    for g in range(clusters):
-        high, low = split(wide[g] + decode(got[g * ranks : (g + 1) * ranks, :], power))
-        both = jnp.concatenate([high, low], axis=1)
-        none = jnp.zeros(both.shape, BF)
-        totals[2 * g * ranks : (2 * g + 1) * ranks, :] = pick(row, none, both)
-        totals[(2 * g + 1) * ranks : (2 * g + 2) * ranks, :] = pick(row, both, none)
-    blocks, rank = chosen_ref.shape[:2]
-    for b in range(blocks):
-        rows[b * rank : (b + 1) * rank, :] = translation[
-            pl.ds(pl.multiple_of(member[b] * rank, rank), rank), :
-        ]
-    both = jnp.dot(rows[...], totals[...], preferred_element_type=F32)
-    for b in range(blocks):
-        block = both[b * rank : (b + 1) * rank]
-        chosen_ref[b] = block[:, :scen] + block[:, scen:]
 
 
 def near_kernel(meta, places, induct, induct_other, own, pair, past, part_ref, around, stacked):
@@ -240,19 +225,29 @@
         part_ref[t] = (parts[0] + parts[1]).T
 
 
-def finish_kernel(step, last, meta, part, chosen, target, *refs):
+def finish_kernel(step, last, meta, wide, got, translation, part, target, *refs):
     blocks, cells, scen = part.shape
     row = meta[1]
     if last:
-        message, keep_ref, ready = refs
+        message, keep_ref, totals, ready = refs
     else:
         current, voltage, cells_ref, damp, symbols, basis = refs[:6]
-        message, keep_ref, coef_ref, ready, ready_coefs, change = refs[6:]
-    rows = cells // 2
+        message, keep_ref, coef_ref, totals, ready, ready_coefs, change = refs[6:]
+    clusters, ranks, _ = wide.shape
+    power, _ = get_powers(got.at[clusters * ranks :, :])
+    for g in range(clusters):
+        high, low = split(wide[g] + decode(got[g * ranks : (g + 1) * ranks, :], power))
+        both = jnp.concatenate([high, low], axis=1)
+        none = jnp.zeros(both.shape, BF)
+        totals[2 * g * ranks : (2 * g + 1) * ranks, :] = pick(row, none, both)
+        totals[(2 * g + 1) * ranks : (2 * g + 2) * ranks, :] = pick(row, both, none)
+    both = jnp.dot(translation[...], totals[...], preferred_element_type=F32)
+    chosen = both[:, :scen] + both[:, scen:]
+    rows, rank = cells // 2, 2 * ranks
     bound = jnp.zeros((8, scen), F32)
     second = jnp.zeros((8, scen), F32)
     for b in range(blocks):
-        high, low = split(chosen[b])
+        high, low = split(chosen[b * rank : (b + 1) * rank])
         total = part[b] + lax.dot_general(
             jnp.concatenate([target[b], target[b]], axis=0),
             jnp.concatenate([high, low], axis=0),
@@ -279,18 +274,17 @@
                 jnp.concatenate([high, low], axis=0),
                 preferred_element_type=F32,
             )
-            rank = coefs.shape[0] // 2
-            coef_ref[b] = pick(row, coefs[rank:], coefs[:rank])
-            sent = pick(row, coefs[:rank], coefs[rank:])
+            coef_ref[b] = pick(row, coefs[ranks:], coefs[:ranks])
+            sent = pick(row, coefs[:ranks], coefs[ranks:])
             ready_coefs[b] = sent
             second = jnp.maximum(second, top(sent))
     power, second = exponent(bound), exponent(second)
     for b in range(blocks):
         message[b * rows : (b + 1) * rows, :] = encode(ready[b], power)
     if not last:
-        start, rank = blocks * rows, ready_coefs.shape[1]
+        start = blocks * rows
         for b in range(blocks):
-            message[start + b * rank : start + (b + 1) * rank, :] = encode(ready_coefs[b], second)
+            message[start + b * ranks : start + (b + 1) * ranks, :] = encode(ready_coefs[b], second)
     put_powers(message.at[message.shape[0] - TILE :, :], power, second)
 
 
@@ -366,7 +360,7 @@
     group, col = lax.axis_index("cells"), lax.axis_index("cols")
     core = col & 1
     meta = jnp.stack([core, col >> 1, col]).astype(jnp.int32)
-    member = membership[:, 0]
+    member = jnp.minimum(membership[:, 0], CLUSTERS - 1)
     owner = neighbours // blocks
     slot = jnp.where(owner == group, 0, jnp.where(owner == (group ^ 1), 1, 2))
     live = jnp.arange(entries, dtype=jnp.int32)[None, :] < live_counts[:, None]
@@ -379,6 +373,7 @@
     wide_f32 = shaped((CLUSTERS, hrank, half), F32)
     wide_msg = shaped((CLUSTERS * hrank + TILE, half), I16)
     coef_f32 = shaped((blocks, hrank, half), F32)
+    totals = pltpu.VMEM((CLUSTERS * rank, scen), BF)
 
     first, columns, damp, source_basis, target_basis = local_call(
         first_kernel,
@@ -421,22 +416,21 @@
     )
     for step in range(STEPS):
         last = step == STEPS - 1
+        if step == 0:
+            got = swap(send, "cols", 2)
         pair = swap(excite, "cells", 1)
         if step == 0:
-            got = swap(send, "cols", 2)
             later, _ = lax.optimization_barrier(((current, voltage, induct), send))
             current_other, voltage_other, induct_other = (swap(a, "cols", 1) for a in later)
             wide, send = local_call(cluster_kernel, (member, kept, got), (wide_f32, wide_msg), scalars=1)
         distance = 2
         while distance < groups:
             got = swap(send, "cells", distance)
-            if step == 0 and distance == 2:
-                got, pair = lax.optimization_barrier((got, pair))
             wide, send = local_call(
                 add_kernel,
                 (wide, got),
                 (wide_f32, wide_msg),
-                after=(current,) if step == 0 and distance == 4 else (),
+                after={4: (current,)}.get(distance, ()) if step == 0 else (),
             )
             if distance == 2:
                 pair, _ = lax.optimization_barrier((pair, send))
@@ -452,26 +446,17 @@
                 left=(1, 2, 3, 4),
                 after=(send,),
             )
-        got = swap(send, "cells", 1)
+        far_got = swap(send, "cells", 1)
         if step == 0:
             induct_other, translation = local_call(
                 stage_kernel,
-                (induct_other, translation),
-                (shaped(induct.shape, BF), shaped(translation.shape, BF)),
-                scratch=(pltpu.SemaphoreType.DMA((2,)),),
-                left=(0, 1),
+                (member, induct_other, translation),
+                (shaped(induct.shape, BF), shaped((blocks * rank, translation.shape[1]), BF)),
+                scratch=(pltpu.SemaphoreType.DMA((blocks + 1,)),),
+                scalars=1,
+                left=(1, 2),
                 after=(send,),
             )
-        (chosen,) = local_call(
-            translate_kernel,
-            (meta, member, wide, got, translation),
-            (shaped((blocks, rank, half), F32),),
-            scratch=(
-                pltpu.VMEM((CLUSTERS * rank, scen), BF),
-                pltpu.VMEM((blocks * rank, CLUSTERS * rank), BF),
-            ),
-            scalars=2,
-        )
         past = pass_on(pair, "cells")
         (part,) = local_call(
             near_kernel,
@@ -483,12 +468,13 @@
             ),
             scalars=2,
         )
+        far_got, part = lax.optimization_barrier((far_got, part))
         if last:
             send, kept = local_call(
                 functools.partial(finish_kernel, step, last),
-                (meta, part, chosen, target_basis),
+                (meta, wide, far_got, translation, part, target_basis),
                 (shaped((blocks * rows + TILE, half), I16), state_f32),
-                scratch=(pltpu.VMEM((blocks, rows, half), F32),),
+                scratch=(totals, pltpu.VMEM((blocks, rows, half), F32)),
                 scalars=1,
             )
             got = swap(send, "cols", 2)
@@ -501,9 +487,23 @@
         else:
             send, kept, coefs = local_call(
                 functools.partial(finish_kernel, step, last),
-                (meta, part, chosen, target_basis, current, voltage, columns, damp, symbols_half, source_basis),
+                (
+                    meta,
+                    wide,
+                    far_got,
+                    translation,
+                    part,
+                    target_basis,
+                    current,
+                    voltage,
+                    columns,
+                    damp,
+                    symbols_half,
+                    source_basis,
+                ),
                 (shaped((blocks * (rows + hrank) + TILE, half), I16), state_f32, coef_f32),
                 scratch=(
+                    totals,
                     pltpu.VMEM((blocks, rows, half), F32),
                     pltpu.VMEM((blocks, hrank, half), F32),
                     pltpu.VMEM((blocks, cells, half), F32),

time: 116 us -> 109 us (0.940)
  waiting for transfers between devices: 50.7 us -> 39.5 us
  starting transfers between devices: 32.2 us -> 37.8 us
  Pallas kernels: 29.9 us -> 28.5 us
    ppermute x21, waiting for transfers between devices: 50.7 us -> 38.3 us  [swap(): return lax.ppermute(array, axis, [(i, i ^ distance) for i in range(count)])]
    ppermute x21, starting transfers between devices: 21.2 us -> 28.1 us  [swap(): return lax.ppermute(array, axis, [(i, i ^ distance) for i in range(count)])]
    pallas_call x24 -> x21, Pallas kernels: 29.9 us -> 28.5 us  [local_call(): pl.pallas_call(run, out_shape=tuple(outs), in_specs=specs, out_specs=tupl...]
    ppermute x3, starting transfers between devices: 11.1 us -> 9.75 us  [pass_on(): return lax.ppermute(array, axis, up + down)]
    ppermute x3, waiting for transfers between devices: 0.01 us -> 1.24 us  [pass_on(): return lax.ppermute(array, axis, up + down)]
  transfers between devices with their start and end apart: 24 -> 24, of which waited for: 15 -> 14; matrix products, arithmetic and copies ran while one was open for 0% -> 1% of each run, Pallas kernels for 8% -> 14%
where the time goes in v3:
time: 109 us
  waiting for transfers between devices  39.5 us (36%)
  starting transfers between devices  37.8 us (35%)
  Pallas kernels  28.5 us (26%)
  local copies, waits for them, and re-layouts  1.21 us (1%)
    ppermute x21, waiting for transfers between devices, swap(): return lax.ppermute(array, axis, [(i, i ^ distance) for i in range(count)])  38.3 us
    pallas_call x21, Pallas kernels, local_call(): pl.pallas_call(run, out_shape=tuple(outs), in_specs=specs, out_specs=tupl...  28.5 us
    ppermute x21, starting transfers between devices, swap(): return lax.ppermute(array, axis, [(i, i ^ distance) for i in range(count)])  28.1 us
    ppermute x3, starting transfers between devices, pass_on(): return lax.ppermute(array, axis, up + down)  9.75 us
  transfers between devices with their start and end apart: 24, of which 14 were waited for; matrix products, arithmetic and copies ran while one was open for 1% of the time, Pallas kernels for 14%

profile of v3, /device:TPU:0, one launch (start us, length us, event | category | flops | bytes accessed | tf_op | source)
XLA Modules:
  0.0 108.8 jit_solution(15161473038101860864)
XLA Ops:
  0.7 2.1 %first_kernel.1 = (bf16[8,64,256]{2,1,0:T(8,128)(2,1)S(1)}, f32[3,128,8]{2,1,0:T(8,128)S(1)}, f32[256,8]{1,0:T(8,128)S(1)}, bf16[8,64,256]{2,1,0:T(8,128)(2,1)S(1)}, bf16[8,64,256]{2,1,0:T(8,128)(2,1)S(1)}) custom-call(s32[3]{0:T(128)S(1)} %pad_add_fusion.refs_0_, f32[8,64,256]{2,1,0:T(8,128)} %refs_1_.3, f32[8,64,256]{2,1,0:T(8,128)} %refs_3_.3, ...), custom_call_target="tpu_custom_call" | custom-call | bytes 2416652 | tf_op jit(solution)/shard_map/first_kernel/pallas_call | solution.py:33
  6.3 2.7 %collective-permute-start.3 = (s16[272,128]{1,0:T(8,128)(2,1)S(1)}, s16[272,128]{1,0:T(8,128)(2,1)S(1)}, u32[]{:S(2)}, u32[]{:S(2)}) collective-permute-start(s16[272,128]{1,0:T(8,128)(2,1)S(1)} %get-tuple-element.62), channel_id=1, source_target_pairs={{0,2},{1,3},{2,0},{3,1},{4,6},{5,7},{6,4},{7,5},{8,10},{9,11},{10,... | collective-permute-start | bytes 208904 | tf_op jit(solution)/shard_map/ppermute | solution.py:329
  9.6 2.0 %collective-permute-done.3.refs_2_ = s16[272,128]{1,0:T(8,128)(2,1)S(1)} collective-permute-done((s16[272,128]{1,0:T(8,128)(2,1)S(1)}, s16[272,128]{1,0:T(8,128)(2,1)S(1)}, u32[]{:S(2)}, u32[]{:S(2)}) %collective-permute-start.3) | collective-permute-done | bytes 69664 | tf_op jit(solution)/shard_map/ppermute | solution.py:329
  15.7 2.0 %collective-permute-done.4.refs_1_ = s16[528,128]{1,0:T(8,128)(2,1)S(1)} collective-permute-done((s16[528,128]{1,0:T(8,128)(2,1)S(1)}, s16[528,128]{1,0:T(8,128)(2,1)S(1)}, u32[]{:S(2)}, u32[]{:S(2)}) %collective-permute-start.4) | collective-permute-done | bytes 135200 | tf_op jit(solution)/shard_map/ppermute | solution.py:329
  17.8 2.6 %collective-permute-start.5 = (s16[528,128]{1,0:T(8,128)(2,1)S(1)}, s16[528,128]{1,0:T(8,128)(2,1)S(1)}, u32[]{:S(2)}, u32[]{:S(2)}) collective-permute-start(s16[528,128]{1,0:T(8,128)(2,1)S(1)} %get-tuple-element.68.refs_5_), channel_id=1, source_target_pairs={{0,16},{4,20},{8,24},{12,28},{16,0},{20,4},{24,8},{28,12},{1,17},{... | collective-permute-start | bytes 405512 | tf_op jit(solution)/shard_map/ppermute | solution.py:329
  21.7 2.4 %collective-permute-start.9 = (bf16[8,128,128]{2,1,0:T(8,128)(2,1)S(1)}, bf16[8,128,128]{2,1,0:T(8,128)(2,1)S(1)}, u32[]{:S(2)}, u32[]{:S(2)}) collective-permute-start(bf16[8,128,128]{2,1,0:T(8,128)(2,1)S(1)} %collective-permute-done.8.refs_5_), channel_id=1, source_target_pairs={{0,8},{8,16},{16,24},{12,4},{20,12},{28,20},{1,9},{9,17},{17,25},{... | collective-permute-start | bytes 786440 | tf_op jit(solution)/shard_map/ppermute | solution.py:336
  24.9 2.2 %layout_kernel.1 = (f32[8,128,128]{2,1,0:T(8,128)S(1)}, f32[8,128,128]{2,1,0:T(8,128)S(1)}) custom-call(s32[3]{0:T(128)S(1)} %pad_add_fusion.refs_0_, f32[8,64,256]{2,1,0:T(8,128)} %refs_1_.3, f32[8,64,256]{2,1,0:T(8,128)} %copy-done.1, f32[8,64,256]{2,1,0:T(8,128)} %refs_3_.3, f32[8,64,256]{2,1,0:T(8,128)} %collective-permute-done.2.refs_4_, ...), custom_call_target="tpu_custom_call" | custom-call | bytes 3145740 | tf_op jit(solution)/shard_map/layout_kernel/pallas_call | solution.py:33
  27.7 3.3 %stage_kernel.1 = (bf16[8,1024,256]{2,1,0:T(8,128)(2,1)S(1)}, bf16[512,1024]{1,0:T(8,128)(2,1)S(1)}) custom-call(s32[8]{0:T(128)S(1)} %minimum_bitcast_fusion.refs_0_, bf16[8,1024,256]{2,1,0:T(8,128)(2,1)} %collective-permute-done.7.refs_1_, bf16[1024,1024]{1,0:T(8,128)(2,1)} %refs_2_.3, s16[528,128]{1,0:T(8,128)(2,1)S(1)} %get-tuple-element.73.refs_3_), custom_call_target="tpu_custom_call" | custom-call | bytes 11534368 | tf_op jit(solution)/shard_map/stage_kernel/pallas_call | solution.py:33
  31.5 2.9 %near_kernel.3.refs_4_ = f32[8,256,128]{2,1,0:T(8,128)S(1)} custom-call(s32[3]{0:T(128)S(1)} %pad_add_fusion.refs_0_, s32[8,16]{1,0:T(8,128)S(1)} %fusion.1.refs_1_, bf16[8,1024,256]{2,1,0:T(8,128)(2,1)S(1)} %bitcast.7, bf16[8,1024,256]{2,1,0:T(8,128)(2,1)S(1)} %get-tuple-element.75.refs_3_, bf16[8,128,128]{2,1,0:T(8,128)(2,1)S(1)} %get-tuple-element.76.refs_4_, ...), custom_call_target="tpu_custom_call" | custom-call | bytes 10224140 | tf_op jit(solution)/shard_map/near_kernel/pallas_call | solution.py:33
  34.4 2.1 %finish_kernel.3 = (s16[1296,128]{1,0:T(8,128)(2,1)S(1)}, f32[8,128,128]{2,1,0:T(8,128)S(1)}, f32[8,32,128]{2,1,0:T(8,128)S(1)}) custom-call(s32[3]{0:T(128)S(1)} %pad_add_fusion.refs_0_, f32[16,32,128]{2,1,0:T(8,128)S(1)} %get-tuple-element.72.refs_1_, s16[528,128]{1,0:T(8,128)(2,1)S(1)} %collective-permute-done.6.refs_2_, ...), custom_call_target="tpu_custom_call" | custom-call | bytes 5081100 | tf_op jit(solution)/shard_map/finish_kernel/pallas_call | solution.py:33
  38.1 6.3 %collective-permute-done.10.refs_4_ = s16[1296,128]{1,0:T(8,128)(2,1)S(1)} collective-permute-done((s16[1296,128]{1,0:T(8,128)(2,1)S(1)}, s16[1296,128]{1,0:T(8,128)(2,1)S(1)}, u32[]{:S(2)}, u32[]{:S(2)}) %collective-permute-start.10) | collective-permute-done | bytes 331808 | tf_op jit(solution)/shard_map/ppermute | solution.py:329
  47.1 2.3 %collective-permute-start.11 = (s16[528,128]{1,0:T(8,128)(2,1)S(1)}, s16[528,128]{1,0:T(8,128)(2,1)S(1)}, u32[]{:S(2)}, u32[]{:S(2)}) collective-permute-start(s16[528,128]{1,0:T(8,128)(2,1)S(1)} %get-tuple-element.90), channel_id=1, source_target_pairs={{0,8},{4,12},{8,0},{12,4},{16,24},{20,28},{24,16},{28,20},{1,9},{5... | collective-permute-start | bytes 405512 | tf_op jit(solution)/shard_map/ppermute | solution.py:329
  49.5 4.4 %collective-permute-done.11.refs_1_ = s16[528,128]{1,0:T(8,128)(2,1)S(1)} collective-permute-done((s16[528,128]{1,0:T(8,128)(2,1)S(1)}, s16[528,128]{1,0:T(8,128)(2,1)S(1)}, u32[]{:S(2)}, u32[]{:S(2)}) %collective-permute-start.11) | collective-permute-done | bytes 135200 | tf_op jit(solution)/shard_map/ppermute | solution.py:329
  55.4 2.8 %collective-permute-start.15 = (bf16[8,128,128]{2,1,0:T(8,128)(2,1)S(1)}, bf16[8,128,128]{2,1,0:T(8,128)(2,1)S(1)}, u32[]{:S(2)}, u32[]{:S(2)}) collective-permute-start(bf16[8,128,128]{2,1,0:T(8,128)(2,1)S(1)} %collective-permute-done.14.refs_5_), channel_id=1, source_target_pairs={{0,8},{8,16},{16,24},{12,4},{20,12},{28,20},{1,9},{9,17},{17,25},{... | collective-permute-start | bytes 786440 | tf_op jit(solution)/shard_map/ppermute | solution.py:336
  58.2 3.2 %collective-permute-done.12.refs_1_ = s16[528,128]{1,0:T(8,128)(2,1)S(1)} collective-permute-done((s16[528,128]{1,0:T(8,128)(2,1)S(1)}, s16[528,128]{1,0:T(8,128)(2,1)S(1)}, u32[]{:S(2)}, u32[]{:S(2)}) %collective-permute-start.12) | collective-permute-done | bytes 135200 | tf_op jit(solution)/shard_map/ppermute | solution.py:329
  62.5 2.9 %near_kernel.4.refs_4_ = f32[8,256,128]{2,1,0:T(8,128)S(1)} custom-call(s32[3]{0:T(128)S(1)} %pad_add_fusion.refs_0_, s32[8,16]{1,0:T(8,128)S(1)} %fusion.1.refs_1_, bf16[8,1024,256]{2,1,0:T(8,128)(2,1)S(1)} %bitcast.8, bf16[8,1024,256]{2,1,0:T(8,128)(2,1)S(1)} %get-tuple-element.75.refs_3_, bf16[8,128,128]{2,1,0:T(8,128)(2,1)S(1)} %get-tuple-element.95.refs_4_, ...), custom_call_target="tpu_custom_call" | custom-call | bytes 10224140 | tf_op jit(solution)/shard_map/near_kernel/pallas_call | solution.py:33
  66.6 2.1 %finish_kernel.4 = (s16[1296,128]{1,0:T(8,128)(2,1)S(1)}, f32[8,128,128]{2,1,0:T(8,128)S(1)}, f32[8,32,128]{2,1,0:T(8,128)S(1)}) custom-call(s32[3]{0:T(128)S(1)} %pad_add_fusion.refs_0_, f32[16,32,128]{2,1,0:T(8,128)S(1)} %get-tuple-element.93.refs_1_, s16[528,128]{1,0:T(8,128)(2,1)S(1)} %collective-permute-done.13.refs_2_, ...), custom_call_target="tpu_custom_call" | custom-call | bytes 5081100 | tf_op jit(solution)/shard_map/finish_kernel/pallas_call | solution.py:33
  70.3 5.6 %collective-permute-done.16.refs_4_ = s16[1296,128]{1,0:T(8,128)(2,1)S(1)} collective-permute-done((s16[1296,128]{1,0:T(8,128)(2,1)S(1)}, s16[1296,128]{1,0:T(8,128)(2,1)S(1)}, u32[]{:S(2)}, u32[]{:S(2)}) %collective-permute-start.16) | collective-permute-done | bytes 331808 | tf_op jit(solution)/shard_map/ppermute | solution.py:329
  77.0 2.0 %collective-permute-start.20 = (bf16[8,128,128]{2,1,0:T(8,128)(2,1)S(1)}, bf16[8,128,128]{2,1,0:T(8,128)(2,1)S(1)}, u32[]{:S(2)}, u32[]{:S(2)}) collective-permute-start(bf16[8,128,128]{2,1,0:T(8,128)(2,1)S(1)} %get-tuple-element.110.refs_4_), channel_id=1, source_target_pairs={{0,4},{4,0},{8,12},{12,8},{16,20},{20,16},{24,28},{28,24},{1,5},{5... | collective-permute-start | bytes 786440 | tf_op jit(solution)/shard_map/ppermute | solution.py:329
  80.0 4.1 %collective-permute-done.17.refs_1_ = s16[528,128]{1,0:T(8,128)(2,1)S(1)} collective-permute-done((s16[528,128]{1,0:T(8,128)(2,1)S(1)}, s16[528,128]{1,0:T(8,128)(2,1)S(1)}, u32[]{:S(2)}, u32[]{:S(2)}) %collective-permute-start.17) | collective-permute-done | bytes 135200 | tf_op jit(solution)/shard_map/ppermute | solution.py:329
  85.3 4.6 %collective-permute-start.21 = (bf16[8,128,128]{2,1,0:T(8,128)(2,1)S(1)}, bf16[8,128,128]{2,1,0:T(8,128)(2,1)S(1)}, u32[]{:S(2)}, u32[]{:S(2)}) collective-permute-start(bf16[8,128,128]{2,1,0:T(8,128)(2,1)S(1)} %collective-permute-done.20.refs_5_), channel_id=1, source_target_pairs={{0,8},{8,16},{16,24},{12,4},{20,12},{28,20},{1,9},{9,17},{17,25},{... | collective-permute-start | bytes 786440 | tf_op jit(solution)/shard_map/ppermute | solution.py:336
  90.2 2.1 %collective-permute-start.19 = (s16[528,128]{1,0:T(8,128)(2,1)S(1)}, s16[528,128]{1,0:T(8,128)(2,1)S(1)}, u32[]{:S(2)}, u32[]{:S(2)}) collective-permute-start(s16[528,128]{1,0:T(8,128)(2,1)S(1)} %get-tuple-element.109), channel_id=1, source_target_pairs={{0,4},{4,0},{8,12},{12,8},{16,20},{20,16},{24,28},{28,24},{1,5},{5... | collective-permute-start | bytes 405512 | tf_op jit(solution)/shard_map/ppermute | solution.py:329
  93.5 2.9 %near_kernel.5.refs_4_ = f32[8,256,128]{2,1,0:T(8,128)S(1)} custom-call(s32[3]{0:T(128)S(1)} %pad_add_fusion.refs_0_, s32[8,16]{1,0:T(8,128)S(1)} %fusion.1.refs_1_, bf16[8,1024,256]{2,1,0:T(8,128)(2,1)S(1)} %bitcast.9, bf16[8,1024,256]{2,1,0:T(8,128)(2,1)S(1)} %get-tuple-element.75.refs_3_, bf16[8,128,128]{2,1,0:T(8,128)(2,1)S(1)} %get-tuple-element.110.refs_4_, ...), custom_call_target="tpu_custom_call" | custom-call | bytes 10224140 | tf_op jit(solution)/shard_map/near_kernel/pallas_call | solution.py:33
  99.5 4.9 %collective-permute-done.22.refs_4_ = s16[1040,128]{1,0:T(8,128)(2,1)S(1)} collective-permute-done((s16[1040,128]{1,0:T(8,128)(2,1)S(1)}, s16[1040,128]{1,0:T(8,128)(2,1)S(1)}, u32[]{:S(2)}, u32[]{:S(2)}) %collective-permute-start.22) | collective-permute-done | bytes 266272 | tf_op jit(solution)/shard_map/ppermute | solution.py:329
  (59 shorter events, 33.2 us)
Async XLA Ops:
  2.9 1.7 %collective-permute-start = (bf16[8,64,256]{2,1,0:T(8,128)(2,1)S(1)}, bf16[8,64,256]{2,1,0:T(8,128)(2,1)S(1)}, u32[]{:S(2)}, u32[]{:S(2)}) collective-permute-start(bf16[8,64,256]{2,1,0:T(8,128)(2,1)S(1)} %get-tuple-element.60.refs_1_), channel_id=1, source_target_pairs={{0,1},{1,0},{2,3},{3,2},{4,5},{5,4},{6,7},{7,6},{8,9},{9,8},{10,11... | collective-permute-start | bytes 786440 | tf_op jit(solution)/shard_map/ppermute | solution.py:329
  5.3 22.4 %collective-permute-start.7 = (bf16[8,1024,256]{2,1,0:T(8,128)(2,1)}, bf16[8,1024,256]{2,1,0:T(8,128)(2,1)}, u32[]{:S(2)}, u32[]{:S(2)}) collective-permute-start(bf16[8,1024,256]{2,1,0:T(8,128)(2,1)} %bitcast.6), channel_id=1, source_target_pairs={{0,1},{1,0},{2,3},{3,2},{4,5},{5,4},{6,7},{7,6},{8,9},{9,8},{10,11... | collective-permute-start | bytes 12582920 | tf_op jit(solution)/shard_map/ppermute | solution.py:329
  5.8 18.3 %collective-permute-start.1 = (f32[8,64,256]{2,1,0:T(8,128)}, f32[8,64,256]{2,1,0:T(8,128)S(1)}, u32[]{:S(2)}, u32[]{:S(2)}) collective-permute-start(f32[8,64,256]{2,1,0:T(8,128)} %refs_1_.3), channel_id=1, source_target_pairs={{0,1},{1,0},{2,3},{3,2},{4,5},{5,4},{6,7},{7,6},{8,9},{9,8},{10,11... | collective-permute-start | bytes 1572872 | tf_op jit(solution)/shard_map/ppermute | solution.py:329
  5.9 18.9 %collective-permute-start.2 = (f32[8,64,256]{2,1,0:T(8,128)}, f32[8,64,256]{2,1,0:T(8,128)}, u32[]{:S(2)}, u32[]{:S(2)}) collective-permute-start(f32[8,64,256]{2,1,0:T(8,128)} %refs_3_.3), channel_id=1, source_target_pairs={{0,1},{1,0},{2,3},{3,2},{4,5},{5,4},{6,7},{7,6},{8,9},{9,8},{10,11... | collective-permute-start | bytes 1572872 | tf_op jit(solution)/shard_map/ppermute | solution.py:329
  6.3 5.4 %collective-permute-start.3 = (s16[272,128]{1,0:T(8,128)(2,1)S(1)}, s16[272,128]{1,0:T(8,128)(2,1)S(1)}, u32[]{:S(2)}, u32[]{:S(2)}) collective-permute-start(s16[272,128]{1,0:T(8,128)(2,1)S(1)} %get-tuple-element.62), channel_id=1, source_target_pairs={{0,2},{1,3},{2,0},{3,1},{4,6},{5,7},{6,4},{7,5},{8,10},{9,11},{10,... | collective-permute-start | bytes 208904 | tf_op jit(solution)/shard_map/ppermute | solution.py:329
  12.3 5.4 %collective-permute-start.4 = (s16[528,128]{1,0:T(8,128)(2,1)S(1)}, s16[528,128]{1,0:T(8,128)(2,1)S(1)}, u32[]{:S(2)}, u32[]{:S(2)}) collective-permute-start(s16[528,128]{1,0:T(8,128)(2,1)S(1)} %get-tuple-element.67), channel_id=1, source_target_pairs={{0,8},{4,12},{8,0},{12,4},{16,24},{20,28},{24,16},{28,20},{1,9},{5... | collective-permute-start | bytes 405512 | tf_op jit(solution)/shard_map/ppermute | solution.py:329
  14.2 7.5 %collective-permute-start.8 = (bf16[8,128,128]{2,1,0:T(8,128)(2,1)S(1)}, bf16[8,128,128]{2,1,0:T(8,128)(2,1)S(1)}, u32[]{:S(2)}, u32[]{:S(2)}) collective-permute-start(bf16[8,128,128]{2,1,0:T(8,128)(2,1)S(1)} %get-tuple-element.76.refs_4_), channel_id=1, source_target_pairs={{0,4},{4,0},{8,12},{12,8},{16,20},{20,16},{24,28},{28,24},{1,5},{5... | collective-permute-start | bytes 786440 | tf_op jit(solution)/shard_map/ppermute | solution.py:329
  17.8 9.3 %collective-permute-start.5 = (s16[528,128]{1,0:T(8,128)(2,1)S(1)}, s16[528,128]{1,0:T(8,128)(2,1)S(1)}, u32[]{:S(2)}, u32[]{:S(2)}) collective-permute-start(s16[528,128]{1,0:T(8,128)(2,1)S(1)} %get-tuple-element.68.refs_5_), channel_id=1, source_target_pairs={{0,16},{4,20},{8,24},{12,28},{16,0},{20,4},{24,8},{28,12},{1,17},{... | collective-permute-start | bytes 405512 | tf_op jit(solution)/shard_map/ppermute | solution.py:329
  21.7 9.4 %collective-permute-start.9 = (bf16[8,128,128]{2,1,0:T(8,128)(2,1)S(1)}, bf16[8,128,128]{2,1,0:T(8,128)(2,1)S(1)}, u32[]{:S(2)}, u32[]{:S(2)}) collective-permute-start(bf16[8,128,128]{2,1,0:T(8,128)(2,1)S(1)} %collective-permute-done.8.refs_5_), channel_id=1, source_target_pairs={{0,8},{8,16},{16,24},{12,4},{20,12},{28,20},{1,9},{9,17},{17,25},{... | collective-permute-start | bytes 786440 | tf_op jit(solution)/shard_map/ppermute | solution.py:336
  27.2 7.2 %collective-permute-start.6 = (s16[528,128]{1,0:T(8,128)(2,1)S(1)}, s16[528,128]{1,0:T(8,128)(2,1)S(1)}, u32[]{:S(2)}, u32[]{:S(2)}) collective-permute-start(s16[528,128]{1,0:T(8,128)(2,1)S(1)} %get-tuple-element.73.refs_3_), channel_id=1, source_target_pairs={{0,4},{4,0},{8,12},{12,8},{16,20},{20,16},{24,28},{28,24},{1,5},{5... | collective-permute-start | bytes 405512 | tf_op jit(solution)/shard_map/ppermute | solution.py:329
  36.5 7.8 %collective-permute-start.10 = (s16[1296,128]{1,0:T(8,128)(2,1)S(1)}, s16[1296,128]{1,0:T(8,128)(2,1)S(1)}, u32[]{:S(2)}, u32[]{:S(2)}) collective-permute-start(s16[1296,128]{1,0:T(8,128)(2,1)S(1)} %get-tuple-element.85), channel_id=1, source_target_pairs={{0,2},{1,3},{2,0},{3,1},{4,6},{5,7},{6,4},{7,5},{8,10},{9,11},{10,... | collective-permute-start | bytes 995336 | tf_op jit(solution)/shard_map/ppermute | solution.py:329
  45.4 10.0 %collective-permute-start.14 = (bf16[8,128,128]{2,1,0:T(8,128)(2,1)S(1)}, bf16[8,128,128]{2,1,0:T(8,128)(2,1)S(1)}, u32[]{:S(2)}, u32[]{:S(2)}) collective-permute-start(bf16[8,128,128]{2,1,0:T(8,128)(2,1)S(1)} %get-tuple-element.95.refs_4_), channel_id=1, source_target_pairs={{0,4},{4,0},{8,12},{12,8},{16,20},{20,16},{24,28},{28,24},{1,5},{5... | collective-permute-start | bytes 786440 | tf_op jit(solution)/shard_map/ppermute | solution.py:329
  47.1 6.8 %collective-permute-start.11 = (s16[528,128]{1,0:T(8,128)(2,1)S(1)}, s16[528,128]{1,0:T(8,128)(2,1)S(1)}, u32[]{:S(2)}, u32[]{:S(2)}) collective-permute-start(s16[528,128]{1,0:T(8,128)(2,1)S(1)} %get-tuple-element.90), channel_id=1, source_target_pairs={{0,8},{4,12},{8,0},{12,4},{16,24},{20,28},{24,16},{28,20},{1,9},{5... | collective-permute-start | bytes 405512 | tf_op jit(solution)/shard_map/ppermute | solution.py:329
  54.0 7.4 %collective-permute-start.12 = (s16[528,128]{1,0:T(8,128)(2,1)S(1)}, s16[528,128]{1,0:T(8,128)(2,1)S(1)}, u32[]{:S(2)}, u32[]{:S(2)}) collective-permute-start(s16[528,128]{1,0:T(8,128)(2,1)S(1)} %get-tuple-element.92), channel_id=1, source_target_pairs={{0,16},{4,20},{8,24},{12,28},{16,0},{20,4},{24,8},{28,12},{1,17},{... | collective-permute-start | bytes 405512 | tf_op jit(solution)/shard_map/ppermute | solution.py:329
  55.4 7.1 %collective-permute-start.15 = (bf16[8,128,128]{2,1,0:T(8,128)(2,1)S(1)}, bf16[8,128,128]{2,1,0:T(8,128)(2,1)S(1)}, u32[]{:S(2)}, u32[]{:S(2)}) collective-permute-start(bf16[8,128,128]{2,1,0:T(8,128)(2,1)S(1)} %collective-permute-done.14.refs_5_), channel_id=1, source_target_pairs={{0,8},{8,16},{16,24},{12,4},{20,12},{28,20},{1,9},{9,17},{17,25},{... | collective-permute-start | bytes 786440 | tf_op jit(solution)/shard_map/ppermute | solution.py:336
  61.5 5.1 %collective-permute-start.13 = (s16[528,128]{1,0:T(8,128)(2,1)S(1)}, s16[528,128]{1,0:T(8,128)(2,1)S(1)}, u32[]{:S(2)}, u32[]{:S(2)}) collective-permute-start(s16[528,128]{1,0:T(8,128)(2,1)S(1)} %get-tuple-element.94), channel_id=1, source_target_pairs={{0,4},{4,0},{8,12},{12,8},{16,20},{20,16},{24,28},{28,24},{1,5},{5... | collective-permute-start | bytes 405512 | tf_op jit(solution)/shard_map/ppermute | solution.py:329
  68.7 7.2 %collective-permute-start.16 = (s16[1296,128]{1,0:T(8,128)(2,1)S(1)}, s16[1296,128]{1,0:T(8,128)(2,1)S(1)}, u32[]{:S(2)}, u32[]{:S(2)}) collective-permute-start(s16[1296,128]{1,0:T(8,128)(2,1)S(1)} %get-tuple-element.100), channel_id=1, source_target_pairs={{0,2},{1,3},{2,0},{3,1},{4,6},{5,7},{6,4},{7,5},{8,10},{9,11},{10,... | collective-permute-start | bytes 995336 | tf_op jit(solution)/shard_map/ppermute | solution.py:329
  77.0 8.3 %collective-permute-start.20 = (bf16[8,128,128]{2,1,0:T(8,128)(2,1)S(1)}, bf16[8,128,128]{2,1,0:T(8,128)(2,1)S(1)}, u32[]{:S(2)}, u32[]{:S(2)}) collective-permute-start(bf16[8,128,128]{2,1,0:T(8,128)(2,1)S(1)} %get-tuple-element.110.refs_4_), channel_id=1, source_target_pairs={{0,4},{4,0},{8,12},{12,8},{16,20},{20,16},{24,28},{28,24},{1,5},{5... | collective-permute-start | bytes 786440 | tf_op jit(solution)/shard_map/ppermute | solution.py:329
  79.0 5.1 %collective-permute-start.17 = (s16[528,128]{1,0:T(8,128)(2,1)S(1)}, s16[528,128]{1,0:T(8,128)(2,1)S(1)}, u32[]{:S(2)}, u32[]{:S(2)}) collective-permute-start(s16[528,128]{1,0:T(8,128)(2,1)S(1)} %get-tuple-element.105), channel_id=1, source_target_pairs={{0,8},{4,12},{8,0},{12,4},{16,24},{20,28},{24,16},{28,20},{1,9},{5... | collective-permute-start | bytes 405512 | tf_op jit(solution)/shard_map/ppermute | solution.py:329
  84.1 6.0 %collective-permute-start.18 = (s16[528,128]{1,0:T(8,128)(2,1)S(1)}, s16[528,128]{1,0:T(8,128)(2,1)S(1)}, u32[]{:S(2)}, u32[]{:S(2)}) collective-permute-start(s16[528,128]{1,0:T(8,128)(2,1)S(1)} %get-tuple-element.107), channel_id=1, source_target_pairs={{0,16},{4,20},{8,24},{12,28},{16,0},{20,4},{24,8},{28,12},{1,17},{... | collective-permute-start | bytes 405512 | tf_op jit(solution)/shard_map/ppermute | solution.py:329
  85.3 8.3 %collective-permute-start.21 = (bf16[8,128,128]{2,1,0:T(8,128)(2,1)S(1)}, bf16[8,128,128]{2,1,0:T(8,128)(2,1)S(1)}, u32[]{:S(2)}, u32[]{:S(2)}) collective-permute-start(bf16[8,128,128]{2,1,0:T(8,128)(2,1)S(1)} %collective-permute-done.20.refs_5_), channel_id=1, source_target_pairs={{0,8},{8,16},{16,24},{12,4},{20,12},{28,20},{1,9},{9,17},{17,25},{... | collective-permute-start | bytes 786440 | tf_op jit(solution)/shard_map/ppermute | solution.py:336
  90.2 6.3 %collective-permute-start.19 = (s16[528,128]{1,0:T(8,128)(2,1)S(1)}, s16[528,128]{1,0:T(8,128)(2,1)S(1)}, u32[]{:S(2)}, u32[]{:S(2)}) collective-permute-start(s16[528,128]{1,0:T(8,128)(2,1)S(1)} %get-tuple-element.109), channel_id=1, source_target_pairs={{0,4},{4,0},{8,12},{12,8},{16,20},{20,16},{24,28},{28,24},{1,5},{5... | collective-permute-start | bytes 405512 | tf_op jit(solution)/shard_map/ppermute | solution.py:329
  98.0 6.5 %collective-permute-start.22 = (s16[1040,128]{1,0:T(8,128)(2,1)S(1)}, s16[1040,128]{1,0:T(8,128)(2,1)S(1)}, u32[]{:S(2)}, u32[]{:S(2)}) collective-permute-start(s16[1040,128]{1,0:T(8,128)(2,1)S(1)} %get-tuple-element.115), channel_id=1, source_target_pairs={{0,2},{1,3},{2,0},{3,1},{4,6},{5,7},{6,4},{7,5},{8,10},{9,11},{10,... | collective-permute-start | bytes 798728 | tf_op jit(solution)/shard_map/ppermute | solution.py:329
  105.2 2.0 %collective-permute-start.23 = (f32[2,8,64,128]{3,2,1,0:T(8,128)S(1)}, f32[2,8,64,128]{3,2,1,0:T(8,128)S(1)}, u32[]{:S(2)}, u32[]{:S(2)}) collective-permute-start(f32[2,8,64,128]{3,2,1,0:T(8,128)S(1)} %get-tuple-element.117), channel_id=1, source_target_pairs={{0,1},{1,0},{2,3},{3,2},{4,5},{5,4},{6,7},{7,6},{8,9},{9,8},{10,11... | collective-permute-start | bytes 1572872 | tf_op jit(solution)/shard_map/ppermute | solution.py:329
  (5 other events, 85.6 us)

commit v4 on v3

--- a/solution.py
+++ b/solution.py
@@ -268,12 +268,7 @@
             )
     if not last:
         for b in range(blocks):
-            high, low = split(change[b])
-            coefs = jnp.dot(
-                jnp.concatenate([basis[b], basis[b]], axis=1),
-                jnp.concatenate([high, low], axis=0),
-                preferred_element_type=F32,
-            )
+            coefs = jnp.dot(basis[b], change[b].astype(BF), preferred_element_type=F32)
             coef_ref[b] = pick(row, coefs[ranks:], coefs[:ranks])
             sent = pick(row, coefs[:ranks], coefs[ranks:])
             ready_coefs[b] = sent

time: 109 us -> 109 us (level)
  no operation moved by 1% of the time
where the time goes in v4:
time: 109 us; the launch traced here: 108 us
  waiting for transfers between devices  39.5 us (36%)
  starting transfers between devices  37.8 us (35%)
  Pallas kernels  28.1 us (26%)
  local copies, waits for them, and re-layouts  1.21 us (1%)
    ppermute x21, waiting for transfers between devices, swap(): return lax.ppermute(array, axis, [(i, i ^ distance) for i in range(count)])  38.3 us
    pallas_call x21, Pallas kernels, local_call(): pl.pallas_call(run, out_shape=tuple(outs), in_specs=specs, out_specs=tupl...  28.1 us
    ppermute x21, starting transfers between devices, swap(): return lax.ppermute(array, axis, [(i, i ^ distance) for i in range(count)])  28 us
    ppermute x3, starting transfers between devices, pass_on(): return lax.ppermute(array, axis, up + down)  9.81 us
  transfers between devices with their start and end apart: 24, of which 14 were waited for; matrix products, arithmetic and copies ran while one was open for 1% of the time, Pallas kernels for 14%

profile of v4, /device:TPU:0, one launch (start us, length us, event | category | flops | bytes accessed | tf_op | source)
XLA Modules:
  0.0 108.4 jit_solution(8454694805916716033)
XLA Ops:
  0.7 2.1 %first_kernel.1 = (bf16[8,64,256]{2,1,0:T(8,128)(2,1)S(1)}, f32[3,128,8]{2,1,0:T(8,128)S(1)}, f32[256,8]{1,0:T(8,128)S(1)}, bf16[8,64,256]{2,1,0:T(8,128)(2,1)S(1)}, bf16[8,64,256]{2,1,0:T(8,128)(2,1)S(1)}) custom-call(s32[3]{0:T(128)S(1)} %pad_add_fusion.refs_0_, f32[8,64,256]{2,1,0:T(8,128)} %refs_1_.3, f32[8,64,256]{2,1,0:T(8,128)} %refs_3_.3, ...), custom_call_target="tpu_custom_call" | custom-call | bytes 2416652 | tf_op jit(solution)/shard_map/first_kernel/pallas_call | solution.py:33
  6.3 2.7 %collective-permute-start.3 = (s16[272,128]{1,0:T(8,128)(2,1)S(1)}, s16[272,128]{1,0:T(8,128)(2,1)S(1)}, u32[]{:S(2)}, u32[]{:S(2)}) collective-permute-start(s16[272,128]{1,0:T(8,128)(2,1)S(1)} %get-tuple-element.62), channel_id=1, source_target_pairs={{0,2},{1,3},{2,0},{3,1},{4,6},{5,7},{6,4},{7,5},{8,10},{9,11},{10,... | collective-permute-start | bytes 208904 | tf_op jit(solution)/shard_map/ppermute | solution.py:324
  9.6 2.0 %collective-permute-done.3.refs_2_ = s16[272,128]{1,0:T(8,128)(2,1)S(1)} collective-permute-done((s16[272,128]{1,0:T(8,128)(2,1)S(1)}, s16[272,128]{1,0:T(8,128)(2,1)S(1)}, u32[]{:S(2)}, u32[]{:S(2)}) %collective-permute-start.3) | collective-permute-done | bytes 69664 | tf_op jit(solution)/shard_map/ppermute | solution.py:324
  15.7 2.0 %collective-permute-done.4.refs_1_ = s16[528,128]{1,0:T(8,128)(2,1)S(1)} collective-permute-done((s16[528,128]{1,0:T(8,128)(2,1)S(1)}, s16[528,128]{1,0:T(8,128)(2,1)S(1)}, u32[]{:S(2)}, u32[]{:S(2)}) %collective-permute-start.4) | collective-permute-done | bytes 135200 | tf_op jit(solution)/shard_map/ppermute | solution.py:324
  17.8 2.6 %collective-permute-start.5 = (s16[528,128]{1,0:T(8,128)(2,1)S(1)}, s16[528,128]{1,0:T(8,128)(2,1)S(1)}, u32[]{:S(2)}, u32[]{:S(2)}) collective-permute-start(s16[528,128]{1,0:T(8,128)(2,1)S(1)} %get-tuple-element.68.refs_5_), channel_id=1, source_target_pairs={{0,16},{4,20},{8,24},{12,28},{16,0},{20,4},{24,8},{28,12},{1,17},{... | collective-permute-start | bytes 405512 | tf_op jit(solution)/shard_map/ppermute | solution.py:324
  21.7 2.4 %collective-permute-start.9 = (bf16[8,128,128]{2,1,0:T(8,128)(2,1)S(1)}, bf16[8,128,128]{2,1,0:T(8,128)(2,1)S(1)}, u32[]{:S(2)}, u32[]{:S(2)}) collective-permute-start(bf16[8,128,128]{2,1,0:T(8,128)(2,1)S(1)} %collective-permute-done.8.refs_5_), channel_id=1, source_target_pairs={{0,8},{8,16},{16,24},{12,4},{20,12},{28,20},{1,9},{9,17},{17,25},{... | collective-permute-start | bytes 786440 | tf_op jit(solution)/shard_map/ppermute | solution.py:331
  24.9 2.2 %layout_kernel.1 = (f32[8,128,128]{2,1,0:T(8,128)S(1)}, f32[8,128,128]{2,1,0:T(8,128)S(1)}) custom-call(s32[3]{0:T(128)S(1)} %pad_add_fusion.refs_0_, f32[8,64,256]{2,1,0:T(8,128)} %refs_1_.3, f32[8,64,256]{2,1,0:T(8,128)} %copy-done.1, f32[8,64,256]{2,1,0:T(8,128)} %refs_3_.3, f32[8,64,256]{2,1,0:T(8,128)} %collective-permute-done.2.refs_4_, ...), custom_call_target="tpu_custom_call" | custom-call | bytes 3145740 | tf_op jit(solution)/shard_map/layout_kernel/pallas_call | solution.py:33
  27.7 3.3 %stage_kernel.1 = (bf16[8,1024,256]{2,1,0:T(8,128)(2,1)S(1)}, bf16[512,1024]{1,0:T(8,128)(2,1)S(1)}) custom-call(s32[8]{0:T(128)S(1)} %minimum_bitcast_fusion.refs_0_, bf16[8,1024,256]{2,1,0:T(8,128)(2,1)} %collective-permute-done.7.refs_1_, bf16[1024,1024]{1,0:T(8,128)(2,1)} %refs_2_.3, s16[528,128]{1,0:T(8,128)(2,1)S(1)} %get-tuple-element.73.refs_3_), custom_call_target="tpu_custom_call" | custom-call | bytes 11534368 | tf_op jit(solution)/shard_map/stage_kernel/pallas_call | solution.py:33
  31.5 2.9 %near_kernel.3.refs_4_ = f32[8,256,128]{2,1,0:T(8,128)S(1)} custom-call(s32[3]{0:T(128)S(1)} %pad_add_fusion.refs_0_, s32[8,16]{1,0:T(8,128)S(1)} %fusion.1.refs_1_, bf16[8,1024,256]{2,1,0:T(8,128)(2,1)S(1)} %bitcast.7, bf16[8,1024,256]{2,1,0:T(8,128)(2,1)S(1)} %get-tuple-element.75.refs_3_, bf16[8,128,128]{2,1,0:T(8,128)(2,1)S(1)} %get-tuple-element.76.refs_4_, ...), custom_call_target="tpu_custom_call" | custom-call | bytes 10224140 | tf_op jit(solution)/shard_map/near_kernel/pallas_call | solution.py:33
  37.9 6.3 %collective-permute-done.10.refs_4_ = s16[1296,128]{1,0:T(8,128)(2,1)S(1)} collective-permute-done((s16[1296,128]{1,0:T(8,128)(2,1)S(1)}, s16[1296,128]{1,0:T(8,128)(2,1)S(1)}, u32[]{:S(2)}, u32[]{:S(2)}) %collective-permute-start.10) | collective-permute-done | bytes 331808 | tf_op jit(solution)/shard_map/ppermute | solution.py:324
  46.9 2.4 %collective-permute-start.11 = (s16[528,128]{1,0:T(8,128)(2,1)S(1)}, s16[528,128]{1,0:T(8,128)(2,1)S(1)}, u32[]{:S(2)}, u32[]{:S(2)}) collective-permute-start(s16[528,128]{1,0:T(8,128)(2,1)S(1)} %get-tuple-element.90), channel_id=1, source_target_pairs={{0,8},{4,12},{8,0},{12,4},{16,24},{20,28},{24,16},{28,20},{1,9},{5... | collective-permute-start | bytes 405512 | tf_op jit(solution)/shard_map/ppermute | solution.py:324
  49.3 4.4 %collective-permute-done.11.refs_1_ = s16[528,128]{1,0:T(8,128)(2,1)S(1)} collective-permute-done((s16[528,128]{1,0:T(8,128)(2,1)S(1)}, s16[528,128]{1,0:T(8,128)(2,1)S(1)}, u32[]{:S(2)}, u32[]{:S(2)}) %collective-permute-start.11) | collective-permute-done | bytes 135200 | tf_op jit(solution)/shard_map/ppermute | solution.py:324
  55.2 2.9 %collective-permute-start.15 = (bf16[8,128,128]{2,1,0:T(8,128)(2,1)S(1)}, bf16[8,128,128]{2,1,0:T(8,128)(2,1)S(1)}, u32[]{:S(2)}, u32[]{:S(2)}) collective-permute-start(bf16[8,128,128]{2,1,0:T(8,128)(2,1)S(1)} %collective-permute-done.14.refs_5_), channel_id=1, source_target_pairs={{0,8},{8,16},{16,24},{12,4},{20,12},{28,20},{1,9},{9,17},{17,25},{... | collective-permute-start | bytes 786440 | tf_op jit(solution)/shard_map/ppermute | solution.py:331
  58.0 3.2 %collective-permute-done.12.refs_1_ = s16[528,128]{1,0:T(8,128)(2,1)S(1)} collective-permute-done((s16[528,128]{1,0:T(8,128)(2,1)S(1)}, s16[528,128]{1,0:T(8,128)(2,1)S(1)}, u32[]{:S(2)}, u32[]{:S(2)}) %collective-permute-start.12) | collective-permute-done | bytes 135200 | tf_op jit(solution)/shard_map/ppermute | solution.py:324
  62.3 2.9 %near_kernel.4.refs_4_ = f32[8,256,128]{2,1,0:T(8,128)S(1)} custom-call(s32[3]{0:T(128)S(1)} %pad_add_fusion.refs_0_, s32[8,16]{1,0:T(8,128)S(1)} %fusion.1.refs_1_, bf16[8,1024,256]{2,1,0:T(8,128)(2,1)S(1)} %bitcast.8, bf16[8,1024,256]{2,1,0:T(8,128)(2,1)S(1)} %get-tuple-element.75.refs_3_, bf16[8,128,128]{2,1,0:T(8,128)(2,1)S(1)} %get-tuple-element.95.refs_4_, ...), custom_call_target="tpu_custom_call" | custom-call | bytes 10224140 | tf_op jit(solution)/shard_map/near_kernel/pallas_call | solution.py:33
  66.4 1.9 %finish_kernel.4 = (s16[1296,128]{1,0:T(8,128)(2,1)S(1)}, f32[8,128,128]{2,1,0:T(8,128)S(1)}, f32[8,32,128]{2,1,0:T(8,128)S(1)}) custom-call(s32[3]{0:T(128)S(1)} %pad_add_fusion.refs_0_, f32[16,32,128]{2,1,0:T(8,128)S(1)} %get-tuple-element.93.refs_1_, s16[528,128]{1,0:T(8,128)(2,1)S(1)} %collective-permute-done.13.refs_2_, ...), custom_call_target="tpu_custom_call" | custom-call | bytes 5081100 | tf_op jit(solution)/shard_map/finish_kernel/pallas_call | solution.py:33
  69.9 5.6 %collective-permute-done.16.refs_4_ = s16[1296,128]{1,0:T(8,128)(2,1)S(1)} collective-permute-done((s16[1296,128]{1,0:T(8,128)(2,1)S(1)}, s16[1296,128]{1,0:T(8,128)(2,1)S(1)}, u32[]{:S(2)}, u32[]{:S(2)}) %collective-permute-start.16) | collective-permute-done | bytes 331808 | tf_op jit(solution)/shard_map/ppermute | solution.py:324
  76.6 2.0 %collective-permute-start.20 = (bf16[8,128,128]{2,1,0:T(8,128)(2,1)S(1)}, bf16[8,128,128]{2,1,0:T(8,128)(2,1)S(1)}, u32[]{:S(2)}, u32[]{:S(2)}) collective-permute-start(bf16[8,128,128]{2,1,0:T(8,128)(2,1)S(1)} %get-tuple-element.110.refs_4_), channel_id=1, source_target_pairs={{0,4},{4,0},{8,12},{12,8},{16,20},{20,16},{24,28},{28,24},{1,5},{5... | collective-permute-start | bytes 786440 | tf_op jit(solution)/shard_map/ppermute | solution.py:324
  79.6 4.1 %collective-permute-done.17.refs_1_ = s16[528,128]{1,0:T(8,128)(2,1)S(1)} collective-permute-done((s16[528,128]{1,0:T(8,128)(2,1)S(1)}, s16[528,128]{1,0:T(8,128)(2,1)S(1)}, u32[]{:S(2)}, u32[]{:S(2)}) %collective-permute-start.17) | collective-permute-done | bytes 135200 | tf_op jit(solution)/shard_map/ppermute | solution.py:324
  84.9 4.6 %collective-permute-start.21 = (bf16[8,128,128]{2,1,0:T(8,128)(2,1)S(1)}, bf16[8,128,128]{2,1,0:T(8,128)(2,1)S(1)}, u32[]{:S(2)}, u32[]{:S(2)}) collective-permute-start(bf16[8,128,128]{2,1,0:T(8,128)(2,1)S(1)} %collective-permute-done.20.refs_5_), channel_id=1, source_target_pairs={{0,8},{8,16},{16,24},{12,4},{20,12},{28,20},{1,9},{9,17},{17,25},{... | collective-permute-start | bytes 786440 | tf_op jit(solution)/shard_map/ppermute | solution.py:331
  89.8 2.1 %collective-permute-start.19 = (s16[528,128]{1,0:T(8,128)(2,1)S(1)}, s16[528,128]{1,0:T(8,128)(2,1)S(1)}, u32[]{:S(2)}, u32[]{:S(2)}) collective-permute-start(s16[528,128]{1,0:T(8,128)(2,1)S(1)} %get-tuple-element.109), channel_id=1, source_target_pairs={{0,4},{4,0},{8,12},{12,8},{16,20},{20,16},{24,28},{28,24},{1,5},{5... | collective-permute-start | bytes 405512 | tf_op jit(solution)/shard_map/ppermute | solution.py:324
  93.1 2.9 %near_kernel.5.refs_4_ = f32[8,256,128]{2,1,0:T(8,128)S(1)} custom-call(s32[3]{0:T(128)S(1)} %pad_add_fusion.refs_0_, s32[8,16]{1,0:T(8,128)S(1)} %fusion.1.refs_1_, bf16[8,1024,256]{2,1,0:T(8,128)(2,1)S(1)} %bitcast.9, bf16[8,1024,256]{2,1,0:T(8,128)(2,1)S(1)} %get-tuple-element.75.refs_3_, bf16[8,128,128]{2,1,0:T(8,128)(2,1)S(1)} %get-tuple-element.110.refs_4_, ...), custom_call_target="tpu_custom_call" | custom-call | bytes 10224140 | tf_op jit(solution)/shard_map/near_kernel/pallas_call | solution.py:33
  99.1 4.9 %collective-permute-done.22.refs_4_ = s16[1040,128]{1,0:T(8,128)(2,1)S(1)} collective-permute-done((s16[1040,128]{1,0:T(8,128)(2,1)S(1)}, s16[1040,128]{1,0:T(8,128)(2,1)S(1)}, u32[]{:S(2)}, u32[]{:S(2)}) %collective-permute-start.22) | collective-permute-done | bytes 266272 | tf_op jit(solution)/shard_map/ppermute | solution.py:324
  104.9 1.9 %collective-permute-done.23.refs_2_ = f32[2,8,64,128]{3,2,1,0:T(8,128)S(1)} collective-permute-done((f32[2,8,64,128]{3,2,1,0:T(8,128)S(1)}, f32[2,8,64,128]{3,2,1,0:T(8,128)S(1)}, u32[]{:S(2)}, u32[]{:S(2)}) %collective-permute-start.23) | collective-permute-done | bytes 524320 | tf_op jit(solution)/shard_map/ppermute | solution.py:324
  (59 shorter events, 33.1 us)
Async XLA Ops:
  2.9 1.7 %collective-permute-start = (bf16[8,64,256]{2,1,0:T(8,128)(2,1)S(1)}, bf16[8,64,256]{2,1,0:T(8,128)(2,1)S(1)}, u32[]{:S(2)}, u32[]{:S(2)}) collective-permute-start(bf16[8,64,256]{2,1,0:T(8,128)(2,1)S(1)} %get-tuple-element.60.refs_1_), channel_id=1, source_target_pairs={{0,1},{1,0},{2,3},{3,2},{4,5},{5,4},{6,7},{7,6},{8,9},{9,8},{10,11... | collective-permute-start | bytes 786440 | tf_op jit(solution)/shard_map/ppermute | solution.py:324
  5.3 22.4 %collective-permute-start.7 = (bf16[8,1024,256]{2,1,0:T(8,128)(2,1)}, bf16[8,1024,256]{2,1,0:T(8,128)(2,1)}, u32[]{:S(2)}, u32[]{:S(2)}) collective-permute-start(bf16[8,1024,256]{2,1,0:T(8,128)(2,1)} %bitcast.6), channel_id=1, source_target_pairs={{0,1},{1,0},{2,3},{3,2},{4,5},{5,4},{6,7},{7,6},{8,9},{9,8},{10,11... | collective-permute-start | bytes 12582920 | tf_op jit(solution)/shard_map/ppermute | solution.py:324
  5.8 18.3 %collective-permute-start.1 = (f32[8,64,256]{2,1,0:T(8,128)}, f32[8,64,256]{2,1,0:T(8,128)S(1)}, u32[]{:S(2)}, u32[]{:S(2)}) collective-permute-start(f32[8,64,256]{2,1,0:T(8,128)} %refs_1_.3), channel_id=1, source_target_pairs={{0,1},{1,0},{2,3},{3,2},{4,5},{5,4},{6,7},{7,6},{8,9},{9,8},{10,11... | collective-permute-start | bytes 1572872 | tf_op jit(solution)/shard_map/ppermute | solution.py:324
  5.9 18.9 %collective-permute-start.2 = (f32[8,64,256]{2,1,0:T(8,128)}, f32[8,64,256]{2,1,0:T(8,128)}, u32[]{:S(2)}, u32[]{:S(2)}) collective-permute-start(f32[8,64,256]{2,1,0:T(8,128)} %refs_3_.3), channel_id=1, source_target_pairs={{0,1},{1,0},{2,3},{3,2},{4,5},{5,4},{6,7},{7,6},{8,9},{9,8},{10,11... | collective-permute-start | bytes 1572872 | tf_op jit(solution)/shard_map/ppermute | solution.py:324
  6.3 5.4 %collective-permute-start.3 = (s16[272,128]{1,0:T(8,128)(2,1)S(1)}, s16[272,128]{1,0:T(8,128)(2,1)S(1)}, u32[]{:S(2)}, u32[]{:S(2)}) collective-permute-start(s16[272,128]{1,0:T(8,128)(2,1)S(1)} %get-tuple-element.62), channel_id=1, source_target_pairs={{0,2},{1,3},{2,0},{3,1},{4,6},{5,7},{6,4},{7,5},{8,10},{9,11},{10,... | collective-permute-start | bytes 208904 | tf_op jit(solution)/shard_map/ppermute | solution.py:324
  12.3 5.4 %collective-permute-start.4 = (s16[528,128]{1,0:T(8,128)(2,1)S(1)}, s16[528,128]{1,0:T(8,128)(2,1)S(1)}, u32[]{:S(2)}, u32[]{:S(2)}) collective-permute-start(s16[528,128]{1,0:T(8,128)(2,1)S(1)} %get-tuple-element.67), channel_id=1, source_target_pairs={{0,8},{4,12},{8,0},{12,4},{16,24},{20,28},{24,16},{28,20},{1,9},{5... | collective-permute-start | bytes 405512 | tf_op jit(solution)/shard_map/ppermute | solution.py:324
  14.2 7.5 %collective-permute-start.8 = (bf16[8,128,128]{2,1,0:T(8,128)(2,1)S(1)}, bf16[8,128,128]{2,1,0:T(8,128)(2,1)S(1)}, u32[]{:S(2)}, u32[]{:S(2)}) collective-permute-start(bf16[8,128,128]{2,1,0:T(8,128)(2,1)S(1)} %get-tuple-element.76.refs_4_), channel_id=1, source_target_pairs={{0,4},{4,0},{8,12},{12,8},{16,20},{20,16},{24,28},{28,24},{1,5},{5... | collective-permute-start | bytes 786440 | tf_op jit(solution)/shard_map/ppermute | solution.py:324
  17.8 9.3 %collective-permute-start.5 = (s16[528,128]{1,0:T(8,128)(2,1)S(1)}, s16[528,128]{1,0:T(8,128)(2,1)S(1)}, u32[]{:S(2)}, u32[]{:S(2)}) collective-permute-start(s16[528,128]{1,0:T(8,128)(2,1)S(1)} %get-tuple-element.68.refs_5_), channel_id=1, source_target_pairs={{0,16},{4,20},{8,24},{12,28},{16,0},{20,4},{24,8},{28,12},{1,17},{... | collective-permute-start | bytes 405512 | tf_op jit(solution)/shard_map/ppermute | solution.py:324
  21.7 9.4 %collective-permute-start.9 = (bf16[8,128,128]{2,1,0:T(8,128)(2,1)S(1)}, bf16[8,128,128]{2,1,0:T(8,128)(2,1)S(1)}, u32[]{:S(2)}, u32[]{:S(2)}) collective-permute-start(bf16[8,128,128]{2,1,0:T(8,128)(2,1)S(1)} %collective-permute-done.8.refs_5_), channel_id=1, source_target_pairs={{0,8},{8,16},{16,24},{12,4},{20,12},{28,20},{1,9},{9,17},{17,25},{... | collective-permute-start | bytes 786440 | tf_op jit(solution)/shard_map/ppermute | solution.py:331
  27.2 7.2 %collective-permute-start.6 = (s16[528,128]{1,0:T(8,128)(2,1)S(1)}, s16[528,128]{1,0:T(8,128)(2,1)S(1)}, u32[]{:S(2)}, u32[]{:S(2)}) collective-permute-start(s16[528,128]{1,0:T(8,128)(2,1)S(1)} %get-tuple-element.73.refs_3_), channel_id=1, source_target_pairs={{0,4},{4,0},{8,12},{12,8},{16,20},{20,16},{24,28},{28,24},{1,5},{5... | collective-permute-start | bytes 405512 | tf_op jit(solution)/shard_map/ppermute | solution.py:324
  36.3 7.8 %collective-permute-start.10 = (s16[1296,128]{1,0:T(8,128)(2,1)S(1)}, s16[1296,128]{1,0:T(8,128)(2,1)S(1)}, u32[]{:S(2)}, u32[]{:S(2)}) collective-permute-start(s16[1296,128]{1,0:T(8,128)(2,1)S(1)} %get-tuple-element.85), channel_id=1, source_target_pairs={{0,2},{1,3},{2,0},{3,1},{4,6},{5,7},{6,4},{7,5},{8,10},{9,11},{10,... | collective-permute-start | bytes 995336 | tf_op jit(solution)/shard_map/ppermute | solution.py:324
  45.2 10.0 %collective-permute-start.14 = (bf16[8,128,128]{2,1,0:T(8,128)(2,1)S(1)}, bf16[8,128,128]{2,1,0:T(8,128)(2,1)S(1)}, u32[]{:S(2)}, u32[]{:S(2)}) collective-permute-start(bf16[8,128,128]{2,1,0:T(8,128)(2,1)S(1)} %get-tuple-element.95.refs_4_), channel_id=1, source_target_pairs={{0,4},{4,0},{8,12},{12,8},{16,20},{20,16},{24,28},{28,24},{1,5},{5... | collective-permute-start | bytes 786440 | tf_op jit(solution)/shard_map/ppermute | solution.py:324
  46.9 6.8 %collective-permute-start.11 = (s16[528,128]{1,0:T(8,128)(2,1)S(1)}, s16[528,128]{1,0:T(8,128)(2,1)S(1)}, u32[]{:S(2)}, u32[]{:S(2)}) collective-permute-start(s16[528,128]{1,0:T(8,128)(2,1)S(1)} %get-tuple-element.90), channel_id=1, source_target_pairs={{0,8},{4,12},{8,0},{12,4},{16,24},{20,28},{24,16},{28,20},{1,9},{5... | collective-permute-start | bytes 405512 | tf_op jit(solution)/shard_map/ppermute | solution.py:324
  53.8 7.4 %collective-permute-start.12 = (s16[528,128]{1,0:T(8,128)(2,1)S(1)}, s16[528,128]{1,0:T(8,128)(2,1)S(1)}, u32[]{:S(2)}, u32[]{:S(2)}) collective-permute-start(s16[528,128]{1,0:T(8,128)(2,1)S(1)} %get-tuple-element.92), channel_id=1, source_target_pairs={{0,16},{4,20},{8,24},{12,28},{16,0},{20,4},{24,8},{28,12},{1,17},{... | collective-permute-start | bytes 405512 | tf_op jit(solution)/shard_map/ppermute | solution.py:324
  55.2 7.2 %collective-permute-start.15 = (bf16[8,128,128]{2,1,0:T(8,128)(2,1)S(1)}, bf16[8,128,128]{2,1,0:T(8,128)(2,1)S(1)}, u32[]{:S(2)}, u32[]{:S(2)}) collective-permute-start(bf16[8,128,128]{2,1,0:T(8,128)(2,1)S(1)} %collective-permute-done.14.refs_5_), channel_id=1, source_target_pairs={{0,8},{8,16},{16,24},{12,4},{20,12},{28,20},{1,9},{9,17},{17,25},{... | collective-permute-start | bytes 786440 | tf_op jit(solution)/shard_map/ppermute | solution.py:331
  61.3 5.1 %collective-permute-start.13 = (s16[528,128]{1,0:T(8,128)(2,1)S(1)}, s16[528,128]{1,0:T(8,128)(2,1)S(1)}, u32[]{:S(2)}, u32[]{:S(2)}) collective-permute-start(s16[528,128]{1,0:T(8,128)(2,1)S(1)} %get-tuple-element.94), channel_id=1, source_target_pairs={{0,4},{4,0},{8,12},{12,8},{16,20},{20,16},{24,28},{28,24},{1,5},{5... | collective-permute-start | bytes 405512 | tf_op jit(solution)/shard_map/ppermute | solution.py:324
  68.3 7.2 %collective-permute-start.16 = (s16[1296,128]{1,0:T(8,128)(2,1)S(1)}, s16[1296,128]{1,0:T(8,128)(2,1)S(1)}, u32[]{:S(2)}, u32[]{:S(2)}) collective-permute-start(s16[1296,128]{1,0:T(8,128)(2,1)S(1)} %get-tuple-element.100), channel_id=1, source_target_pairs={{0,2},{1,3},{2,0},{3,1},{4,6},{5,7},{6,4},{7,5},{8,10},{9,11},{10,... | collective-permute-start | bytes 995336 | tf_op jit(solution)/shard_map/ppermute | solution.py:324
  76.6 8.3 %collective-permute-start.20 = (bf16[8,128,128]{2,1,0:T(8,128)(2,1)S(1)}, bf16[8,128,128]{2,1,0:T(8,128)(2,1)S(1)}, u32[]{:S(2)}, u32[]{:S(2)}) collective-permute-start(bf16[8,128,128]{2,1,0:T(8,128)(2,1)S(1)} %get-tuple-element.110.refs_4_), channel_id=1, source_target_pairs={{0,4},{4,0},{8,12},{12,8},{16,20},{20,16},{24,28},{28,24},{1,5},{5... | collective-permute-start | bytes 786440 | tf_op jit(solution)/shard_map/ppermute | solution.py:324
  78.6 5.0 %collective-permute-start.17 = (s16[528,128]{1,0:T(8,128)(2,1)S(1)}, s16[528,128]{1,0:T(8,128)(2,1)S(1)}, u32[]{:S(2)}, u32[]{:S(2)}) collective-permute-start(s16[528,128]{1,0:T(8,128)(2,1)S(1)} %get-tuple-element.105), channel_id=1, source_target_pairs={{0,8},{4,12},{8,0},{12,4},{16,24},{20,28},{24,16},{28,20},{1,9},{5... | collective-permute-start | bytes 405512 | tf_op jit(solution)/shard_map/ppermute | solution.py:324
  83.7 6.0 %collective-permute-start.18 = (s16[528,128]{1,0:T(8,128)(2,1)S(1)}, s16[528,128]{1,0:T(8,128)(2,1)S(1)}, u32[]{:S(2)}, u32[]{:S(2)}) collective-permute-start(s16[528,128]{1,0:T(8,128)(2,1)S(1)} %get-tuple-element.107), channel_id=1, source_target_pairs={{0,16},{4,20},{8,24},{12,28},{16,0},{20,4},{24,8},{28,12},{1,17},{... | collective-permute-start | bytes 405512 | tf_op jit(solution)/shard_map/ppermute | solution.py:324
  84.9 8.3 %collective-permute-start.21 = (bf16[8,128,128]{2,1,0:T(8,128)(2,1)S(1)}, bf16[8,128,128]{2,1,0:T(8,128)(2,1)S(1)}, u32[]{:S(2)}, u32[]{:S(2)}) collective-permute-start(bf16[8,128,128]{2,1,0:T(8,128)(2,1)S(1)} %collective-permute-done.20.refs_5_), channel_id=1, source_target_pairs={{0,8},{8,16},{16,24},{12,4},{20,12},{28,20},{1,9},{9,17},{17,25},{... | collective-permute-start | bytes 786440 | tf_op jit(solution)/shard_map/ppermute | solution.py:331
  89.8 6.3 %collective-permute-start.19 = (s16[528,128]{1,0:T(8,128)(2,1)S(1)}, s16[528,128]{1,0:T(8,128)(2,1)S(1)}, u32[]{:S(2)}, u32[]{:S(2)}) collective-permute-start(s16[528,128]{1,0:T(8,128)(2,1)S(1)} %get-tuple-element.109), channel_id=1, source_target_pairs={{0,4},{4,0},{8,12},{12,8},{16,20},{20,16},{24,28},{28,24},{1,5},{5... | collective-permute-start | bytes 405512 | tf_op jit(solution)/shard_map/ppermute | solution.py:324
  97.6 6.5 %collective-permute-start.22 = (s16[1040,128]{1,0:T(8,128)(2,1)S(1)}, s16[1040,128]{1,0:T(8,128)(2,1)S(1)}, u32[]{:S(2)}, u32[]{:S(2)}) collective-permute-start(s16[1040,128]{1,0:T(8,128)(2,1)S(1)} %get-tuple-element.115), channel_id=1, source_target_pairs={{0,2},{1,3},{2,0},{3,1},{4,6},{5,7},{6,4},{7,5},{8,10},{9,11},{10,... | collective-permute-start | bytes 798728 | tf_op jit(solution)/shard_map/ppermute | solution.py:324
  104.8 2.0 %collective-permute-start.23 = (f32[2,8,64,128]{3,2,1,0:T(8,128)S(1)}, f32[2,8,64,128]{3,2,1,0:T(8,128)S(1)}, u32[]{:S(2)}, u32[]{:S(2)}) collective-permute-start(f32[2,8,64,128]{3,2,1,0:T(8,128)S(1)} %get-tuple-element.117), channel_id=1, source_target_pairs={{0,1},{1,0},{2,3},{3,2},{4,5},{5,4},{6,7},{7,6},{8,9},{9,8},{10,11... | collective-permute-start | bytes 1572872 | tf_op jit(solution)/shard_map/ppermute | solution.py:324
  (5 other events, 85.6 us)
